TPU v7x, 32 devices: a whole 2x2x4 slice. The times are simulated.
32 devices in a mesh: ens: 2 (over x), tile: 16 (over z, y, core).
Axes of the slice: x: 2, y: 2, z: 4, core: 2. Of those that a mesh axis runs over, the one named last changes fastest.
Arguments:
- observations: float32 [1024, 64], P(('ens', 'tile')), parts along dimension 0, may hold values from -24 to 24
- jacobian: float32 [256, 64, 256], P('tile'), may hold values from -0.375 to 0.375
- block_row: int32 [256], P('tile'), may hold values from 0 to 31
- block_col: int32 [256], P('tile'), may hold values from 0 to 127, as said below
- block_count: int32 [16], P('tile'), may hold values from 1 to 16, as said below
- block_band: int32 [512], P('tile'), may hold values from 0 to 127
- carry_decay: float32 [128], replicated, may hold values from 0.3 to 0.99
- sparsity_weight: float32 [1024], replicated, may hold values from 0.1 to 2
Outputs:
- coefficients: float32 [128, 8, 1024], P(('ens', 'tile')), parts along dimension 0
- misfit: float32 [1024, 64], P(('ens', 'tile')), parts along dimension 0
There are 2 independent parts, one for each index of `ens`. A program takes and returns all parts, laid end to end along the dimension named above; an argument that names none is the same for every part. Nothing has to cross between parts.
Inputs may be any that keep to these rules, and one draw needn't show every extreme that they name: block_count[d] slots, 0 to block_count[d] - 1, of index d hold blocks; the other slots hold no blocks; some index uses all 16 slots. `block_col`: owner of a strip j is j // 8; among the 16 slots of one index d at most 2 name strips of one owner, and in every index some owner is named by exactly 2 slots.
All inputs are finite; a program needn't handle non-finite values.
Results may differ from a plain program's by a relative error of at most 0.0003.
Values sent between devices are 32-bit elements; how exact they have to be, the bound alone decides.
No kernel may reach another device: no remote copies, remote signals or barrier semaphores. Data moves between devices by JAX's collectives and lax.ppermute only.
A program may use at most 128 MiB of HBM per device.

v0:
```python
import math

import jax
import jax.numpy as jnp
from jax import lax
from jax.sharding import PartitionSpec as P

WIN = 8
NLAT = 64
SEC_STRIPS = 2
STRIP = 256
SOUNDS = 64
SB_DEV = 32
NBANDS = 128
ITERS = 3


root_half = math.sqrt(0.5)
step_size = 0.2
highest = lax.Precision.HIGHEST


def haar_forward(values):
    details = []
    approx = values
    while approx.shape[-1] % 2 == 0 and approx.shape[-1] > 1:
        paired = approx.reshape(approx.shape[:-1] + (approx.shape[-1] // 2, 2))
        even_part = paired[..., 0]
        odd_part = paired[..., 1]
        details.insert(0, (even_part - odd_part) * root_half)
        approx = (even_part + odd_part) * root_half
    return jnp.concatenate([approx] + details, axis=-1)


def haar_inverse(coeffs):
    length = coeffs.shape[-1]
    widths = []
    while length % 2 == 0 and length > 1:
        length = length // 2
        widths.append(length)
    approx = coeffs[..., :length]
    offset = length
    for detail_len in reversed(widths):
        detail = coeffs[..., offset : offset + detail_len]
        offset = offset + detail_len
        even_part = (approx + detail) * root_half
        odd_part = (approx - detail) * root_half
        approx = jnp.stack([even_part, odd_part], axis=-1).reshape(
            approx.shape[:-1] + (2 * detail_len,)
        )
    return approx


def momentum_weights(total_steps):
    weights = []
    current = 1.0
    for iteration in range(total_steps):
        following = (1.0 + math.sqrt(1.0 + 4.0 * current * current)) / 2.0
        weights.append((current - 1.0) / following)
        current = following
    return weights


def shrink(values, limit):
    return jnp.sign(values) * jnp.maximum(jnp.abs(values) - limit, 0.0)


def carry_collect(values, my_window, sectors, carry_decay, backward):

    def weigh(sources):
        if backward:
            spacing = (sources - my_window).astype(jnp.float32)
        else:
            spacing = (my_window - sources).astype(jnp.float32)
        powered = jnp.power(carry_decay[None, :], jnp.maximum(spacing, 0.0)[:, None])
        return jnp.where(spacing[:, None] >= 0.0, powered, 0.0)

    def fold_rows(piece):
        sources = jnp.arange(piece.shape[0], dtype=jnp.int32) // sectors
        return jnp.sum(weigh(sources) * piece, axis=0)

    if backward:
        return fold_rows(lax.all_gather(values[None, :], "tile", axis=0, tiled=True))
    return fold_rows(lax.all_gather(values[None, :], "tile", axis=0, tiled=True))


def forward_blocks(jacobian, picked, row_hot, valid):
    results = jnp.einsum("kis,ks->ki", jacobian, picked, precision=highest) * valid[:, None]
    return jnp.einsum("kb,ki->bi", row_hot, results, precision=highest)


def adjoint_slots(jacobian, adjoint, row_hot, valid):
    chosen = jnp.einsum("kb,bi->ki", row_hot, adjoint, precision=highest)
    return jnp.einsum("kis,ki->ks", jacobian, chosen, precision=highest) * valid[:, None]


def body(
    observations,
    jacobian,
    block_row,
    block_col,
    block_count,
    block_band,
    carry_decay,
    sparsity_weight,
):
    devices = lax.axis_size("tile")
    sectors = devices // WIN
    sector_width = SEC_STRIPS * STRIP
    local_lat = NLAT // devices
    strips_dev = NLAT * SEC_STRIPS
    slot_total = jacobian.shape[0]
    my_window = lax.axis_index("tile") // sectors
    used = block_count[0]
    row_hot = jax.nn.one_hot(block_row, SB_DEV, dtype=jnp.float32)
    band_hot = jax.nn.one_hot(block_band, NBANDS, dtype=jnp.float32)
    valid = (jnp.arange(slot_total, dtype=jnp.int32) < used).astype(jnp.float32)
    col_hot = jax.nn.one_hot(block_col, strips_dev, dtype=jnp.float32)
    coeffs = jnp.zeros((local_lat, WIN, sectors * sector_width), jnp.float32)
    point = coeffs
    misfit = jnp.zeros_like(observations)
    for beta in momentum_weights(ITERS):
        flux = haar_inverse(point)
        field = lax.all_to_all(
            flux.reshape(local_lat, devices, sector_width),
            "tile",
            split_axis=1,
            concat_axis=0,
            tiled=True,
        )
        picked = jnp.take(field.reshape(strips_dev, STRIP), block_col, axis=0)
        direct = forward_blocks(jacobian, picked, row_hot, valid)
        partial_value = jnp.dot(jnp.sum(direct, axis=1), band_hot, precision=highest) / SOUNDS
        carried = carry_collect(partial_value, my_window, sectors, carry_decay, False)
        predicted = direct + jnp.dot(band_hot, carried, precision=highest)[:, None]
        misfit = predicted - observations
        back_total = jnp.dot(jnp.sum(misfit, axis=1), band_hot, precision=highest)
        returned = carry_collect(back_total, my_window, sectors, carry_decay, True)
        adjoint = misfit + jnp.dot(band_hot, returned, precision=highest)[:, None] / SOUNDS
        slot_grads = adjoint_slots(jacobian, adjoint, row_hot, valid)
        grad_rows = jnp.einsum("kp,ks->ps", col_hot, slot_grads, precision=highest)
        back_lines = lax.all_to_all(
            grad_rows.reshape(NLAT, 1, sector_width),
            "tile",
            split_axis=0,
            concat_axis=1,
            tiled=True,
        )
        gradient = haar_forward(back_lines.reshape(local_lat, WIN, sectors * sector_width))
        updated = shrink(point - step_size * gradient, step_size * sparsity_weight)
        point = updated + beta * (updated - coeffs)
        coeffs = updated
    return (coeffs, misfit)


def solution(mesh):
    return jax.shard_map(
        body,
        mesh=mesh,
        in_specs=(
            P(("ens", "tile"), None),
            P("tile", None, None),
            P("tile"),
            P("tile"),
            P("tile"),
            P("tile"),
            P(),
            P(),
        ),
        out_specs=(P(("ens", "tile"), None, None), P(("ens", "tile"), None)),
        check_vma=False,
    )
```

profile of v0, /device:TPU:0, one launch (start us, length us, event | category | flops | bytes accessed | tf_op | source)
XLA Modules:
  0.0 266.0 jit_solution(7208918923025685149)
XLA Ops:
  3.5 1.0 fusion.19
  4.4 1.0 fusion.87
  6.3 23.0 %all-gather.6 = f32[16,1,128]{2,1,0:T(1,128)S(1)} all-gather(f32[1,1,128]{2,1,0:T(1,128)S(1)} %fusion.8), channel_id=2, replica_groups=mesh['ens'=2,'tile'=16] {'tile'}, dimensions={0}, use_global_device_ids=true | all-gather | bytes 8704 | tf_op jit(solution)/shard_map/all_gather | solution.py:84
  32.7 17.3 %all-gather.7 = f32[16,1,128]{2,1,0:T(1,128)S(1)} all-gather(f32[1,1,128]{2,1,0:T(1,128)S(1)} %convolution_bitcast_fusion.9), channel_id=3, replica_groups=mesh['ens'=2,'tile'=16] {'tile'}, dimensions={0}, use_global_device_ids=true | all-gather | bytes 8704 | tf_op jit(solution)/shard_map/all_gather | solution.py:83
  54.3 3.7 %all-to-all-start = ((f32[64,1,512]{2,1,0:T(1,128)}), f32[64,1,512]{2,1,0:T(1,128)S(1)}, u32[]{:S(2)}, u32[]{:S(2)}) async-start(f32[64,1,512]{2,1,0:T(1,128)} %reshape.710), calls=%async_computation | async-start | bytes 262144 | tf_op jit(solution)/shard_map/all_to_all | solution.py:142
  58.0 7.7 %all-to-all-done = f32[64,1,512]{2,1,0:T(1,128)S(1)} async-done(((f32[64,1,512]{2,1,0:T(1,128)}), f32[64,1,512]{2,1,0:T(1,128)S(1)}, u32[]{:S(2)}, u32[]{:S(2)}) %all-to-all-start) | async-done | bytes 131104 | tf_op jit(solution)/shard_map/all_to_all | solution.py:142
  65.7 2.6 copy.752
  68.3 8.9 %fusion.80 = (f32[4,8,512,1]{0,3,2,1:T(1,128)}, f32[4,8,512,1]{0,3,2,1:T(1,128)S(1)}) fusion(f32[4,8,512,2]{0,3,2,1:T(2,128)} %bitcast.327), kind=kLoop, calls=%fused_computation.252 | loop fusion | bytes 262144 | tf_op jit(solution)/shard_map/slice | solution.py:29
  77.2 2.7 %copy.885 = f32[4,8,512,1]{2,1,3,0:T(8,128)S(1)} copy(f32[4,8,512,1]{0,3,2,1:T(1,128)} %get-tuple-element.25) | data formatting | bytes 131072
  81.2 1.1 subtract_multiply_fusion.2
  88.3 3.1 %copy.800 = f32[4,8,512,2]{0,3,2,1:T(2,128)} copy(f32[4,8,512,2]{2,1,0,3:T(8,128)S(1)} %pad_maximum_fusion) | data formatting | bytes 262144 | tf_op jit(solution)/shard_map/stack | solution.py:48
  91.4 2.9 %copy.801 = f32[4,16,512]{2,0,1:T(4,128)S(1)} copy(f32[4,16,512]{0,2,1:T(8,128)} %bitcast.330) | data formatting | bytes 262144 | tf_op jit(solution)/shard_map/reshape;reshape | solution.py:125
  94.3 10.5 %all_to_all.80 = f32[4,16,512]{2,0,1:T(4,128)S(1)} all-to-all(f32[4,16,512]{2,0,1:T(4,128)S(1)} %copy.801), channel_id=1, replica_groups=mesh['ens'=2,'tile'=16] {'tile'}, dimensions={1} | all-to-all | bytes 262144 | tf_op jit(solution)/shard_map/all_to_all | solution.py:124
  105.5 1.0 fusion.16
  107.1 18.0 %all-gather.8 = f32[16,1,128]{2,1,0:T(1,128)S(1)} all-gather(f32[1,1,128]{2,1,0:T(1,128)S(1)} %fusion.5), channel_id=4, replica_groups=mesh['ens'=2,'tile'=16] {'tile'}, dimensions={0}, use_global_device_ids=true | all-gather | bytes 8704 | tf_op jit(solution)/shard_map/all_gather | solution.py:84
  125.7 18.3 %all-gather.9 = f32[16,1,128]{2,1,0:T(1,128)S(1)} all-gather(f32[1,1,128]{2,1,0:T(1,128)S(1)} %convolution_bitcast_fusion.5), channel_id=5, replica_groups=mesh['ens'=2,'tile'=16] {'tile'}, dimensions={0}, use_global_device_ids=true | all-gather | bytes 8704 | tf_op jit(solution)/shard_map/all_gather | solution.py:83
  145.6 10.5 %all_to_all.81 = f32[64,1,512]{2,1,0:T(1,128)S(1)} all-to-all(f32[64,1,512]{2,1,0:T(1,128)S(1)} %reshape.711), channel_id=1, replica_groups=mesh['ens'=2,'tile'=16] {'tile'}, dimensions={0} | all-to-all | bytes 262144 | tf_op jit(solution)/shard_map/all_to_all | solution.py:142
  156.1 2.6 copy.803
  158.7 8.9 %fusion.79 = (f32[4,8,512,1]{0,3,2,1:T(1,128)}, f32[4,8,512,1]{0,3,2,1:T(1,128)S(1)}) fusion(f32[4,8,512,2]{0,3,2,1:T(2,128)} %bitcast.328), kind=kLoop, calls=%fused_computation.251 | loop fusion | bytes 262144 | tf_op jit(solution)/shard_map/slice | solution.py:29
  167.6 2.7 %copy.891 = f32[4,8,512,1]{2,1,3,0:T(8,128)S(1)} copy(f32[4,8,512,1]{0,3,2,1:T(1,128)} %get-tuple-element.23) | data formatting | bytes 131072
  171.6 1.1 subtract_multiply_fusion.1
  178.8 3.1 %copy.851 = f32[4,8,512,2]{0,3,2,1:T(2,128)} copy(f32[4,8,512,2]{2,1,0,3:T(8,128)S(1)} %pad_maximum_fusion.1) | data formatting | bytes 262144 | tf_op jit(solution)/shard_map/stack | solution.py:48
  181.9 2.8 %copy.852 = f32[4,16,512]{2,0,1:T(4,128)S(1)} copy(f32[4,16,512]{0,2,1:T(8,128)} %bitcast.331) | data formatting | bytes 262144 | tf_op jit(solution)/shard_map/reshape;reshape | solution.py:125
  184.8 10.5 %all_to_all.82 = f32[4,16,512]{2,0,1:T(4,128)S(1)} all-to-all(f32[4,16,512]{2,0,1:T(4,128)S(1)} %copy.852), channel_id=1, replica_groups=mesh['ens'=2,'tile'=16] {'tile'}, dimensions={1} | all-to-all | bytes 262144 | tf_op jit(solution)/shard_map/all_to_all | solution.py:124
  196.0 1.0 fusion.13
  197.5 17.9 %all-gather.10 = f32[16,1,128]{2,1,0:T(1,128)S(1)} all-gather(f32[1,1,128]{2,1,0:T(1,128)S(1)} %fusion.2), channel_id=6, replica_groups=mesh['ens'=2,'tile'=16] {'tile'}, dimensions={0}, use_global_device_ids=true | all-gather | bytes 8704 | tf_op jit(solution)/shard_map/all_gather | solution.py:84
  216.1 18.1 %all-gather.11 = f32[16,1,128]{2,1,0:T(1,128)S(1)} all-gather(f32[1,1,128]{2,1,0:T(1,128)S(1)} %convolution_bitcast_fusion.1), channel_id=7, replica_groups=mesh['ens'=2,'tile'=16] {'tile'}, dimensions={0}, use_global_device_ids=true | all-gather | bytes 8704 | tf_op jit(solution)/shard_map/all_gather | solution.py:83
  235.8 10.5 %all_to_all.83 = f32[64,1,512]{2,1,0:T(1,128)S(1)} all-to-all(f32[64,1,512]{2,1,0:T(1,128)S(1)} %reshape.712), channel_id=1, replica_groups=mesh['ens'=2,'tile'=16] {'tile'}, dimensions={0} | all-to-all | bytes 262144 | tf_op jit(solution)/shard_map/all_to_all | solution.py:142
  246.4 2.6 copy.854
  249.0 8.9 %fusion.78 = (f32[4,8,512,1]{0,3,2,1:T(1,128)}, f32[4,8,512,1]{0,3,2,1:T(1,128)S(1)}) fusion(f32[4,8,512,2]{0,3,2,1:T(2,128)} %bitcast.329), kind=kLoop, calls=%fused_computation.250 | loop fusion | bytes 262144 | tf_op jit(solution)/shard_map/slice | solution.py:29
  257.9 2.7 %copy.897 = f32[4,8,512,1]{2,1,3,0:T(8,128)S(1)} copy(f32[4,8,512,1]{0,3,2,1:T(1,128)} %get-tuple-element.21) | data formatting | bytes 131072
  261.9 1.1 subtract_multiply_fusion
  (232 shorter events, 36.3 us)
Async XLA Ops:
  0.6 2.8 %copy-start = (f32[16,64,256]{2,1,0:T(8,128)S(1)}, f32[16,64,256]{2,1,0:T(8,128)}, u32[]{:S(2)}) copy-start(f32[16,64,256]{2,1,0:T(8,128)} %param.11) | copy-start | bytes 3145732
  0.6 52.5 %copy-start.4 = (s32[16]{0:T(128)S(1)}, s32[16]{0:T(128)}, u32[]{:S(2)}) copy-start(s32[16]{0:T(128)} %param.13) | copy-start | bytes 196
  0.7 57.3 %copy-start.5 = (f32[1024]{0:T(1024)S(1)}, f32[1024]{0:T(1024)}, u32[]{:S(2)}) copy-start(f32[1024]{0:T(1024)} %param.17) | copy-start | bytes 12292
  54.3 11.4 %all-to-all-start = ((f32[64,1,512]{2,1,0:T(1,128)}), f32[64,1,512]{2,1,0:T(1,128)S(1)}, u32[]{:S(2)}, u32[]{:S(2)}) async-start(f32[64,1,512]{2,1,0:T(1,128)} %reshape.710), calls=%async_computation | async-start | bytes 262144 | tf_op jit(solution)/shard_map/all_to_all | solution.py:142
  91.4 15.1 %copy-start.7 = (s32[16]{0:T(128)S(1)}, s32[16]{0:T(128)}, u32[]{:S(2)}) copy-start(s32[16]{0:T(128)} %param.12) | copy-start | bytes 196
  91.4 15.5 %copy-start.6 = (s32[32]{0:T(128)S(1)}, s32[32]{0:T(128)}, u32[]{:S(2)}) copy-start(s32[32]{0:T(128)} %param.15) | copy-start | bytes 388
  91.4 33.6 %copy-start.2 = (f32[128]{0:T(128)S(1)}, f32[128]{0:T(128)}, u32[]{:S(2)}) copy-start(f32[128]{0:T(128)} %param.16) | copy-start | bytes 1540
  91.4 33.9 %copy-start.1 = (f32[32,64]{1,0:T(8,128)S(1)}, f32[32,64]{1,0:T(8,128)}, u32[]{:S(2)}) copy-start(f32[32,64]{1,0:T(8,128)} %param.10) | copy-start | bytes 24580
  215.9 33.1 %copy-start.3 = (f32[32,64]{1,0:T(8,128)}, f32[32,64]{1,0:T(8,128)S(1)}, u32[]{:S(2)}) copy-start(f32[32,64]{1,0:T(8,128)S(1)} %get-tuple-element.20) | copy-start | bytes 24580
where the time goes:
time: 267 us; the launch traced here: 266 us
  blocking collectives  155 us (58%)
  local copies, waits for them, and re-layouts  71.7 us (27%)
  matrix products  13.9 us (5%)
  other arithmetic  12.4 us (5%)
  waiting for transfers between devices  7.7 us (3%)
  starting transfers between devices  3.69 us (1%)
    all_gather x6, blocking collectives, carry_collect(): lax.all_gather(values[None, :], 'tile', axis=0, tiled=True)  112 us
    slice x6, local copies, waits for them, and re-layouts, haar_forward(): odd_part = paired[..., 1]  27.9 us
    all_to_all x2, blocking collectives, body(): lax.all_to_all(flux.reshape(local_lat, devices, sector_width), 'tile', sp...  21 us
    all_to_all x2, blocking collectives, body(): lax.all_to_all(grad_rows.reshape(NLAT, 1, sector_width), 'tile', split_ax...  21 us
    unnamed x28, local copies, waits for them, and re-layouts  11.5 us
    another operation x18, local copies, waits for them, and re-layouts, haar_inverse(): jnp.stack([even_part, odd_part], axis=-1)  8.73 us
    all_to_all x3, local copies, waits for them, and re-layouts, body(): lax.all_to_all(grad_rows.reshape(NLAT, 1, sector_width), 'tile', split_ax...  7.82 us
    all_to_all x1, waiting for transfers between devices, body(): lax.all_to_all(grad_rows.reshape(NLAT, 1, sector_width), 'tile', split_ax...  7.7 us
  transfers between devices with their start and end apart: 1, of which 1 were waited for; matrix products, arithmetic and copies ran while one was open for 0% of the time, Pallas kernels for 0%

commit v1 on v0

v1 whole, which is shorter than its diff:
```python
import functools
import math

import jax
import jax.numpy as jnp
from jax import lax
from jax.experimental import pallas as pl
from jax.experimental.pallas import tpu as pltpu
from jax.sharding import PartitionSpec as P

WIN = 8
NLAT = 64
SEC_STRIPS = 2
STRIP = 256
SOUNDS = 64
SB_DEV = 32
NBANDS = 128
ITERS = 3
SLOTS = 16
LANES = 128
ROWS = 8
STEP = 0.2

F32 = jnp.float32
BF16 = jnp.bfloat16
HIGHEST = lax.Precision.HIGHEST

LINE, SPOT, BAND, TOTAL, APPROX, ROW, COL, VALID, FIRST, RANK = range(10)


def momentum_weights(total_steps):
    weights = []
    current = 1.0
    for _ in range(total_steps):
        following = (1.0 + math.sqrt(1.0 + 4.0 * current * current)) / 2.0
        weights.append((current - 1.0) / following)
        current = following
    return weights


def iota(shape, axis):
    return lax.broadcasted_iota(jnp.int32, shape, axis)


def shrink(values, limit):
    return values - jnp.minimum(jnp.maximum(values, -limit), limit)


def to_col(row):
    n = row.shape[1]
    eye = iota((n, n), 0) == iota((n, n), 1)
    return jnp.sum(jnp.where(eye, row, 0.0), axis=1, keepdims=True)


def to_row(col):
    n = col.shape[0]
    eye = iota((n, n), 0) == iota((n, n), 1)
    return jnp.sum(jnp.where(eye, col, 0.0), axis=0, keepdims=True)


def exact_dot(left, right):
    return jnp.dot(left, right, precision=HIGHEST, preferred_element_type=F32)


def dot(left, right):
    return jnp.dot(left, right, preferred_element_type=F32)


def dot_nt(left, right):
    return lax.dot_general(left, right, (((1,), (1,)), ((), ())), preferred_element_type=F32)


def split(values):
    high = values.astype(BF16)
    return high, (values - high.astype(F32)).astype(BF16)


def haar_signs():
    cell = iota((STRIP, STRIP), 0)
    coef = iota((STRIP, STRIP), 1)
    out = jnp.where(coef == 0, 1.0, 0.0)
    m = 1
    while m < STRIP:
        span = STRIP // m
        level = (coef >= m) & (coef < 2 * m)
        within = cell - (coef - m) * span
        sign = jnp.where(within < span // 2, 1.0, -1.0)
        out = jnp.where(level & (within >= 0) & (within < span), sign, out)
        m *= 2
    return out.astype(BF16)


def haar_scales():
    coef = iota((1, STRIP), 1)
    out = jnp.full((1, STRIP), math.sqrt(1.0 / STRIP), F32)
    m = 1
    while m < STRIP:
        out = jnp.where((coef >= m) & (coef < 2 * m), math.sqrt(m / STRIP), out)
        m *= 2
    return out


def top_entry(spot, index, strips):
    if index == 0:
        return jnp.full(spot.shape, math.sqrt(1.0 / strips), F32)
    m = 1 << (index.bit_length() - 1)
    span = strips // m
    start = float((index - m) * span)
    half = start + span / 2
    end = start + span
    scale = math.sqrt(m / strips)
    positive = (spot >= start) & (spot < half)
    negative = (spot >= half) & (spot < end)
    return jnp.where(positive, scale, jnp.where(negative, -scale, 0.0))


def weekly(rows, sectors):
    return [sum(rows[w * sectors + 1 : (w + 1) * sectors], rows[w * sectors]) for w in range(WIN)]


def scan_back(totals, decay):
    running = totals[WIN - 1]
    out = [running]
    for w in range(WIN - 2, -1, -1):
        running = running * decay + totals[w]
        out.insert(0, running)
    return out


def scan_ahead(totals, decay):
    running = totals[0]
    out = [running]
    for w in range(1, WIN):
        running = running * decay + totals[w]
        out.append(running)
    return out


def pick(rows, index):
    out = rows[0]
    for w in range(1, len(rows)):
        out = jnp.where(index == w, rows[w], out)
    return out


def background(first, partial_rows, decay, sectors):
    counts = weekly([first[t, 0:1, :] for t in range(WIN * sectors)], sectors)
    sums = weekly([first[t, 1:2, :] for t in range(WIN * sectors)], sectors)
    partials = weekly(partial_rows, sectors)
    carried = scan_ahead(partials, decay)
    back = [
        SOUNDS * partials[w] + (SOUNDS * counts[w]) * carried[w] - sums[w] for w in range(WIN)
    ]
    returned = scan_back(back, decay)
    return [carried[w] + returned[w] / SOUNDS for w in range(WIN)], carried


def one_hot_bands(band_col):
    return jnp.where(band_col == iota((band_col.shape[0], NBANDS), 1).astype(F32), 1.0, 0.0)


def own_block_mask(rows):
    return iota((rows, SLOTS * SOUNDS), 0) == iota((rows, SLOTS * SOUNDS), 1) // SOUNDS


def back_project(chosen, high_ref, low_ref):
    wide = jnp.concatenate([chosen] * (SLOTS * SOUNDS // LANES), axis=1)
    spread = jnp.where(own_block_mask(SLOTS), wide, 0.0)
    high, low = split(spread)
    both = dot(jnp.concatenate([high, low], axis=0), high_ref[...])
    return both[:SLOTS] + both[SLOTS:] + dot(high, low_ref[...])


def forward(point, high_ref, low_ref):
    high, low = split(point)
    both = dot_nt(jnp.concatenate([high, low], axis=0), high_ref[...])
    full = both[:SLOTS] + both[SLOTS:] + dot_nt(high, low_ref[...])
    return jnp.sum(jnp.where(own_block_mask(SLOTS), full, 0.0), axis=0, keepdims=True)


def fold(weights, values):
    product = weights * values
    total = product[:, :LANES]
    for start in range(LANES, SLOTS * SOUNDS, LANES):
        total = total + product[:, start : start + LANES]
    return total + pltpu.roll(total, SOUNDS, 1)


def start_kernel(band_ref, obs_ref, out_ref):
    band = to_col(band_ref[...].astype(F32))
    hot = one_hot_bands(band)
    sums = jnp.sum(obs_ref[...], axis=1, keepdims=True)
    counted = jnp.sum(hot, axis=0, keepdims=True)
    summed = jnp.sum(hot * sums, axis=0, keepdims=True)
    for t in range(out_ref.shape[0]):
        out_ref[t, 0:1, :] = counted
        out_ref[t, 1:2, :] = summed


def prepare_kernel(
    strips,
    owners,
    jac_ref,
    obs_ref,
    row_ref,
    col_ref,
    count_ref,
    band_ref,
    weight_ref,
    high_ref,
    low_ref,
    column_ref,
    obs_grad_ref,
    obs_slot_ref,
    row_match_ref,
    info_ref,
    limit_ref,
    send_ref,
    strip_match_ref,
):
    sectors = strips // SEC_STRIPS
    strips_owner = NLAT * SEC_STRIPS // owners
    sector = lax.rem(lax.axis_index("tile"), sectors).astype(F32)
    signs = haar_signs()
    scales = haar_scales()
    chunk = STRIP
    for start in range(0, SLOTS * SOUNDS, chunk):
        high, low = split(jac_ref[start : start + chunk, :])
        changed = (dot(high, signs) + dot(low, signs)) * scales
        high, low = split(changed)
        high_ref[start : start + chunk, :] = high
        low_ref[start : start + chunk, :] = low
        per = chunk // SOUNDS
        column_ref[start // SOUNDS : start // SOUNDS + per, :] = jnp.sum(
            changed.reshape(per, SOUNDS, STRIP), axis=1
        )

    row_of = to_col(row_ref[...].astype(F32))
    col_row = col_ref[...].astype(F32)
    col_of = to_col(col_row)
    valid_row = jnp.where(iota((1, SLOTS), 1) < count_ref[...], 1.0, 0.0)
    valid = to_col(valid_row)
    line = jnp.floor(col_of / SEC_STRIPS)
    spot = sector * SEC_STRIPS + (col_of - line * SEC_STRIPS)
    row_hot = jnp.where(row_of == iota((SLOTS, SB_DEV), 1).astype(F32), 1.0, 0.0)
    band_row = band_ref[...].astype(F32)
    band = jnp.sum(row_hot * band_row, axis=1, keepdims=True)
    band = jnp.where(valid > 0.0, band, -1.0)
    observed = obs_ref[...]
    obs_slot = exact_dot(row_hot, jnp.concatenate([observed, observed], axis=1))
    obs_slot_ref[...] = obs_slot
    obs_grad = back_project(obs_slot, high_ref, low_ref)
    obs_grad_ref[...] = obs_grad
    column = column_ref[...]

    lane = iota((SLOTS, SLOTS * SOUNDS), 1) // SOUNDS
    slot = iota((SLOTS, SLOTS * SOUNDS), 0)
    row_lane = jnp.sum(jnp.where(lane == slot, row_of, 0.0), axis=0, keepdims=True)
    row_lane = jnp.where(
        jnp.sum(jnp.where(lane == slot, valid, 0.0), axis=0, keepdims=True) > 0.0, row_lane, -1.0
    )
    row_match_ref[...] = jnp.where(row_of == row_lane, 1.0, 0.0)

    same = jnp.where(col_of == col_row, 1.0, 0.0)
    before = jnp.where(iota((SLOTS, SLOTS), 1) < iota((SLOTS, SLOTS), 0), 1.0, 0.0)
    strip_match_ref[...] = same * valid_row
    first = jnp.where(jnp.sum(same * before, axis=1, keepdims=True) > 0.0, 0.0, 1.0)
    owner = jnp.floor(col_of / strips_owner)
    owner_row = jnp.floor(col_row / strips_owner)
    rank = jnp.sum(jnp.where(owner == owner_row, before, 0.0), axis=1, keepdims=True)

    at = iota((SLOTS, LANES), 1)
    info = jnp.zeros((SLOTS, LANES), F32)
    for place, values in (
        (LINE, line),
        (SPOT, spot),
        (BAND, band),
        (TOTAL, column[:, 0:1] * valid),
        (APPROX, -obs_grad[:, 0:1] * valid),
        (ROW, row_of),
        (COL, col_of),
        (VALID, valid),
        (FIRST, first),
        (RANK, rank),
    ):
        info = jnp.where(at == place, values, info)
    info_ref[...] = info

    local = iota((1, LANES), 1)
    limits_low = jnp.zeros((SLOTS, LANES), F32)
    limits_high = jnp.zeros((SLOTS, LANES), F32)
    for j in range(strips):
        low_row = jnp.zeros((1, LANES), F32)
        m = 1
        while m < LANES:
            start = strips * m + j * m
            block = weight_ref[0:1, start // LANES * LANES : start // LANES * LANES + LANES]
            shift = (m - start % LANES) % LANES
            moved = pltpu.roll(jnp.broadcast_to(block, (ROWS, LANES)), shift, 1)[0:1] if shift else block
            low_row = jnp.where((local >= m) & (local < 2 * m), moved, low_row)
            m *= 2
        high_row = weight_ref[0:1, (strips + j) * LANES : (strips + j + 1) * LANES]
        limits_low = jnp.where(spot == float(j), low_row, limits_low)
        limits_high = jnp.where(spot == float(j), high_row, limits_high)
    limit_ref[:, :LANES] = STEP * limits_low
    limit_ref[:, LANES:] = STEP * limits_high

    shape = (owners * ROWS, 4 * SLOTS)
    target = (iota(shape, 0) // ROWS).astype(F32)
    kind = iota(shape, 0) % ROWS
    group = iota(shape, 1) // SLOTS
    slim = iota((SLOTS, 4 * SLOTS), 1) % SLOTS == iota((SLOTS, 4 * SLOTS), 0)
    owner_wide = jnp.sum(jnp.where(slim, owner, 0.0), axis=0, keepdims=True)
    rank_wide = jnp.sum(jnp.where(slim, rank, 0.0), axis=0, keepdims=True)
    kind_f = kind.astype(F32)
    mine = owner_wide == target
    hit = (group == 0) & (kind_f == 2.0 * rank_wide)
    hit = hit | ((group == 1) & (kind_f == 2.0 * rank_wide + 1.0))
    hit = hit | ((group == 2) & (kind == 5))
    hit = (hit & mine) | ((iota(shape, 1) == 3 * SLOTS) & (kind == 4))
    send_ref[...] = jnp.where(hit, 1.0, 0.0)


def fill_message(out_ref, send, strips_part, meta, partial):
    bottom = jnp.where(iota((SLOTS, LANES), 0) == 0, partial, 0.0)
    stacked = jnp.concatenate([strips_part[:, :LANES], strips_part[:, LANES:], meta, bottom], axis=0)
    rows = exact_dot(send, stacked)
    out_ref[...] = rows.reshape(out_ref.shape)


def advance(strips, scalar, local_grad, column, info, info_all, approx_all, strip_match, limit, top_limit, point, top):
    c_all = jnp.sum(one_hot_bands(info_all[:, BAND : BAND + 1]) * scalar, axis=1, keepdims=True)
    grads = exact_dot(strip_match, local_grad + c_all[:SLOTS] * column)
    approx_row = to_row(approx_all + c_all * info_all[:, TOTAL : TOTAL + 1])
    line_row = to_row(info_all[:, LINE : LINE + 1])
    spot_row = to_row(info_all[:, SPOT : SPOT + 1])
    on_line = jnp.where(info[:, LINE : LINE + 1] == line_row, approx_row, 0.0)
    at = iota((SLOTS, LANES), 1)
    top_grad = jnp.zeros((SLOTS, LANES), F32)
    for t in range(strips):
        value = jnp.sum(on_line * top_entry(spot_row, t, strips), axis=1, keepdims=True)
        top_grad = jnp.where(at == t, value, top_grad)
    if point is None:
        return shrink(-STEP * grads, limit), shrink(-STEP * top_grad, top_limit)
    return shrink(point - STEP * grads, limit), shrink(top - STEP * top_grad, top_limit)


def with_approx(point, top, info, strips):
    at = iota((SLOTS, LANES), 1)
    matrix = jnp.zeros((SLOTS, LANES), F32)
    for t in range(strips):
        matrix = jnp.where(at == t, top_entry(info[:, SPOT : SPOT + 1], t, strips), matrix)
    approx = jnp.sum(matrix * top, axis=1, keepdims=True)
    return jnp.where(iota((SLOTS, STRIP), 1) == 0, approx, point)


def band_partial(point, column, info):
    dots = jnp.sum(point * column, axis=1, keepdims=True)
    hot = one_hot_bands(info[:, BAND : BAND + 1])
    return jnp.sum(hot * dots, axis=0, keepdims=True) / SOUNDS


def gather_info(info_ref, others_refs):
    return jnp.concatenate([info_ref[...]] + [r[...] for r in others_refs], axis=0)


def first_step_kernel(
    strips,
    owners,
    first_ref,
    info_ref,
    column_ref,
    obs_grad_ref,
    limit_ref,
    strip_match_ref,
    send_ref,
    decay_ref,
    weight_ref,
    *rest,
):
    sectors = strips // SEC_STRIPS
    others_refs = rest[: sectors - 1]
    point_ref, top_ref, message_ref = rest[sectors - 1 :]
    window = lax.axis_index("tile") // sectors
    decay = decay_ref[...]
    sums = weekly([first_ref[t, 1:2, :] for t in range(owners)], sectors)
    returned = scan_back([-s for s in sums], decay)
    scalar = pick(returned, window) / SOUNDS
    info = info_ref[...]
    info_all = gather_info(info_ref, others_refs)
    column = column_ref[...]
    top_limit = STEP * weight_ref[0:1, :LANES]
    updated, top = advance(
        strips,
        scalar,
        -obs_grad_ref[...],
        column,
        info,
        info_all,
        info_all[:, APPROX : APPROX + 1],
        strip_match_ref[...],
        limit_ref[...],
        top_limit,
        None,
        None,
    )
    point = with_approx(updated, top, info, strips)
    point_ref[...] = point
    top_ref[...] = top
    partial = band_partial(point, column, info)
    at = iota((SLOTS, LANES), 1).astype(F32)
    strips_owner = NLAT * SEC_STRIPS // owners
    col = info[:, COL : COL + 1]
    local = col - jnp.floor(col / strips_owner) * strips_owner
    base = info[:, RANK : RANK + 1] * (LANES // 2)
    meta = jnp.where(at == base, local + 1.0, 0.0)
    meta = jnp.where(at == base + 1.0, info[:, BAND : BAND + 1] + 1.0, meta)
    fill_message(message_ref, send_ref[...], column * info[:, VALID : VALID + 1], meta, partial)


def local_grad_kernel(point_ref, high_ref, low_ref, row_match_ref, obs_slot_ref, info_ref, grad_ref, approx_ref):
    values = forward(point_ref[...], high_ref, low_ref)
    chosen = fold(row_match_ref[...], values) - obs_slot_ref[...]
    grad = back_project(chosen, high_ref, low_ref)
    grad_ref[...] = grad
    approx_ref[...] = jnp.broadcast_to(
        grad[:, 0:1] * info_ref[:, VALID : VALID + 1], approx_ref.shape
    )


def second_step_kernel(
    strips,
    owners,
    beta,
    first_ref,
    second_ref,
    info_ref,
    column_ref,
    grad_ref,
    limit_ref,
    strip_match_ref,
    send_ref,
    decay_ref,
    weight_ref,
    point_ref,
    top_ref,
    high_ref,
    low_ref,
    row_match_ref,
    obs_slot_ref,
    obs_ref,
    approx_ref,
    *rest,
):
    sectors = strips // SEC_STRIPS
    others_refs = rest[: sectors - 1]
    approx_refs = rest[sectors - 1 : 2 * (sectors - 1)]
    message_ref, differ_ref = rest[2 * (sectors - 1) :]
    my_index = lax.axis_index("tile")
    window = my_index // sectors
    sector = lax.rem(my_index, sectors).astype(F32)
    decay = decay_ref[...]
    combined, _ = background(first_ref, [second_ref[t, 4:5, :] for t in range(owners)], decay, sectors)
    info = info_ref[...]
    info_all = gather_info(info_ref, others_refs)
    approx_all = gather_info(approx_ref, approx_refs)[:, 0:1]
    column = column_ref[...]
    top_limit = STEP * weight_ref[0:1, :LANES]
    old = point_ref[...]
    old_top = top_ref[...]
    updated, top = advance(
        strips,
        pick(combined, window),
        grad_ref[...],
        column,
        info,
        info_all,
        approx_all,
        strip_match_ref[...],
        limit_ref[...],
        top_limit,
        old,
        old_top,
    )
    point = updated + beta * (updated - old)
    top = top + beta * (top - old_top)
    point = with_approx(point, top, info, strips)
    partial = band_partial(point, column, info)
    values = forward(point, high_ref, low_ref)
    chosen = fold(row_match_ref[...], values) - obs_slot_ref[...]
    grad = back_project(chosen, high_ref, low_ref)

    valid = info[:, VALID : VALID + 1]
    lane = iota((SLOTS, SLOTS * SOUNDS), 1) // SOUNDS
    slot = iota((SLOTS, SLOTS * SOUNDS), 0)
    row_lane = jnp.sum(
        jnp.where(lane == slot, (info[:, ROW : ROW + 1] + 1.0) * valid, 0.0), axis=0, keepdims=True
    )
    per_row = jnp.where(
        iota((SB_DEV, SLOTS * SOUNDS), 0).astype(F32) + 1.0 == row_lane, 1.0, 0.0
    )
    differ_ref[...] = fold(per_row, values)[:, :SOUNDS] - obs_ref[...]

    count = info_all.shape[0]
    line_row = to_row(info_all[:, LINE : LINE + 1])
    sector_row = to_row(jnp.floor(info_all[:, SPOT : SPOT + 1] / SEC_STRIPS))
    lane = iota((SLOTS, count), 1)
    earlier = jnp.where(lane < SLOTS, jnp.where(lane < iota((SLOTS, count), 0), 1.0, 0.0), jnp.where(sector_row < sector, 1.0, 0.0))
    taken = jnp.sum(jnp.where(info[:, LINE : LINE + 1] == line_row, earlier, 0.0), axis=1, keepdims=True)
    top = jnp.where(taken > 0.0, 0.0, top)
    rank = info[:, RANK : RANK + 1]
    meta = jnp.where(rank == 0.0, pltpu.roll(top, ROWS, 1), pltpu.roll(top, LANES // 2 + ROWS, 1))
    kept = jnp.where(iota((SLOTS, STRIP), 1) == 0, 0.0, point * info[:, FIRST : FIRST + 1])
    fill_message(message_ref, send_ref[...], kept - STEP * (valid * grad), meta, partial)


def place_kernel(strips, owners, second_ref, place_ref, band_hot_ref):
    sectors = strips // SEC_STRIPS
    lines = NLAT // owners
    count = owners * ROWS
    meta = second_ref[:, 5, :]
    wide = (owners, count)
    pair_of = iota(wide, 1) // ROWS == iota(wide, 0)
    kind = iota((1, count), 1) % ROWS
    tall = (count, owners)
    tall_pair = iota(tall, 0) // ROWS == iota(tall, 1)
    tall_kind = iota((count, 1), 0) % ROWS
    strip_rows = []
    band_col = jnp.zeros((count, 1), F32)
    for q in range(2):
        strip = meta[:, q * (LANES // 2) : q * (LANES // 2) + 1]
        band = meta[:, q * (LANES // 2) + 1 : q * (LANES // 2) + 2]
        strip_rows.append(jnp.sum(jnp.where(pair_of, strip, 0.0), axis=0, keepdims=True) - 1.0)
        band_tall = jnp.sum(jnp.where(tall_pair, to_row(band), 0.0), axis=1, keepdims=True)
        band_col = jnp.where(tall_kind // 2 == q, band_tall, band_col)
    band_hot_ref[...] = one_hot_bands(band_col - 1.0)

    def line_of(strip):
        return jnp.floor(strip / SEC_STRIPS)

    blocks = lines * WIN
    pair = iota((1, count), 1) // ROWS
    window = pair // sectors
    sector = (pair - window * sectors).astype(F32)
    line_col = (iota((blocks, 1), 0) // WIN).astype(F32)
    window_col = iota((blocks, 1), 0) % WIN
    strip_row = jnp.where(kind < 2, strip_rows[0], strip_rows[1])
    slot_line = line_of(strip_row)
    slot_spot = sector * SEC_STRIPS + strip_row - slot_line * SEC_STRIPS
    base = (window == window_col) & (slot_line == line_col) & (strip_row >= 0.0)
    base = jnp.where(base & (kind < 4), 1.0, 0.0)
    for half in range(2):
        part = jnp.where(kind % 2 == half, base, 0.0)
        for j in range(strips):
            start = (half * strips + j) * blocks
            place_ref[start : start + blocks, :] = jnp.where(slot_spot == float(j), part, 0.0)
    for q in range(2):
        start = (2 * strips + q) * blocks
        hit = (window == window_col) & (line_of(strip_rows[q]) == line_col) & (strip_rows[q] >= 0.0) & (kind == 5)
        place_ref[start : start + blocks, :] = jnp.where(hit, 1.0, 0.0)


def finish_kernel(
    strips,
    owners,
    first_ref,
    second_ref,
    third_ref,
    place_ref,
    band_hot_ref,
    decay_ref,
    weight_ref,
    differ_ref,
    band_ref,
    out_ref,
    misfit_ref,
):
    sectors = strips // SEC_STRIPS
    blocks = NLAT // owners * WIN
    count = owners * ROWS
    window = lax.axis_index("tile") // sectors
    combined, carried = background(
        first_ref, [third_ref[t, 4:5, :] for t in range(owners)], decay_ref[...], sectors
    )
    hot = one_hot_bands(to_col(band_ref[...].astype(F32)))
    offset = jnp.sum(hot * pick(carried, window), axis=1, keepdims=True)
    misfit_ref[...] = differ_ref[...] + offset

    spread = jnp.concatenate(
        [jnp.broadcast_to(row, (sectors * ROWS, NBANDS)) for row in combined], axis=0
    )
    scalars = jnp.sum(band_hot_ref[...] * spread, axis=1, keepdims=True)
    third = third_ref[...].reshape(count, LANES)
    second = second_ref[...].reshape(count, LANES)
    kind = iota((count, 1), 0) % ROWS
    rows = third - (STEP * scalars) * jnp.where(kind < 4, second, 0.0)
    placed = exact_dot(place_ref[...], rows)

    lane = iota((1, LANES), 1)
    for j in range(strips):
        start = (strips + j) * LANES
        values = placed[(strips + j) * blocks : (strips + j + 1) * blocks]
        out_ref[:, start : start + LANES] = shrink(values, STEP * weight_ref[0:1, start : start + LANES])

    low = [placed[j * blocks : (j + 1) * blocks] for j in range(strips)]
    tops = [placed[(2 * strips + q) * blocks : (2 * strips + q + 1) * blocks] for q in range(2)]
    top = pltpu.roll(tops[0], LANES - ROWS, 1) + pltpu.roll(tops[1], LANES // 2 - ROWS, 1)
    made = [jnp.zeros((blocks, LANES), F32) for _ in range(strips)]
    for t in range(strips):
        value = jnp.zeros((blocks, 1), F32)
        for j in range(strips):
            entry = top_value(j, t, strips)
            if entry:
                value = value + entry * low[j][:, 0:1]
        made[0] = jnp.where(lane == t, value + top, made[0])
    m = 1
    while m < LANES:
        for j in range(strips):
            start = strips * m + j * m
            block = start // LANES
            shift = (start % LANES - m) % LANES
            moved = pltpu.roll(low[j], shift, 1) if shift else low[j]
            inside = (lane >= start % LANES) & (lane < start % LANES + m)
            made[block] = jnp.where(inside, moved, made[block])
        m *= 2
    for block in range(strips):
        start = block * LANES
        out_ref[:, start : start + LANES] = shrink(made[block], STEP * weight_ref[0:1, start : start + LANES])


def top_value(spot, index, strips):
    if index == 0:
        return math.sqrt(1.0 / strips)
    m = 1 << (index.bit_length() - 1)
    span = strips // m
    within = spot - (index - m) * span
    if within < 0 or within >= span:
        return 0.0
    return math.sqrt(m / strips) * (1.0 if within < span // 2 else -1.0)


def call(kernel, outs, *operands):
    return pl.pallas_call(
        kernel,
        out_shape=[jax.ShapeDtypeStruct(shape, dtype) for shape, dtype in outs],
        compiler_params=pltpu.CompilerParams(vmem_limit_bytes=48 * 1024 * 1024),
    )(*operands)


def body(
    observations,
    jacobian,
    block_row,
    block_col,
    block_count,
    block_band,
    carry_decay,
    sparsity_weight,
):
    owners = lax.axis_size("tile")
    sectors = owners // WIN
    strips = sectors * SEC_STRIPS
    lines = NLAT // owners
    betas = momentum_weights(ITERS)
    rows = block_row.reshape(1, SLOTS)
    cols = block_col.reshape(1, SLOTS)
    count = block_count.reshape(1, 1)
    bands = block_band.reshape(1, SB_DEV)
    decay = carry_decay.reshape(1, NBANDS)
    weight = sparsity_weight.reshape(1, -1)
    flat = jacobian.reshape(SLOTS * SOUNDS, STRIP)
    message = ((owners, ROWS, LANES), F32)
    table = ((SLOTS, LANES), F32)
    strip_rows = ((SLOTS, STRIP), F32)

    def trade(values):
        return lax.all_to_all(values, "tile", 0, 0, tiled=True)

    def from_sectors(values):
        found = []
        for shift in range(1, sectors):
            pairs = [
                (d, d // sectors * sectors + (d + shift) % sectors) for d in range(owners)
            ]
            found.append(lax.ppermute(values, "tile", pairs))
        return found

    (first,) = call(start_kernel, [((owners, 2, LANES), F32)], bands, observations)
    first = trade(first)
    high, low, column, obs_grad, obs_slot, row_match, info, limit, send, strip_match = call(
        functools.partial(prepare_kernel, strips, owners),
        [
            ((SLOTS * SOUNDS, STRIP), BF16),
            ((SLOTS * SOUNDS, STRIP), BF16),
            strip_rows,
            strip_rows,
            table,
            ((SLOTS, SLOTS * SOUNDS), F32),
            table,
            strip_rows,
            ((owners * ROWS, 4 * SLOTS), F32),
            ((SLOTS, SLOTS), F32),
        ],
        flat,
        observations,
        rows,
        cols,
        count,
        bands,
        weight,
    )
    others = from_sectors(info)
    point, top, second = call(
        functools.partial(first_step_kernel, strips, owners),
        [strip_rows, table, message],
        first,
        info,
        column,
        obs_grad,
        limit,
        strip_match,
        send,
        decay,
        weight,
        *others,
    )
    second = trade(second)
    grad, approx = call(
        local_grad_kernel, [strip_rows, table], point, high, low, row_match, obs_slot, info
    )
    others_approx = from_sectors(approx)
    third, differ = call(
        functools.partial(second_step_kernel, strips, owners, betas[1]),
        [message, ((SB_DEV, SOUNDS), F32)],
        first,
        second,
        info,
        column,
        grad,
        limit,
        strip_match,
        send,
        decay,
        weight,
        point,
        top,
        high,
        low,
        row_match,
        obs_slot,
        observations,
        approx,
        *others,
        *others_approx,
    )
    third = trade(third)
    place, band_hot = call(
        functools.partial(place_kernel, strips, owners),
        [
            (((2 * strips + 2) * lines * WIN, owners * ROWS), F32),
            ((owners * ROWS, NBANDS), F32),
        ],
        second,
    )
    coeffs, misfit = call(
        functools.partial(finish_kernel, strips, owners),
        [((lines * WIN, strips * STRIP), F32), ((SB_DEV, SOUNDS), F32)],
        first,
        second,
        third,
        place,
        band_hot,
        decay,
        weight,
        differ,
        bands,
    )
    return (coeffs.reshape(lines, WIN, strips * STRIP), misfit)


def solution(mesh):
    return jax.shard_map(
        body,
        mesh=mesh,
        in_specs=(
            P(("ens", "tile"), None),
            P("tile", None, None),
            P("tile"),
            P("tile"),
            P("tile"),
            P("tile"),
            P(),
            P(),
        ),
        out_specs=(P(("ens", "tile"), None, None), P(("ens", "tile"), None)),
        check_vma=False,
    )
```

time: 267 us -> 44.6 us (0.17)
  blocking collectives: 155 us -> 0 us
  local copies, waits for them, and re-layouts: 71.7 us -> 3.91 us
  matrix products: 13.9 us -> 0 us
  starting transfers between devices: 3.69 us -> 16.5 us
  other arithmetic: 12.4 us -> 0 us
  Pallas kernels: 0 us -> 8.17 us
  waiting for transfers between devices: 7.7 us -> 14.2 us
    all_gather x6 -> x0, blocking collectives: 112 us -> none  [carry_collect(): lax.all_gather(values[None, :], 'tile', axis=0, tiled=True)]
    all_to_all x4 -> x0, blocking collectives: 42.1 us -> none  [the longest x2 21 us: body(): lax.all_to_all(flux.reshape(local_lat, devices, sector_width), 'tile', sp...]
    slice x9 -> x0, local copies, waits for them, and re-layouts: 28 us -> none  [the longest x6 27.9 us: haar_forward(): odd_part = paired[..., 1]]
    another operation x20 -> x0, local copies, waits for them, and re-layouts: 14.5 us -> none  [the longest x18 8.73 us: haar_inverse(): jnp.stack([even_part, odd_part], axis=-1)]
    dot_general x27 -> x0, matrix products: 13.9 us -> none  [the longest x3 2.87 us: forward_blocks(): jnp.einsum('kis,ks->ki', jacobian, picked, precision=highest)]
    all_to_all x1 -> x3, starting transfers between devices: 3.69 us -> 15.6 us  [trade(): return lax.all_to_all(values, 'tile', 0, 0, tiled=True)]
    pallas_call x0 -> x7, Pallas kernels: none -> 8.17 us  [call(): pl.pallas_call(kernel, out_shape=[jax.ShapeDtypeStruct(shape, dtype) for...]
    all_to_all x3 -> x0, local copies, waits for them, and re-layouts: 7.82 us -> none  [body(): lax.all_to_all(grad_rows.reshape(NLAT, 1, sector_width), 'tile', split_ax...]
  transfers between devices with their start and end apart: 1 -> 5, of which waited for: 1 -> 5; matrix products, arithmetic and copies ran while one was open for 0% -> 0% of each run, Pallas kernels for 0% -> 6%
where the time goes in v1:
time: 44.6 us; the launch traced here: 44.1 us
  starting transfers between devices  16.5 us (37%)
  waiting for transfers between devices  14.2 us (32%)
  Pallas kernels  8.17 us (18%)
  local copies, waits for them, and re-layouts  3.91 us (9%)
  between operations  1.36 us (3%)
    all_to_all x3, starting transfers between devices, trade(): return lax.all_to_all(values, 'tile', 0, 0, tiled=True)  15.6 us
    all_to_all x3, waiting for transfers between devices, trade(): return lax.all_to_all(values, 'tile', 0, 0, tiled=True)  12.5 us
    pallas_call x7, Pallas kernels, call(): pl.pallas_call(kernel, out_shape=[jax.ShapeDtypeStruct(shape, dtype) for...  8.17 us
    unnamed x16, local copies, waits for them, and re-layouts  3.91 us
    ppermute x2, waiting for transfers between devices, from_sectors(): found.append(lax.ppermute(values, 'tile', pairs))  1.66 us
  transfers between devices with their start and end apart: 5, of which 5 were waited for; matrix products, arithmetic and copies ran while one was open for 0% of the time, Pallas kernels for 6%

profile of v1, /device:TPU:0, one launch (start us, length us, event | category | flops | bytes accessed | tf_op | source)
XLA Modules:
  0.0 44.1 jit_solution(11118879953668081131)
XLA Ops:
  0.6 0.0 copy-start.5
  0.6 0.6 %copy-done.5 = s32[32]{0:T(128)S(1)} copy-done((s32[32]{0:T(128)S(1)}, s32[32]{0:T(128)}, u32[]{:S(2)}) %copy-start.5) | copy-done | bytes 152
  1.3 0.0 copy-start.1
  1.3 0.7 %copy-done.1 = f32[32,64]{1,0:T(8,128)S(1)} copy-done((f32[32,64]{1,0:T(8,128)S(1)}, f32[32,64]{1,0:T(8,128)}, u32[]{:S(2)}) %copy-start.1) | copy-done | bytes 8216
  2.0 0.7 %shard_map.95 = f32[16,2,128]{2,1,0:T(2,128)} custom-call(s32[1,32]{1,0:T(1,128)S(1)} %bitcast.17, f32[32,64]{1,0:T(8,128)S(1)} %copy-done.1), custom_call_target="tpu_custom_call" | custom-call | tf_op jit(solution)/shard_map/pallas_call | solution.py:643
  2.7 0.0 copy-start.2
  2.7 7.5 %all-to-all-start = ((f32[16,2,128]{2,1,0:T(2,128)}), f32[16,2,128]{2,1,0:T(2,128)S(1)}, u32[]{:S(2)}, u32[]{:S(2)}) async-start(f32[16,2,128]{2,1,0:T(2,128)} %shard_map.95), calls=%async_computation | async-start | bytes 32768 | tf_op jit(solution)/shard_map/all_to_all | solution.py:677
  10.9 0.0 copy-start.3
  10.9 0.0 copy-start.6
  10.9 0.0 copy-start.7
  10.9 0.0 copy-done.2
  10.9 0.6 %copy-done.3 = f32[1024]{0:T(1024)S(1)} copy-done((f32[1024]{0:T(1024)S(1)}, f32[1024]{0:T(1024)}, u32[]{:S(2)}) %copy-start.3) | copy-done | bytes 4120
  11.6 0.0 copy-done.6
  11.6 0.0 copy-done.7
  11.6 0.0 copy-start
  11.6 1.2 %copy-done = f32[16,64,256]{2,1,0:T(8,128)S(1)} copy-done((f32[16,64,256]{2,1,0:T(8,128)S(1)}, f32[16,64,256]{2,1,0:T(8,128)}, u32[]{:S(2)}) %copy-start) | copy-done | bytes 1048600
  12.8 1.3 %shard_map.96 = (bf16[1024,256]{1,0:T(8,128)(2,1)S(1)}, bf16[1024,256]{1,0:T(8,128)(2,1)S(1)}, f32[16,256]{1,0:T(8,128)S(1)}, f32[16,256]{1,0:T(8,128)S(1)}, f32...) custom-call(f32[1024,256]{1,0:T(8,128)S(1)} %bitcast.9, ...), custom_call_target="tpu_custom_call" | custom-call | tf_op jit(solution)/shard_map/pallas_call | solution.py:643
  14.1 0.4 collective-permute-start
  14.5 0.8 %collective-permute-done.rest_0_ = f32[16,128]{1,0:T(8,128)S(1)} collective-permute-done((f32[16,128]{1,0:T(8,128)S(1)}, f32[16,128]{1,0:T(8,128)S(1)}, u32[]{:S(2)}, u32[]{:S(2)}) %collective-permute-start) | collective-permute-done | bytes 8224 | tf_op jit(solution)/shard_map/ppermute | solution.py:685
  15.4 1.4 %all-to-all-done.first_ref = f32[16,2,128]{2,1,0:T(2,128)S(1)} async-done(((f32[16,2,128]{2,1,0:T(2,128)}), f32[16,2,128]{2,1,0:T(2,128)S(1)}, u32[]{:S(2)}, u32[]{:S(2)}) %all-to-all-start) | async-done | bytes 16416 | tf_op jit(solution)/shard_map/all_to_all | solution.py:677
  16.7 0.7 %copy-done.4 = f32[128]{0:T(128)S(1)} copy-done((f32[128]{0:T(128)S(1)}, f32[128]{0:T(128)}, u32[]{:S(2)}) %copy-start.4) | copy-done | bytes 536
  17.4 1.4 %shard_map.97 = (f32[16,256]{1,0:T(8,128)S(1)}, f32[16,128]{1,0:T(8,128)S(1)}, f32[16,8,128]{2,1,0:T(8,128)}) custom-call(f32[16,2,128]{2,1,0:T(2,128)S(1)} %all-to-all-done.first_ref, f32[16,128]{1,0:T(8,128)S(1)} %get-tuple-element.23.info_ref, f32[16,256]{1,0:T(8,128)S(1)} %get-tuple-element.24.column_ref, f32[16,256]{1,0:T(8,128)S(1)} %get-tuple-element.25.obs_grad_ref, ...), custom_call_target="tpu_custom_call" | custom-call | tf_op jit(solution)/shard_map/pallas_call | solution.py:643
  18.8 4.6 %all-to-all-start.1 = ((f32[16,8,128]{2,1,0:T(8,128)}), f32[16,8,128]{2,1,0:T(8,128)S(1)}, u32[]{:S(2)}, u32[]{:S(2)}) async-start(f32[16,8,128]{2,1,0:T(8,128)} %get-tuple-element.29), calls=%async_computation.1 | async-start | bytes 131072 | tf_op jit(solution)/shard_map/all_to_all | solution.py:677
  23.4 1.0 %shard_map.98 = (f32[16,256]{1,0:T(8,128)S(1)}, f32[16,128]{1,0:T(8,128)S(1)}) custom-call(f32[16,256]{1,0:T(8,128)S(1)} %get-tuple-element.30.point_ref, bf16[1024,256]{1,0:T(8,128)(2,1)S(1)} %get-tuple-element.31.high_ref, bf16[1024,256]{1,0:T(8,128)(2,1)S(1)} %get-tuple-element.32.low_ref, f32[16,1024]{1,0:T(8,128)S(1)} %get-tuple-element.33.row_match_ref, ...), custom_call_target="tpu_custom_call" | custom-call | tf_op jit(solution)/shard_map/pallas_call | solution.py:643
  24.4 0.4 collective-permute-start.1
  24.8 0.8 %collective-permute-done.1.rest_1_ = f32[16,128]{1,0:T(8,128)S(1)} collective-permute-done((f32[16,128]{1,0:T(8,128)S(1)}, f32[16,128]{1,0:T(8,128)S(1)}, u32[]{:S(2)}, u32[]{:S(2)}) %collective-permute-start.1) | collective-permute-done | bytes 8224 | tf_op jit(solution)/shard_map/ppermute | solution.py:685
  25.7 4.6 %all-to-all-done.1.second_ref = f32[16,8,128]{2,1,0:T(8,128)S(1)} async-done(((f32[16,8,128]{2,1,0:T(8,128)}), f32[16,8,128]{2,1,0:T(8,128)S(1)}, u32[]{:S(2)}, u32[]{:S(2)}) %all-to-all-start.1) | async-done | bytes 65568 | tf_op jit(solution)/shard_map/all_to_all | solution.py:677
  30.3 2.2 %shard_map.99 = (f32[16,8,128]{2,1,0:T(8,128)}, f32[32,64]{1,0:T(8,128)S(1)}) custom-call(f32[16,2,128]{2,1,0:T(2,128)S(1)} %all-to-all-done.first_ref, f32[16,8,128]{2,1,0:T(8,128)S(1)} %all-to-all-done.1.second_ref, f32[16,128]{1,0:T(8,128)S(1)} %get-tuple-element.23.info_ref, f32[16,256]{1,0:T(8,128)S(1)} %get-tuple-element.24.column_ref, ...), custom_call_target="tpu_custom_call" | custom-call | tf_op jit(solution)/shard_map/pallas_call | solution.py:643
  32.5 3.5 %all-to-all-start.2 = ((f32[16,8,128]{2,1,0:T(8,128)}), f32[16,8,128]{2,1,0:T(8,128)S(1)}, u32[]{:S(2)}, u32[]{:S(2)}) async-start(f32[16,8,128]{2,1,0:T(8,128)} %get-tuple-element.38), calls=%async_computation.2 | async-start | bytes 131072 | tf_op jit(solution)/shard_map/all_to_all | solution.py:677
  36.0 0.3 shard_map.100
  36.3 6.5 %all-to-all-done.2.third_ref = f32[16,8,128]{2,1,0:T(8,128)S(1)} async-done(((f32[16,8,128]{2,1,0:T(8,128)}), f32[16,8,128]{2,1,0:T(8,128)S(1)}, u32[]{:S(2)}, u32[]{:S(2)}) %all-to-all-start.2) | async-done | bytes 65568 | tf_op jit(solution)/shard_map/all_to_all | solution.py:677
  42.8 1.2 %shard_map.101 = (f32[32,1024]{1,0:T(8,128)}, f32[32,64]{1,0:T(8,128)}) custom-call(f32[16,2,128]{2,1,0:T(2,128)S(1)} %all-to-all-done.first_ref, f32[16,8,128]{2,1,0:T(8,128)S(1)} %all-to-all-done.1.second_ref, f32[16,8,128]{2,1,0:T(8,128)S(1)} %all-to-all-done.2.third_ref, f32[320,128]{1,0:T(8,128)S(1)} %get-tuple-element.39.place_ref, ...), custom_call_target="tpu_custom_call" | custom-call | tf_op jit(solution)/shard_map/pallas_call | solution.py:643
  (1 shorter events, 0.0 us)
Async XLA Ops:
  0.6 0.7 %copy-start.5 = (s32[32]{0:T(128)S(1)}, s32[32]{0:T(128)}, u32[]{:S(2)}) copy-start(s32[32]{0:T(128)} %param.13) | copy-start | bytes 388
  1.3 0.7 %copy-start.1 = (f32[32,64]{1,0:T(8,128)S(1)}, f32[32,64]{1,0:T(8,128)}, u32[]{:S(2)}) copy-start(f32[32,64]{1,0:T(8,128)} %obs_ref.5) | copy-start | bytes 24580
  2.7 8.2 %copy-start.2 = (f32[32,64]{1,0:T(8,128)S(1)}, f32[32,64]{1,0:T(8,128)}, u32[]{:S(2)}) copy-start(f32[32,64]{1,0:T(8,128)} %obs_ref.5) | copy-start | bytes 24580
  2.7 14.0 %all-to-all-start = ((f32[16,2,128]{2,1,0:T(2,128)}), f32[16,2,128]{2,1,0:T(2,128)S(1)}, u32[]{:S(2)}, u32[]{:S(2)}) async-start(f32[16,2,128]{2,1,0:T(2,128)} %shard_map.95), calls=%async_computation | async-start | bytes 32768 | tf_op jit(solution)/shard_map/all_to_all | solution.py:677
  10.9 0.7 %copy-start.3 = (f32[1024]{0:T(1024)S(1)}, f32[1024]{0:T(1024)}, u32[]{:S(2)}) copy-start(f32[1024]{0:T(1024)} %param.15) | copy-start | bytes 12292
  10.9 0.7 %copy-start.6 = (s32[16]{0:T(128)S(1)}, s32[16]{0:T(128)}, u32[]{:S(2)}) copy-start(s32[16]{0:T(128)} %param.10) | copy-start | bytes 196
  10.9 0.7 %copy-start.7 = (s32[16]{0:T(128)S(1)}, s32[16]{0:T(128)}, u32[]{:S(2)}) copy-start(s32[16]{0:T(128)} %param.11) | copy-start | bytes 196
  11.6 1.2 %copy-start = (f32[16,64,256]{2,1,0:T(8,128)S(1)}, f32[16,64,256]{2,1,0:T(8,128)}, u32[]{:S(2)}) copy-start(f32[16,64,256]{2,1,0:T(8,128)} %param.9) | copy-start | bytes 3145732
  14.1 1.3 %collective-permute-start = (f32[16,128]{1,0:T(8,128)S(1)}, f32[16,128]{1,0:T(8,128)S(1)}, u32[]{:S(2)}, u32[]{:S(2)}) collective-permute-start(f32[16,128]{1,0:T(8,128)S(1)} %get-tuple-element.23.info_ref), channel_id=1, source_target_pairs={{0,1},{1,0},{2,3},{3,2},{4,5},{5,4},{6,7},{7,6},{8,9},{9,8},{10,11... | collective-permute-start | bytes 24584 | tf_op jit(solution)/shard_map/ppermute | solution.py:685
  16.7 0.7 %copy-start.4 = (f32[128]{0:T(128)S(1)}, f32[128]{0:T(128)}, u32[]{:S(2)}) copy-start(f32[128]{0:T(128)} %param.14) | copy-start | bytes 1540
  18.8 11.5 %all-to-all-start.1 = ((f32[16,8,128]{2,1,0:T(8,128)}), f32[16,8,128]{2,1,0:T(8,128)S(1)}, u32[]{:S(2)}, u32[]{:S(2)}) async-start(f32[16,8,128]{2,1,0:T(8,128)} %get-tuple-element.29), calls=%async_computation.1 | async-start | bytes 131072 | tf_op jit(solution)/shard_map/all_to_all | solution.py:677
  24.4 1.2 %collective-permute-start.1 = (f32[16,128]{1,0:T(8,128)S(1)}, f32[16,128]{1,0:T(8,128)S(1)}, u32[]{:S(2)}, u32[]{:S(2)}) collective-permute-start(f32[16,128]{1,0:T(8,128)S(1)} %get-tuple-element.37.approx_ref), channel_id=1, source_target_pairs={{0,1},{1,0},{2,3},{3,2},{4,5},{5,4},{6,7},{7,6},{8,9},{9,8},{10,11... | collective-permute-start | bytes 24584 | tf_op jit(solution)/shard_map/ppermute | solution.py:685
  32.5 10.4 %all-to-all-start.2 = ((f32[16,8,128]{2,1,0:T(8,128)}), f32[16,8,128]{2,1,0:T(8,128)S(1)}, u32[]{:S(2)}, u32[]{:S(2)}) async-start(f32[16,8,128]{2,1,0:T(8,128)} %get-tuple-element.38), calls=%async_computation.2 | async-start | bytes 131072 | tf_op jit(solution)/shard_map/all_to_all | solution.py:677

commit v2 on v1

--- a/solution.py
+++ b/solution.py
@@ -25,7 +25,9 @@
 BF16 = jnp.bfloat16
 HIGHEST = lax.Precision.HIGHEST
 
-LINE, SPOT, BAND, TOTAL, APPROX, ROW, COL, VALID, FIRST, RANK = range(10)
+LINE, SPOT, BAND, TOTAL, ROW, COL, VALID, FIRST, RANK = range(9)
+LINE_ROW, SPOT_ROW, TOTAL_ROW, APPROX_ROW = range(SLOTS, SLOTS + 4)
+TABLE_ROWS = SLOTS + ROWS
 
 
 def momentum_weights(total_steps):
@@ -73,6 +75,13 @@
 def split(values):
     high = values.astype(BF16)
     return high, (values - high.astype(F32)).astype(BF16)
+
+
+def split_rows(values):
+    high = values.astype(BF16)
+    rest = values - high.astype(F32)
+    middle = rest.astype(BF16)
+    return jnp.concatenate([high, middle, (rest - middle.astype(F32)).astype(BF16)], axis=0)
 
 
 def haar_signs():
@@ -186,15 +195,34 @@
     return total + pltpu.roll(total, SOUNDS, 1)
 
 
-def start_kernel(band_ref, obs_ref, out_ref):
-    band = to_col(band_ref[...].astype(F32))
-    hot = one_hot_bands(band)
+def start_kernel(*refs):
+    fetched = (len(refs) - 2) // 2
+    sources, targets = refs[:fetched], refs[fetched : 2 * fetched]
+    out_ref, sems = refs[2 * fetched :]
+    copies = [
+        pltpu.make_async_copy(source, target, sems.at[i])
+        for i, (source, target) in enumerate(zip(sources, targets))
+    ]
+    for copy in copies:
+        copy.start()
+    copies[0].wait()
+    copies[1].wait()
+    band_ref, obs_ref = targets[:2]
+    hot = one_hot_bands(to_col(band_ref[...].astype(F32)))
     sums = jnp.sum(obs_ref[...], axis=1, keepdims=True)
     counted = jnp.sum(hot, axis=0, keepdims=True)
     summed = jnp.sum(hot * sums, axis=0, keepdims=True)
     for t in range(out_ref.shape[0]):
         out_ref[t, 0:1, :] = counted
         out_ref[t, 1:2, :] = summed
+    for copy in copies[2:]:
+        copy.wait()
+
+
+def along_lanes(col):
+    n = col.shape[0]
+    here = iota((n, LANES), 0) == iota((n, LANES), 1)
+    return jnp.sum(jnp.where(here, col, 0.0), axis=0, keepdims=True)
 
 
 def prepare_kernel(
@@ -210,13 +238,16 @@
     high_ref,
     low_ref,
     column_ref,
-    obs_grad_ref,
+    twin_ref,
+    start_grad_ref,
     obs_slot_ref,
     row_match_ref,
-    info_ref,
+    table_ref,
     limit_ref,
     send_ref,
     strip_match_ref,
+    top_matrix_ref,
+    message_ref,
 ):
     sectors = strips // SEC_STRIPS
     strips_owner = NLAT * SEC_STRIPS // owners
@@ -224,21 +255,21 @@
     signs = haar_signs()
     scales = haar_scales()
     chunk = STRIP
+    per = chunk // SOUNDS
+    columns = []
     for start in range(0, SLOTS * SOUNDS, chunk):
         high, low = split(jac_ref[start : start + chunk, :])
         changed = (dot(high, signs) + dot(low, signs)) * scales
         high, low = split(changed)
         high_ref[start : start + chunk, :] = high
         low_ref[start : start + chunk, :] = low
-        per = chunk // SOUNDS
-        column_ref[start // SOUNDS : start // SOUNDS + per, :] = jnp.sum(
-            changed.reshape(per, SOUNDS, STRIP), axis=1
-        )
+        columns.append(jnp.sum(changed.reshape(per, SOUNDS, STRIP), axis=1))
+    column = jnp.concatenate(columns, axis=0)
 
     row_of = to_col(row_ref[...].astype(F32))
     col_row = col_ref[...].astype(F32)
     col_of = to_col(col_row)
-    valid_row = jnp.where(iota((1, SLOTS), 1) < count_ref[...], 1.0, 0.0)
+    valid_row = jnp.where(iota((1, SLOTS), 1) < count_ref[0], 1.0, 0.0)
     valid = to_col(valid_row)
     line = jnp.floor(col_of / SEC_STRIPS)
     spot = sector * SEC_STRIPS + (col_of - line * SEC_STRIPS)
@@ -250,20 +281,22 @@
     obs_slot = exact_dot(row_hot, jnp.concatenate([observed, observed], axis=1))
     obs_slot_ref[...] = obs_slot
     obs_grad = back_project(obs_slot, high_ref, low_ref)
-    obs_grad_ref[...] = obs_grad
-    column = column_ref[...]
+    column = column * valid
+    column_ref[...] = column
 
     lane = iota((SLOTS, SLOTS * SOUNDS), 1) // SOUNDS
     slot = iota((SLOTS, SLOTS * SOUNDS), 0)
-    row_lane = jnp.sum(jnp.where(lane == slot, row_of, 0.0), axis=0, keepdims=True)
-    row_lane = jnp.where(
-        jnp.sum(jnp.where(lane == slot, valid, 0.0), axis=0, keepdims=True) > 0.0, row_lane, -1.0
+    row_lane = jnp.sum(
+        jnp.where(lane == slot, (row_of + 1.0) * valid - 1.0, 0.0), axis=0, keepdims=True
     )
     row_match_ref[...] = jnp.where(row_of == row_lane, 1.0, 0.0)
 
     same = jnp.where(col_of == col_row, 1.0, 0.0)
     before = jnp.where(iota((SLOTS, SLOTS), 1) < iota((SLOTS, SLOTS), 0), 1.0, 0.0)
+    other = jnp.where(iota((SLOTS, SLOTS), 1) != iota((SLOTS, SLOTS), 0), same, 0.0)
     strip_match_ref[...] = same * valid_row
+    start_grad_ref[...] = -exact_dot(same * valid_row, obs_grad)
+    twin_ref[...] = exact_dot(other, column)
     first = jnp.where(jnp.sum(same * before, axis=1, keepdims=True) > 0.0, 0.0, 1.0)
     owner = jnp.floor(col_of / strips_owner)
     owner_row = jnp.floor(col_row / strips_owner)
@@ -275,8 +308,7 @@
         (LINE, line),
         (SPOT, spot),
         (BAND, band),
-        (TOTAL, column[:, 0:1] * valid),
-        (APPROX, -obs_grad[:, 0:1] * valid),
+        (TOTAL, column[:, 0:1]),
         (ROW, row_of),
         (COL, col_of),
         (VALID, valid),
@@ -284,7 +316,16 @@
         (RANK, rank),
     ):
         info = jnp.where(at == place, values, info)
-    info_ref[...] = info
+    table_ref[0:SLOTS, :] = info
+    table_ref[SLOTS:TABLE_ROWS, :] = jnp.zeros((TABLE_ROWS - SLOTS, LANES), F32)
+    table_ref[LINE_ROW : LINE_ROW + 1, :] = along_lanes(line + 1.0)
+    table_ref[SPOT_ROW : SPOT_ROW + 1, :] = along_lanes(spot + 1.0)
+    table_ref[TOTAL_ROW : TOTAL_ROW + 1, :] = along_lanes(column[:, 0:1])
+    table_ref[APPROX_ROW : APPROX_ROW + 1, :] = along_lanes(-obs_grad[:, 0:1] * valid)
+    matrix = jnp.zeros((SLOTS, LANES), F32)
+    for t in range(strips):
+        matrix = jnp.where(at == t, top_entry(spot, t, strips), matrix)
+    top_matrix_ref[...] = matrix
 
     local = iota((1, LANES), 1)
     limits_low = jnp.zeros((SLOTS, LANES), F32)
@@ -305,127 +346,167 @@
     limit_ref[:, :LANES] = STEP * limits_low
     limit_ref[:, LANES:] = STEP * limits_high
 
-    shape = (owners * ROWS, 4 * SLOTS)
+    shape = (owners * ROWS, 3 * 4 * SLOTS)
     target = (iota(shape, 0) // ROWS).astype(F32)
     kind = iota(shape, 0) % ROWS
-    group = iota(shape, 1) // SLOTS
-    slim = iota((SLOTS, 4 * SLOTS), 1) % SLOTS == iota((SLOTS, 4 * SLOTS), 0)
+    place = iota(shape, 1) % (4 * SLOTS)
+    group = place // SLOTS
+    slim_shape = (SLOTS, shape[1])
+    slim = iota(slim_shape, 1) % SLOTS == iota(slim_shape, 0)
     owner_wide = jnp.sum(jnp.where(slim, owner, 0.0), axis=0, keepdims=True)
     rank_wide = jnp.sum(jnp.where(slim, rank, 0.0), axis=0, keepdims=True)
     kind_f = kind.astype(F32)
-    mine = owner_wide == target
     hit = (group == 0) & (kind_f == 2.0 * rank_wide)
     hit = hit | ((group == 1) & (kind_f == 2.0 * rank_wide + 1.0))
     hit = hit | ((group == 2) & (kind == 5))
-    hit = (hit & mine) | ((iota(shape, 1) == 3 * SLOTS) & (kind == 4))
-    send_ref[...] = jnp.where(hit, 1.0, 0.0)
-
-
-def fill_message(out_ref, send, strips_part, meta, partial):
-    bottom = jnp.where(iota((SLOTS, LANES), 0) == 0, partial, 0.0)
+    hit = (hit & (owner_wide == target)) | ((place == 3 * SLOTS) & (kind == 4))
+    send = jnp.where(hit, 1.0, 0.0).astype(BF16)
+    send_ref[...] = send
+
+    at_f = at.astype(F32)
+    base = rank * (LANES // 2)
+    meta = jnp.where(at_f == base, col_of - owner * strips_owner + 1.0, 0.0)
+    meta = jnp.where(at_f == base + 1.0, band + 1.0, meta)
+    message_ref[...] = message_rows(send, column, meta, None).reshape(message_ref.shape)
+
+
+def message_rows(send, strips_part, meta, partial):
+    if partial is None:
+        bottom = jnp.zeros((SLOTS, LANES), F32)
+    else:
+        bottom = jnp.where(iota((SLOTS, LANES), 0) == 0, partial, 0.0)
     stacked = jnp.concatenate([strips_part[:, :LANES], strips_part[:, LANES:], meta, bottom], axis=0)
-    rows = exact_dot(send, stacked)
-    out_ref[...] = rows.reshape(out_ref.shape)
-
-
-def advance(strips, scalar, local_grad, column, info, info_all, approx_all, strip_match, limit, top_limit, point, top):
-    c_all = jnp.sum(one_hot_bands(info_all[:, BAND : BAND + 1]) * scalar, axis=1, keepdims=True)
-    grads = exact_dot(strip_match, local_grad + c_all[:SLOTS] * column)
-    approx_row = to_row(approx_all + c_all * info_all[:, TOTAL : TOTAL + 1])
-    line_row = to_row(info_all[:, LINE : LINE + 1])
-    spot_row = to_row(info_all[:, SPOT : SPOT + 1])
-    on_line = jnp.where(info[:, LINE : LINE + 1] == line_row, approx_row, 0.0)
+    return dot(send, split_rows(stacked))
+
+
+def side_by_side(rows):
+    out = rows[0]
+    for i, row in enumerate(rows[1:], 1):
+        wide = jnp.broadcast_to(row, (ROWS, LANES))
+        out = out + pltpu.roll(wide, i * SLOTS, 1)[0:1]
+    return out
+
+
+def slot_scalars(hot, scalar):
+    col = jnp.sum(hot * scalar, axis=1, keepdims=True)
+    return col, along_lanes(col)
+
+
+def advance(strips, col, row, grads, column, twin, same, approx_row, total_row, line_tops):
+    other = jnp.sum(jnp.where(same > 0.0, row[:, :SLOTS], 0.0), axis=1, keepdims=True)
+    full = grads + col[:SLOTS] * column + other * twin
+    sources = approx_row + row * total_row
     at = iota((SLOTS, LANES), 1)
     top_grad = jnp.zeros((SLOTS, LANES), F32)
     for t in range(strips):
-        value = jnp.sum(on_line * top_entry(spot_row, t, strips), axis=1, keepdims=True)
+        value = jnp.sum(line_tops[t * SLOTS : (t + 1) * SLOTS] * sources, axis=1, keepdims=True)
         top_grad = jnp.where(at == t, value, top_grad)
-    if point is None:
-        return shrink(-STEP * grads, limit), shrink(-STEP * top_grad, top_limit)
-    return shrink(point - STEP * grads, limit), shrink(top - STEP * top_grad, top_limit)
-
-
-def with_approx(point, top, info, strips):
-    at = iota((SLOTS, LANES), 1)
-    matrix = jnp.zeros((SLOTS, LANES), F32)
-    for t in range(strips):
-        matrix = jnp.where(at == t, top_entry(info[:, SPOT : SPOT + 1], t, strips), matrix)
+    return full, top_grad
+
+
+def with_approx(point, top, matrix):
     approx = jnp.sum(matrix * top, axis=1, keepdims=True)
     return jnp.where(iota((SLOTS, STRIP), 1) == 0, approx, point)
 
 
-def band_partial(point, column, info):
+def band_partial(point, column, hot):
     dots = jnp.sum(point * column, axis=1, keepdims=True)
-    hot = one_hot_bands(info[:, BAND : BAND + 1])
     return jnp.sum(hot * dots, axis=0, keepdims=True) / SOUNDS
 
 
-def gather_info(info_ref, others_refs):
-    return jnp.concatenate([info_ref[...]] + [r[...] for r in others_refs], axis=0)
+def twins(strip_match):
+    return jnp.where(iota((SLOTS, SLOTS), 0) == iota((SLOTS, SLOTS), 1), 0.0, strip_match)
 
 
 def first_step_kernel(
     strips,
     owners,
     first_ref,
-    info_ref,
     column_ref,
-    obs_grad_ref,
+    twin_ref,
+    grad_ref,
     limit_ref,
     strip_match_ref,
-    send_ref,
+    top_matrix_ref,
     decay_ref,
     weight_ref,
+    prepared_ref,
     *rest,
 ):
     sectors = strips // SEC_STRIPS
-    others_refs = rest[: sectors - 1]
-    point_ref, top_ref, message_ref = rest[sectors - 1 :]
+    tables = rest[:sectors]
+    point_ref, top_ref, message_ref, hot_ref, line_tops_ref = rest[sectors:]
     window = lax.axis_index("tile") // sectors
-    decay = decay_ref[...]
     sums = weekly([first_ref[t, 1:2, :] for t in range(owners)], sectors)
-    returned = scan_back([-s for s in sums], decay)
+    returned = scan_back([-s for s in sums], decay_ref[...])
     scalar = pick(returned, window) / SOUNDS
-    info = info_ref[...]
-    info_all = gather_info(info_ref, others_refs)
+    hot = jnp.concatenate([one_hot_bands(t[0:SLOTS, BAND : BAND + 1]) for t in tables], axis=0)
+    hot_ref[...] = hot
+
+    def row(index):
+        return side_by_side([t[index : index + 1, :] for t in tables])
+
+    spot_row = row(SPOT_ROW) - 1.0
+    on_line = tables[0][0:SLOTS, LINE : LINE + 1] + 1.0 == row(LINE_ROW)
+    line_tops = jnp.concatenate(
+        [jnp.where(on_line, top_entry(spot_row, t, strips), 0.0) for t in range(strips)], axis=0
+    )
+    line_tops_ref[...] = line_tops
     column = column_ref[...]
-    top_limit = STEP * weight_ref[0:1, :LANES]
-    updated, top = advance(
+    col, along = slot_scalars(hot, scalar)
+    grads, top_grad = advance(
         strips,
-        scalar,
-        -obs_grad_ref[...],
+        col,
+        along,
+        grad_ref[...],
         column,
-        info,
-        info_all,
-        info_all[:, APPROX : APPROX + 1],
-        strip_match_ref[...],
-        limit_ref[...],
-        top_limit,
-        None,
-        None,
-    )
-    point = with_approx(updated, top, info, strips)
+        twin_ref[...],
+        twins(strip_match_ref[...]),
+        row(APPROX_ROW),
+        row(TOTAL_ROW),
+        line_tops,
+    )
+    updated = shrink(-STEP * grads, limit_ref[...])
+    top = shrink(-STEP * top_grad, STEP * weight_ref[0:1, :LANES])
+    point = with_approx(updated, top, top_matrix_ref[...])
     point_ref[...] = point
     top_ref[...] = top
-    partial = band_partial(point, column, info)
-    at = iota((SLOTS, LANES), 1).astype(F32)
-    strips_owner = NLAT * SEC_STRIPS // owners
-    col = info[:, COL : COL + 1]
-    local = col - jnp.floor(col / strips_owner) * strips_owner
-    base = info[:, RANK : RANK + 1] * (LANES // 2)
-    meta = jnp.where(at == base, local + 1.0, 0.0)
-    meta = jnp.where(at == base + 1.0, info[:, BAND : BAND + 1] + 1.0, meta)
-    fill_message(message_ref, send_ref[...], column * info[:, VALID : VALID + 1], meta, partial)
-
-
-def local_grad_kernel(point_ref, high_ref, low_ref, row_match_ref, obs_slot_ref, info_ref, grad_ref, approx_ref):
+    partial = band_partial(point, column, hot[:SLOTS])
+    is_partial = iota(message_ref.shape, 1) == 4
+    message_ref[...] = jnp.where(is_partial, partial.reshape(1, 1, LANES), prepared_ref[...])
+
+
+def local_grad_kernel(
+    strips,
+    point_ref,
+    high_ref,
+    low_ref,
+    row_match_ref,
+    obs_slot_ref,
+    strip_match_ref,
+    *rest,
+):
+    sectors = strips // SEC_STRIPS
+    tables = rest[:sectors]
+    grad_ref, approx_ref, lead_ref = rest[sectors:]
     values = forward(point_ref[...], high_ref, low_ref)
     chosen = fold(row_match_ref[...], values) - obs_slot_ref[...]
     grad = back_project(chosen, high_ref, low_ref)
-    grad_ref[...] = grad
-    approx_ref[...] = jnp.broadcast_to(
-        grad[:, 0:1] * info_ref[:, VALID : VALID + 1], approx_ref.shape
-    )
+    grad_ref[...] = exact_dot(strip_match_ref[...], grad)
+    info = tables[0][0:SLOTS, :]
+    approx = grad[:, 0:1] * info[:, VALID : VALID + 1]
+    approx_ref[...] = jnp.broadcast_to(along_lanes(approx), approx_ref.shape)
+
+    sector = lax.rem(lax.axis_index("tile"), sectors).astype(F32)
+    line_row = side_by_side([t[LINE_ROW : LINE_ROW + 1, :] for t in tables])
+    spot_row = side_by_side([t[SPOT_ROW : SPOT_ROW + 1, :] for t in tables])
+    sector_row = jnp.floor((spot_row - 1.0) / SEC_STRIPS)
+    lane = iota((SLOTS, LANES), 1)
+    before = jnp.where(lane < iota((SLOTS, LANES), 0), 1.0, 0.0)
+    earlier = jnp.where(lane < SLOTS, before, jnp.where(sector_row < sector, 1.0, 0.0))
+    on_line = info[:, LINE : LINE + 1] + 1.0 == line_row
+    taken = jnp.sum(jnp.where(on_line, earlier, 0.0), axis=1, keepdims=True)
+    lead_ref[...] = jnp.broadcast_to(jnp.where(taken > 0.0, 0.0, 1.0), lead_ref.shape)
 
 
 def second_step_kernel(
@@ -434,87 +515,86 @@
     beta,
     first_ref,
     second_ref,
-    info_ref,
     column_ref,
+    twin_ref,
     grad_ref,
     limit_ref,
     strip_match_ref,
-    send_ref,
+    top_matrix_ref,
     decay_ref,
     weight_ref,
+    hot_ref,
+    line_tops_ref,
+    lead_ref,
+    send_ref,
     point_ref,
     top_ref,
     high_ref,
     low_ref,
     row_match_ref,
     obs_slot_ref,
-    obs_ref,
-    approx_ref,
     *rest,
 ):
     sectors = strips // SEC_STRIPS
-    others_refs = rest[: sectors - 1]
-    approx_refs = rest[sectors - 1 : 2 * (sectors - 1)]
-    message_ref, differ_ref = rest[2 * (sectors - 1) :]
-    my_index = lax.axis_index("tile")
-    window = my_index // sectors
-    sector = lax.rem(my_index, sectors).astype(F32)
-    decay = decay_ref[...]
-    combined, _ = background(first_ref, [second_ref[t, 4:5, :] for t in range(owners)], decay, sectors)
-    info = info_ref[...]
-    info_all = gather_info(info_ref, others_refs)
-    approx_all = gather_info(approx_ref, approx_refs)[:, 0:1]
+    tables, rest = rest[:sectors], rest[sectors:]
+    approx_refs, rest = rest[:sectors], rest[sectors:]
+    message_ref, values_ref = rest
+    window = lax.axis_index("tile") // sectors
+    combined, _ = background(
+        first_ref, [second_ref[t, 4:5, :] for t in range(owners)], decay_ref[...], sectors
+    )
+    hot = hot_ref[...]
     column = column_ref[...]
-    top_limit = STEP * weight_ref[0:1, :LANES]
+    col, along = slot_scalars(hot, pick(combined, window))
+    grads, top_grad = advance(
+        strips,
+        col,
+        along,
+        grad_ref[...],
+        column,
+        twin_ref[...],
+        twins(strip_match_ref[...]),
+        side_by_side([r[0:1, :] for r in approx_refs]),
+        side_by_side([t[TOTAL_ROW : TOTAL_ROW + 1, :] for t in tables]),
+        line_tops_ref[...],
+    )
     old = point_ref[...]
     old_top = top_ref[...]
-    updated, top = advance(
-        strips,
-        pick(combined, window),
-        grad_ref[...],
-        column,
-        info,
-        info_all,
-        approx_all,
-        strip_match_ref[...],
-        limit_ref[...],
-        top_limit,
-        old,
-        old_top,
-    )
+    updated = shrink(old - STEP * grads, limit_ref[...])
+    top = shrink(old_top - STEP * top_grad, STEP * weight_ref[0:1, :LANES])
     point = updated + beta * (updated - old)
     top = top + beta * (top - old_top)
-    point = with_approx(point, top, info, strips)
-    partial = band_partial(point, column, info)
+    point = with_approx(point, top, top_matrix_ref[...])
     values = forward(point, high_ref, low_ref)
+    values_ref[...] = values
     chosen = fold(row_match_ref[...], values) - obs_slot_ref[...]
     grad = back_project(chosen, high_ref, low_ref)
 
+    partial = band_partial(point, column, hot[:SLOTS])
+    info = tables[0][0:SLOTS, :]
     valid = info[:, VALID : VALID + 1]
-    lane = iota((SLOTS, SLOTS * SOUNDS), 1) // SOUNDS
-    slot = iota((SLOTS, SLOTS * SOUNDS), 0)
-    row_lane = jnp.sum(
-        jnp.where(lane == slot, (info[:, ROW : ROW + 1] + 1.0) * valid, 0.0), axis=0, keepdims=True
-    )
-    per_row = jnp.where(
-        iota((SB_DEV, SLOTS * SOUNDS), 0).astype(F32) + 1.0 == row_lane, 1.0, 0.0
-    )
-    differ_ref[...] = fold(per_row, values)[:, :SOUNDS] - obs_ref[...]
-
-    count = info_all.shape[0]
-    line_row = to_row(info_all[:, LINE : LINE + 1])
-    sector_row = to_row(jnp.floor(info_all[:, SPOT : SPOT + 1] / SEC_STRIPS))
-    lane = iota((SLOTS, count), 1)
-    earlier = jnp.where(lane < SLOTS, jnp.where(lane < iota((SLOTS, count), 0), 1.0, 0.0), jnp.where(sector_row < sector, 1.0, 0.0))
-    taken = jnp.sum(jnp.where(info[:, LINE : LINE + 1] == line_row, earlier, 0.0), axis=1, keepdims=True)
-    top = jnp.where(taken > 0.0, 0.0, top)
+    top = top * lead_ref[:, 0:1]
     rank = info[:, RANK : RANK + 1]
     meta = jnp.where(rank == 0.0, pltpu.roll(top, ROWS, 1), pltpu.roll(top, LANES // 2 + ROWS, 1))
     kept = jnp.where(iota((SLOTS, STRIP), 1) == 0, 0.0, point * info[:, FIRST : FIRST + 1])
-    fill_message(message_ref, send_ref[...], kept - STEP * (valid * grad), meta, partial)
-
-
-def place_kernel(strips, owners, second_ref, place_ref, band_hot_ref):
+    rows = message_rows(send_ref[...], kept - STEP * (valid * grad), meta, partial)
+    message_ref[...] = rows.reshape(message_ref.shape)
+
+
+def place_kernel(
+    strips,
+    owners,
+    second_ref,
+    table_ref,
+    values_ref,
+    obs_ref,
+    band_ref,
+    place_ref,
+    band_hot_ref,
+    scaled_ref,
+    differ_ref,
+    block_hot_ref,
+):
     sectors = strips // SEC_STRIPS
     lines = NLAT // owners
     count = owners * ROWS
@@ -534,6 +614,7 @@
         band_tall = jnp.sum(jnp.where(tall_pair, to_row(band), 0.0), axis=1, keepdims=True)
         band_col = jnp.where(tall_kind // 2 == q, band_tall, band_col)
     band_hot_ref[...] = one_hot_bands(band_col - 1.0)
+    scaled_ref[...] = jnp.where(tall_kind < 4, STEP * second_ref[...].reshape(count, LANES), 0.0)
 
     def line_of(strip):
         return jnp.floor(strip / SEC_STRIPS)
@@ -549,29 +630,42 @@
     slot_spot = sector * SEC_STRIPS + strip_row - slot_line * SEC_STRIPS
     base = (window == window_col) & (slot_line == line_col) & (strip_row >= 0.0)
     base = jnp.where(base & (kind < 4), 1.0, 0.0)
+    parts = []
     for half in range(2):
         part = jnp.where(kind % 2 == half, base, 0.0)
         for j in range(strips):
-            start = (half * strips + j) * blocks
-            place_ref[start : start + blocks, :] = jnp.where(slot_spot == float(j), part, 0.0)
+            parts.append(jnp.where(slot_spot == float(j), part, 0.0))
     for q in range(2):
-        start = (2 * strips + q) * blocks
         hit = (window == window_col) & (line_of(strip_rows[q]) == line_col) & (strip_rows[q] >= 0.0) & (kind == 5)
-        place_ref[start : start + blocks, :] = jnp.where(hit, 1.0, 0.0)
+        parts.append(jnp.where(hit, 1.0, 0.0))
+    place = jnp.concatenate(parts, axis=0).astype(BF16)
+    place_ref[...] = jnp.concatenate([place, place, place], axis=1)
+
+    info = table_ref[0:SLOTS, :]
+    lane = iota((SLOTS, SLOTS * SOUNDS), 1) // SOUNDS
+    slot = iota((SLOTS, SLOTS * SOUNDS), 0)
+    row_lane = jnp.sum(
+        jnp.where(lane == slot, (info[:, ROW : ROW + 1] + 1.0) * info[:, VALID : VALID + 1], 0.0),
+        axis=0,
+        keepdims=True,
+    )
+    per_row = jnp.where(iota((SB_DEV, SLOTS * SOUNDS), 0).astype(F32) + 1.0 == row_lane, 1.0, 0.0)
+    differ_ref[...] = fold(per_row, values_ref[...])[:, :SOUNDS] - obs_ref[...]
+    block_hot_ref[...] = one_hot_bands(to_col(band_ref[...].astype(F32)))
 
 
 def finish_kernel(
     strips,
     owners,
     first_ref,
-    second_ref,
     third_ref,
     place_ref,
     band_hot_ref,
+    scaled_ref,
     decay_ref,
     weight_ref,
     differ_ref,
-    band_ref,
+    block_hot_ref,
     out_ref,
     misfit_ref,
 ):
@@ -582,19 +676,14 @@
     combined, carried = background(
         first_ref, [third_ref[t, 4:5, :] for t in range(owners)], decay_ref[...], sectors
     )
-    hot = one_hot_bands(to_col(band_ref[...].astype(F32)))
-    offset = jnp.sum(hot * pick(carried, window), axis=1, keepdims=True)
-    misfit_ref[...] = differ_ref[...] + offset
-
     spread = jnp.concatenate(
         [jnp.broadcast_to(row, (sectors * ROWS, NBANDS)) for row in combined], axis=0
     )
     scalars = jnp.sum(band_hot_ref[...] * spread, axis=1, keepdims=True)
-    third = third_ref[...].reshape(count, LANES)
-    second = second_ref[...].reshape(count, LANES)
-    kind = iota((count, 1), 0) % ROWS
-    rows = third - (STEP * scalars) * jnp.where(kind < 4, second, 0.0)
-    placed = exact_dot(place_ref[...], rows)
+    rows = third_ref[...].reshape(count, LANES) - scalars * scaled_ref[...]
+    placed = dot(place_ref[...], split_rows(rows))
+    offset = jnp.sum(block_hot_ref[...] * pick(carried, window), axis=1, keepdims=True)
+    misfit_ref[...] = differ_ref[...] + offset
 
     lane = iota((1, LANES), 1)
     for j in range(strips):
@@ -639,11 +728,12 @@
     return math.sqrt(m / strips) * (1.0 if within < span // 2 else -1.0)
 
 
-def call(kernel, outs, *operands):
+def call(kernel, outs, *operands, **kwargs):
     return pl.pallas_call(
         kernel,
         out_shape=[jax.ShapeDtypeStruct(shape, dtype) for shape, dtype in outs],
-        compiler_params=pltpu.CompilerParams(vmem_limit_bytes=48 * 1024 * 1024),
+        compiler_params=pltpu.CompilerParams(vmem_limit_bytes=40 * 1024 * 1024),
+        **kwargs,
     )(*operands)
 
 
@@ -662,22 +752,25 @@
     strips = sectors * SEC_STRIPS
     lines = NLAT // owners
     betas = momentum_weights(ITERS)
-    rows = block_row.reshape(1, SLOTS)
-    cols = block_col.reshape(1, SLOTS)
-    count = block_count.reshape(1, 1)
-    bands = block_band.reshape(1, SB_DEV)
-    decay = carry_decay.reshape(1, NBANDS)
-    weight = sparsity_weight.reshape(1, -1)
-    flat = jacobian.reshape(SLOTS * SOUNDS, STRIP)
+    arguments = [
+        block_band.reshape(1, SB_DEV),
+        observations,
+        jacobian.reshape(SLOTS * SOUNDS, STRIP),
+        block_row.reshape(1, SLOTS),
+        block_col.reshape(1, SLOTS),
+        carry_decay.reshape(1, NBANDS),
+        sparsity_weight.reshape(1, -1),
+    ]
     message = ((owners, ROWS, LANES), F32)
-    table = ((SLOTS, LANES), F32)
+    narrow = ((SLOTS, LANES), F32)
     strip_rows = ((SLOTS, STRIP), F32)
+    table_rows = ((TABLE_ROWS, LANES), F32)
 
     def trade(values):
         return lax.all_to_all(values, "tile", 0, 0, tiled=True)
 
-    def from_sectors(values):
-        found = []
+    def with_sectors(values):
+        found = [values]
         for shift in range(1, sectors):
             pairs = [
                 (d, d // sectors * sectors + (d + shift) % sectors) for d in range(owners)
@@ -685,95 +778,147 @@
             found.append(lax.ppermute(values, "tile", pairs))
         return found
 
-    (first,) = call(start_kernel, [((owners, 2, LANES), F32)], bands, observations)
+    arguments = [pltpu.with_memory_space_constraint(a, pltpu.HBM) for a in arguments]
+    bands, observed, flat, rows, cols, decay, weight, first = call(
+        start_kernel,
+        [(a.shape, a.dtype) for a in arguments] + [((owners, 2, LANES), F32)],
+        *arguments,
+        in_specs=[pl.BlockSpec(memory_space=pltpu.HBM)] * len(arguments),
+        out_specs=[pl.BlockSpec(memory_space=pltpu.VMEM)] * (len(arguments) + 1),
+        scratch_shapes=[pltpu.SemaphoreType.DMA((len(arguments),))],
+    )
     first = trade(first)
-    high, low, column, obs_grad, obs_slot, row_match, info, limit, send, strip_match = call(
+    (
+        high,
+        low,
+        column,
+        twin,
+        start_grad,
+        obs_slot,
+        row_match,
+        table,
+        limit,
+        send,
+        strip_match,
+        top_matrix,
+        prepared,
+    ) = call(
         functools.partial(prepare_kernel, strips, owners),
         [
             ((SLOTS * SOUNDS, STRIP), BF16),
             ((SLOTS * SOUNDS, STRIP), BF16),
             strip_rows,
             strip_rows,
-            table,
+            strip_rows,
+            narrow,
             ((SLOTS, SLOTS * SOUNDS), F32),
-            table,
+            table_rows,
             strip_rows,
-            ((owners * ROWS, 4 * SLOTS), F32),
+            ((owners * ROWS, 3 * 4 * SLOTS), BF16),
             ((SLOTS, SLOTS), F32),
+            narrow,
+            message,
         ],
         flat,
-        observations,
+        observed,
         rows,
         cols,
-        count,
+        block_count,
         bands,
         weight,
-    )
-    others = from_sectors(info)
-    point, top, second = call(
+        in_specs=[
+            pl.BlockSpec(memory_space=pltpu.SMEM if i == 4 else pltpu.VMEM) for i in range(7)
+        ],
+    )
+    tables = with_sectors(table)
+    point, top, second, hot, line_tops = call(
         functools.partial(first_step_kernel, strips, owners),
-        [strip_rows, table, message],
+        [
+            strip_rows,
+            narrow,
+            message,
+            ((sectors * SLOTS, NBANDS), F32),
+            ((strips * SLOTS, LANES), F32),
+        ],
         first,
-        info,
         column,
-        obs_grad,
+        twin,
+        start_grad,
         limit,
         strip_match,
-        send,
+        top_matrix,
         decay,
         weight,
-        *others,
+        prepared,
+        *tables,
     )
     second = trade(second)
-    grad, approx = call(
-        local_grad_kernel, [strip_rows, table], point, high, low, row_match, obs_slot, info
-    )
-    others_approx = from_sectors(approx)
-    third, differ = call(
+    grad, approx, lead = call(
+        functools.partial(local_grad_kernel, strips),
+        [strip_rows, ((ROWS, LANES), F32), narrow],
+        point,
+        high,
+        low,
+        row_match,
+        obs_slot,
+        strip_match,
+        *tables,
+    )
+    third, values = call(
         functools.partial(second_step_kernel, strips, owners, betas[1]),
-        [message, ((SB_DEV, SOUNDS), F32)],
+        [message, ((1, SLOTS * SOUNDS), F32)],
         first,
         second,
-        info,
         column,
+        twin,
         grad,
         limit,
         strip_match,
-        send,
+        top_matrix,
         decay,
         weight,
+        hot,
+        line_tops,
+        lead,
+        send,
         point,
         top,
         high,
         low,
         row_match,
         obs_slot,
-        observations,
-        approx,
-        *others,
-        *others_approx,
+        *tables,
+        *with_sectors(approx),
     )
     third = trade(third)
-    place, band_hot = call(
+    placed_rows = (2 * strips + 2) * lines * WIN
+    place, band_hot, scaled, differ, block_hot = call(
         functools.partial(place_kernel, strips, owners),
         [
-            (((2 * strips + 2) * lines * WIN, owners * ROWS), F32),
+            ((placed_rows, 3 * owners * ROWS), BF16),
             ((owners * ROWS, NBANDS), F32),
+            ((owners * ROWS, LANES), F32),
+            ((SB_DEV, SOUNDS), F32),
+            ((SB_DEV, NBANDS), F32),
         ],
         second,
+        table,
+        values,
+        observed,
+        bands,
     )
     coeffs, misfit = call(
         functools.partial(finish_kernel, strips, owners),
         [((lines * WIN, strips * STRIP), F32), ((SB_DEV, SOUNDS), F32)],
         first,
-        second,
         third,
         place,
         band_hot,
+        scaled,
         decay,
         weight,
         differ,
-        bands,
+        block_hot,
     )
     return (coeffs.reshape(lines, WIN, strips * STRIP), misfit)
 

time: 44.6 us -> 41.7 us (0.935)
  local copies, waits for them, and re-layouts: 3.91 us -> 0 us
  waiting for transfers between devices: 14.2 us -> 15.9 us
  starting transfers between devices: 16.5 us -> 15.2 us
  Pallas kernels: 8.17 us -> 8.98 us
    unnamed x16 -> x0, local copies, waits for them, and re-layouts: 3.91 us -> none
    all_to_all x3, waiting for transfers between devices: 12.5 us -> 14.2 us  [trade(): return lax.all_to_all(values, 'tile', 0, 0, tiled=True)]
    all_to_all x3, starting transfers between devices: 15.6 us -> 14.4 us  [trade(): return lax.all_to_all(values, 'tile', 0, 0, tiled=True)]
    pallas_call x7, Pallas kernels: 8.17 us -> 8.98 us  [call(): pl.pallas_call(kernel, out_shape=[jax.ShapeDtypeStruct(shape, dtype) for...]
  transfers between devices with their start and end apart: 5 -> 5, of which waited for: 5 -> 5; matrix products, arithmetic and copies ran while one was open for 0% -> 0% of each run, Pallas kernels for 6% -> 7%
where the time goes in v2:
time: 41.7 us; the launch traced here: 41.4 us
  waiting for transfers between devices  15.9 us (38%)
  starting transfers between devices  15.2 us (36%)
  Pallas kernels  8.98 us (22%)
  between operations  1.32 us (3%)
    all_to_all x3, starting transfers between devices, trade(): return lax.all_to_all(values, 'tile', 0, 0, tiled=True)  14.4 us
    all_to_all x3, waiting for transfers between devices, trade(): return lax.all_to_all(values, 'tile', 0, 0, tiled=True)  14.2 us
    pallas_call x7, Pallas kernels, call(): pl.pallas_call(kernel, out_shape=[jax.ShapeDtypeStruct(shape, dtype) for...  8.98 us
    ppermute x2, waiting for transfers between devices, with_sectors(): found.append(lax.ppermute(values, 'tile', pairs))  1.71 us
  transfers between devices with their start and end apart: 5, of which 5 were waited for; matrix products, arithmetic and copies ran while one was open for 0% of the time, Pallas kernels for 7%

profile of v2, /device:TPU:0, one launch (start us, length us, event | category | flops | bytes accessed | tf_op | source)
XLA Modules:
  0.0 41.4 jit_solution(5439592077563634730)
XLA Ops:
  0.6 1.9 %shard_map.95 = (s32[1,32]{1,0:T(1,128)S(1)}, f32[32,64]{1,0:T(8,128)S(1)}, f32[1024,256]{1,0:T(8,128)S(1)}, s32[1,16]{1,0:T(1,128)S(1)}, s32[1,16]{1,0:T(1,128)...) custom-call(s32[1,32]{1,0:T(1,128)} %bitcast.9, f32[32,64]{1,0:T(8,128)} %refs_1_.1, ...), custom_call_target="tpu_custom_call" | custom-call | tf_op jit(solution)/shard_map/pallas_call | solution.py:732
  2.6 7.4 %all-to-all-start = ((f32[16,2,128]{2,1,0:T(2,128)}), f32[16,2,128]{2,1,0:T(2,128)S(1)}, u32[]{:S(2)}, u32[]{:S(2)}) async-start(f32[16,2,128]{2,1,0:T(2,128)} %get-tuple-element.40), calls=%async_computation | async-start | bytes 32768 | tf_op jit(solution)/shard_map/all_to_all | solution.py:770
  10.6 1.5 %shard_map.96 = (bf16[1024,256]{1,0:T(8,128)(2,1)S(1)}, bf16[1024,256]{1,0:T(8,128)(2,1)S(1)}, f32[16,256]{1,0:T(8,128)S(1)}, f32[16,256]{1,0:T(8,128)S(1)}, f32...) custom-call(f32[1024,256]{1,0:T(8,128)S(1)} %get-tuple-element.41.ja, ...), custom_call_target="tpu_custom_call" | custom-call | tf_op jit(solution)/shard_map/pallas_call | solution.py:732
  12.1 0.4 %collective-permute-start = (f32[24,128]{1,0:T(8,128)S(1)}, f32[24,128]{1,0:T(8,128)S(1)}, u32[]{:S(2)}, u32[]{:S(2)}) collective-permute-start(f32[24,128]{1,0:T(8,128)S(1)} %get-tuple-element.55.rest_0_.table_ref), channel_id=1, source_target_pairs={{0,1},{1,0},{2,3},{3,2},{4,5},{5,4},{6,7},{7,6},{8,9},{9,8},{10,11... | collective-permute-start | bytes 36872 | tf_op jit(solution)/shard_map/ppermute | solution.py:778
  12.5 0.8 %collective-permute-done.rest_1_ = f32[24,128]{1,0:T(8,128)S(1)} collective-permute-done((f32[24,128]{1,0:T(8,128)S(1)}, f32[24,128]{1,0:T(8,128)S(1)}, u32[]{:S(2)}, u32[]{:S(2)}) %collective-permute-start) | collective-permute-done | bytes 12320 | tf_op jit(solution)/shard_map/ppermute | solution.py:778
  13.4 3.1 %all-to-all-done.first_ref = f32[16,2,128]{2,1,0:T(2,128)S(1)} async-done(((f32[16,2,128]{2,1,0:T(2,128)}), f32[16,2,128]{2,1,0:T(2,128)S(1)}, u32[]{:S(2)}, u32[]{:S(2)}) %all-to-all-start) | async-done | bytes 16416 | tf_op jit(solution)/shard_map/all_to_all | solution.py:770
  16.5 1.0 %shard_map.97 = (f32[16,256]{1,0:T(8,128)S(1)}, f32[16,128]{1,0:T(8,128)S(1)}, f32[16,8,128]{2,1,0:T(8,128)}, f32[32,128]{1,0:T(8,128)S(1)}, f32[64,128]{1,0:T(8,128)S(1)}) custom-call(f32[16,2,128]{2,1,0:T(2,128)S(1)} %all-to-all-done.first_ref, f32[16,256]{1,0:T(8,128)S(1)} %get-tuple-element.47.column_ref, f32[16,256]{1,0:T(8,128)S(1)} %get-tuple-element.48.twin_ref, ...), custom_call_target="tpu_custom_call" | custom-call | tf_op jit(solution)/shard_map/pallas_call | solution.py:732
  17.5 3.5 %all-to-all-start.1 = ((f32[16,8,128]{2,1,0:T(8,128)}), f32[16,8,128]{2,1,0:T(8,128)S(1)}, u32[]{:S(2)}, u32[]{:S(2)}) async-start(f32[16,8,128]{2,1,0:T(8,128)} %get-tuple-element.56), calls=%async_computation.1 | async-start | bytes 131072 | tf_op jit(solution)/shard_map/all_to_all | solution.py:770
  21.0 1.1 %shard_map.98 = (f32[16,256]{1,0:T(8,128)S(1)}, f32[8,128]{1,0:T(8,128)S(1)}, f32[16,128]{1,0:T(8,128)S(1)}) custom-call(f32[16,256]{1,0:T(8,128)S(1)} %get-tuple-element.57.point_ref, bf16[1024,256]{1,0:T(8,128)(2,1)S(1)} %get-tuple-element.58.high_ref, bf16[1024,256]{1,0:T(8,128)(2,1)S(1)} %get-tuple-element.59.low_ref, ...), custom_call_target="tpu_custom_call" | custom-call | tf_op jit(solution)/shard_map/pallas_call | solution.py:732
  22.1 0.3 collective-permute-start.1
  22.4 0.9 %collective-permute-done.1.rest_3_ = f32[8,128]{1,0:T(8,128)S(1)} collective-permute-done((f32[8,128]{1,0:T(8,128)S(1)}, f32[8,128]{1,0:T(8,128)S(1)}, u32[]{:S(2)}, u32[]{:S(2)}) %collective-permute-start.1) | collective-permute-done | bytes 4128 | tf_op jit(solution)/shard_map/ppermute | solution.py:778
  23.3 4.6 %all-to-all-done.1.second_ref = f32[16,8,128]{2,1,0:T(8,128)S(1)} async-done(((f32[16,8,128]{2,1,0:T(8,128)}), f32[16,8,128]{2,1,0:T(8,128)S(1)}, u32[]{:S(2)}, u32[]{:S(2)}) %all-to-all-start.1) | async-done | bytes 65568 | tf_op jit(solution)/shard_map/all_to_all | solution.py:770
  27.9 1.9 %shard_map.99 = (f32[16,8,128]{2,1,0:T(8,128)}, f32[1,1024]{1,0:T(1,128)S(1)}) custom-call(f32[16,2,128]{2,1,0:T(2,128)S(1)} %all-to-all-done.first_ref, f32[16,8,128]{2,1,0:T(8,128)S(1)} %all-to-all-done.1.second_ref, f32[16,256]{1,0:T(8,128)S(1)} %get-tuple-element.47.column_ref, f32[16,256]{1,0:T(8,128)S(1)} %get-tuple-element.48.twin_ref, ...), custom_call_target="tpu_custom_call" | custom-call | tf_op jit(solution)/shard_map/pallas_call | solution.py:732
  29.8 3.5 %all-to-all-start.2 = ((f32[16,8,128]{2,1,0:T(8,128)}), f32[16,8,128]{2,1,0:T(8,128)S(1)}, u32[]{:S(2)}, u32[]{:S(2)}) async-start(f32[16,8,128]{2,1,0:T(8,128)} %get-tuple-element.69), calls=%async_computation.2 | async-start | bytes 131072 | tf_op jit(solution)/shard_map/all_to_all | solution.py:770
  33.3 0.4 shard_map.100
  33.7 6.5 %all-to-all-done.2.third_ref = f32[16,8,128]{2,1,0:T(8,128)S(1)} async-done(((f32[16,8,128]{2,1,0:T(8,128)}), f32[16,8,128]{2,1,0:T(8,128)S(1)}, u32[]{:S(2)}, u32[]{:S(2)}) %all-to-all-start.2) | async-done | bytes 65568 | tf_op jit(solution)/shard_map/all_to_all | solution.py:770
  40.2 1.2 %shard_map.101 = (f32[32,1024]{1,0:T(8,128)}, f32[32,64]{1,0:T(8,128)}) custom-call(f32[16,2,128]{2,1,0:T(2,128)S(1)} %all-to-all-done.first_ref, f32[16,8,128]{2,1,0:T(8,128)S(1)} %all-to-all-done.2.third_ref, bf16[320,384]{1,0:T(8,128)(2,1)S(1)} %get-tuple-element.71.place_ref, f32[128,128]{1,0:T(8,128)S(1)} %get-tuple-element.72.band_hot_ref, ...), custom_call_target="tpu_custom_call" | custom-call | tf_op jit(solution)/shard_map/pallas_call | solution.py:732
Async XLA Ops:
  2.6 13.9 %all-to-all-start = ((f32[16,2,128]{2,1,0:T(2,128)}), f32[16,2,128]{2,1,0:T(2,128)S(1)}, u32[]{:S(2)}, u32[]{:S(2)}) async-start(f32[16,2,128]{2,1,0:T(2,128)} %get-tuple-element.40), calls=%async_computation | async-start | bytes 32768 | tf_op jit(solution)/shard_map/all_to_all | solution.py:770
  12.1 1.3 %collective-permute-start = (f32[24,128]{1,0:T(8,128)S(1)}, f32[24,128]{1,0:T(8,128)S(1)}, u32[]{:S(2)}, u32[]{:S(2)}) collective-permute-start(f32[24,128]{1,0:T(8,128)S(1)} %get-tuple-element.55.rest_0_.table_ref), channel_id=1, source_target_pairs={{0,1},{1,0},{2,3},{3,2},{4,5},{5,4},{6,7},{7,6},{8,9},{9,8},{10,11... | collective-permute-start | bytes 36872 | tf_op jit(solution)/shard_map/ppermute | solution.py:778
  17.5 10.4 %all-to-all-start.1 = ((f32[16,8,128]{2,1,0:T(8,128)}), f32[16,8,128]{2,1,0:T(8,128)S(1)}, u32[]{:S(2)}, u32[]{:S(2)}) async-start(f32[16,8,128]{2,1,0:T(8,128)} %get-tuple-element.56), calls=%async_computation.1 | async-start | bytes 131072 | tf_op jit(solution)/shard_map/all_to_all | solution.py:770
  22.1 1.2 %collective-permute-start.1 = (f32[8,128]{1,0:T(8,128)S(1)}, f32[8,128]{1,0:T(8,128)S(1)}, u32[]{:S(2)}, u32[]{:S(2)}) collective-permute-start(f32[8,128]{1,0:T(8,128)S(1)} %get-tuple-element.68.rest_2_), channel_id=1, source_target_pairs={{0,1},{1,0},{2,3},{3,2},{4,5},{5,4},{6,7},{7,6},{8,9},{9,8},{10,11... | collective-permute-start | bytes 12296 | tf_op jit(solution)/shard_map/ppermute | solution.py:778
  29.8 10.4 %all-to-all-start.2 = ((f32[16,8,128]{2,1,0:T(8,128)}), f32[16,8,128]{2,1,0:T(8,128)S(1)}, u32[]{:S(2)}, u32[]{:S(2)}) async-start(f32[16,8,128]{2,1,0:T(8,128)} %get-tuple-element.69), calls=%async_computation.2 | async-start | bytes 131072 | tf_op jit(solution)/shard_map/all_to_all | solution.py:770

commit v3 on v2

--- a/solution.py
+++ b/solution.py
@@ -20,12 +20,13 @@
 LANES = 128
 ROWS = 8
 STEP = 0.2
+PIECES = 8
 
 F32 = jnp.float32
 BF16 = jnp.bfloat16
 HIGHEST = lax.Precision.HIGHEST
 
-LINE, SPOT, BAND, TOTAL, ROW, COL, VALID, FIRST, RANK = range(9)
+LINE, SPOT, BAND, TOTAL, ROW, COL, VALID = range(7)
 LINE_ROW, SPOT_ROW, TOTAL_ROW, APPROX_ROW = range(SLOTS, SLOTS + 4)
 TABLE_ROWS = SLOTS + ROWS
 
@@ -199,9 +200,14 @@
     fetched = (len(refs) - 2) // 2
     sources, targets = refs[:fetched], refs[fetched : 2 * fetched]
     out_ref, sems = refs[2 * fetched :]
+    pairs = list(zip(sources, targets))
+    wide_source, wide_target = pairs.pop()
+    part = wide_source.shape[0] // PIECES
+    for start in range(0, wide_source.shape[0], part):
+        pairs.append((wide_source.at[start : start + part], wide_target.at[start : start + part]))
     copies = [
         pltpu.make_async_copy(source, target, sems.at[i])
-        for i, (source, target) in enumerate(zip(sources, targets))
+        for i, (source, target) in enumerate(pairs)
     ]
     for copy in copies:
         copy.start()
@@ -225,32 +231,22 @@
     return jnp.sum(jnp.where(here, col, 0.0), axis=0, keepdims=True)
 
 
-def prepare_kernel(
+def transform_kernel(
     strips,
-    owners,
     jac_ref,
     obs_ref,
     row_ref,
     col_ref,
     count_ref,
     band_ref,
-    weight_ref,
     high_ref,
     low_ref,
     column_ref,
-    twin_ref,
-    start_grad_ref,
+    obs_grad_ref,
     obs_slot_ref,
-    row_match_ref,
     table_ref,
-    limit_ref,
-    send_ref,
-    strip_match_ref,
-    top_matrix_ref,
-    message_ref,
 ):
     sectors = strips // SEC_STRIPS
-    strips_owner = NLAT * SEC_STRIPS // owners
     sector = lax.rem(lax.axis_index("tile"), sectors).astype(F32)
     signs = haar_signs()
     scales = haar_scales()
@@ -267,10 +263,8 @@
     column = jnp.concatenate(columns, axis=0)
 
     row_of = to_col(row_ref[...].astype(F32))
-    col_row = col_ref[...].astype(F32)
-    col_of = to_col(col_row)
-    valid_row = jnp.where(iota((1, SLOTS), 1) < count_ref[0], 1.0, 0.0)
-    valid = to_col(valid_row)
+    col_of = to_col(col_ref[...].astype(F32))
+    valid = jnp.where(iota((SLOTS, 1), 0) < count_ref[0], 1.0, 0.0)
     line = jnp.floor(col_of / SEC_STRIPS)
     spot = sector * SEC_STRIPS + (col_of - line * SEC_STRIPS)
     row_hot = jnp.where(row_of == iota((SLOTS, SB_DEV), 1).astype(F32), 1.0, 0.0)
@@ -281,26 +275,9 @@
     obs_slot = exact_dot(row_hot, jnp.concatenate([observed, observed], axis=1))
     obs_slot_ref[...] = obs_slot
     obs_grad = back_project(obs_slot, high_ref, low_ref)
+    obs_grad_ref[...] = obs_grad
     column = column * valid
     column_ref[...] = column
-
-    lane = iota((SLOTS, SLOTS * SOUNDS), 1) // SOUNDS
-    slot = iota((SLOTS, SLOTS * SOUNDS), 0)
-    row_lane = jnp.sum(
-        jnp.where(lane == slot, (row_of + 1.0) * valid - 1.0, 0.0), axis=0, keepdims=True
-    )
-    row_match_ref[...] = jnp.where(row_of == row_lane, 1.0, 0.0)
-
-    same = jnp.where(col_of == col_row, 1.0, 0.0)
-    before = jnp.where(iota((SLOTS, SLOTS), 1) < iota((SLOTS, SLOTS), 0), 1.0, 0.0)
-    other = jnp.where(iota((SLOTS, SLOTS), 1) != iota((SLOTS, SLOTS), 0), same, 0.0)
-    strip_match_ref[...] = same * valid_row
-    start_grad_ref[...] = -exact_dot(same * valid_row, obs_grad)
-    twin_ref[...] = exact_dot(other, column)
-    first = jnp.where(jnp.sum(same * before, axis=1, keepdims=True) > 0.0, 0.0, 1.0)
-    owner = jnp.floor(col_of / strips_owner)
-    owner_row = jnp.floor(col_row / strips_owner)
-    rank = jnp.sum(jnp.where(owner == owner_row, before, 0.0), axis=1, keepdims=True)
 
     at = iota((SLOTS, LANES), 1)
     info = jnp.zeros((SLOTS, LANES), F32)
@@ -312,8 +289,6 @@
         (ROW, row_of),
         (COL, col_of),
         (VALID, valid),
-        (FIRST, first),
-        (RANK, rank),
     ):
         info = jnp.where(at == place, values, info)
     table_ref[0:SLOTS, :] = info
@@ -322,6 +297,56 @@
     table_ref[SPOT_ROW : SPOT_ROW + 1, :] = along_lanes(spot + 1.0)
     table_ref[TOTAL_ROW : TOTAL_ROW + 1, :] = along_lanes(column[:, 0:1])
     table_ref[APPROX_ROW : APPROX_ROW + 1, :] = along_lanes(-obs_grad[:, 0:1] * valid)
+
+
+def prepare_kernel(
+    strips,
+    owners,
+    column_ref,
+    obs_grad_ref,
+    table_ref,
+    weight_ref,
+    twin_ref,
+    start_grad_ref,
+    row_match_ref,
+    limit_ref,
+    send_ref,
+    strip_match_ref,
+    top_matrix_ref,
+    message_ref,
+    rank_ref,
+):
+    strips_owner = NLAT * SEC_STRIPS // owners
+    column = column_ref[...]
+    info = table_ref[0:SLOTS, :]
+    spot = info[:, SPOT : SPOT + 1]
+    band = info[:, BAND : BAND + 1]
+    row_of = info[:, ROW : ROW + 1]
+    col_of = info[:, COL : COL + 1]
+    valid = info[:, VALID : VALID + 1]
+    col_row = to_row(col_of)
+    valid_row = to_row(valid)
+
+    lane = iota((SLOTS, SLOTS * SOUNDS), 1) // SOUNDS
+    slot = iota((SLOTS, SLOTS * SOUNDS), 0)
+    row_lane = jnp.sum(
+        jnp.where(lane == slot, (row_of + 1.0) * valid - 1.0, 0.0), axis=0, keepdims=True
+    )
+    row_match_ref[...] = jnp.where(row_of == row_lane, 1.0, 0.0)
+
+    same = jnp.where(col_of == col_row, 1.0, 0.0)
+    before = jnp.where(iota((SLOTS, SLOTS), 1) < iota((SLOTS, SLOTS), 0), 1.0, 0.0)
+    other = jnp.where(iota((SLOTS, SLOTS), 1) != iota((SLOTS, SLOTS), 0), same, 0.0)
+    strip_match_ref[...] = same * valid_row
+    start_grad_ref[...] = -exact_dot(same * valid_row, obs_grad_ref[...])
+    twin_ref[...] = exact_dot(other, column)
+    first = jnp.where(jnp.sum(same * before, axis=1, keepdims=True) > 0.0, 0.0, 1.0)
+    owner = jnp.floor(col_of / strips_owner)
+    owner_row = jnp.floor(col_row / strips_owner)
+    rank = jnp.sum(jnp.where(owner == owner_row, before, 0.0), axis=1, keepdims=True)
+
+    at = iota((SLOTS, LANES), 1)
+    rank_ref[...] = jnp.where(at == 0, rank, jnp.where(at == 1, first, 0.0))
     matrix = jnp.zeros((SLOTS, LANES), F32)
     for t in range(strips):
         matrix = jnp.where(at == t, top_entry(spot, t, strips), matrix)
@@ -526,6 +551,7 @@
     hot_ref,
     line_tops_ref,
     lead_ref,
+    rank_ref,
     send_ref,
     point_ref,
     top_ref,
@@ -574,9 +600,9 @@
     info = tables[0][0:SLOTS, :]
     valid = info[:, VALID : VALID + 1]
     top = top * lead_ref[:, 0:1]
-    rank = info[:, RANK : RANK + 1]
+    rank = rank_ref[:, 0:1]
     meta = jnp.where(rank == 0.0, pltpu.roll(top, ROWS, 1), pltpu.roll(top, LANES // 2 + ROWS, 1))
-    kept = jnp.where(iota((SLOTS, STRIP), 1) == 0, 0.0, point * info[:, FIRST : FIRST + 1])
+    kept = jnp.where(iota((SLOTS, STRIP), 1) == 0, 0.0, point * rank_ref[:, 1:2])
     rows = message_rows(send_ref[...], kept - STEP * (valid * grad), meta, partial)
     message_ref[...] = rows.reshape(message_ref.shape)
 
@@ -755,11 +781,11 @@
     arguments = [
         block_band.reshape(1, SB_DEV),
         observations,
-        jacobian.reshape(SLOTS * SOUNDS, STRIP),
         block_row.reshape(1, SLOTS),
         block_col.reshape(1, SLOTS),
         carry_decay.reshape(1, NBANDS),
         sparsity_weight.reshape(1, -1),
+        jacobian.reshape(SLOTS * SOUNDS, STRIP),
     ]
     message = ((owners, ROWS, LANES), F32)
     narrow = ((SLOTS, LANES), F32)
@@ -779,45 +805,24 @@
         return found
 
     arguments = [pltpu.with_memory_space_constraint(a, pltpu.HBM) for a in arguments]
-    bands, observed, flat, rows, cols, decay, weight, first = call(
+    bands, observed, rows, cols, decay, weight, flat, first = call(
         start_kernel,
         [(a.shape, a.dtype) for a in arguments] + [((owners, 2, LANES), F32)],
         *arguments,
         in_specs=[pl.BlockSpec(memory_space=pltpu.HBM)] * len(arguments),
         out_specs=[pl.BlockSpec(memory_space=pltpu.VMEM)] * (len(arguments) + 1),
-        scratch_shapes=[pltpu.SemaphoreType.DMA((len(arguments),))],
+        scratch_shapes=[pltpu.SemaphoreType.DMA((len(arguments) - 1 + PIECES,))],
     )
     first = trade(first)
-    (
-        high,
-        low,
-        column,
-        twin,
-        start_grad,
-        obs_slot,
-        row_match,
-        table,
-        limit,
-        send,
-        strip_match,
-        top_matrix,
-        prepared,
-    ) = call(
-        functools.partial(prepare_kernel, strips, owners),
+    high, low, column, obs_grad, obs_slot, table = call(
+        functools.partial(transform_kernel, strips),
         [
             ((SLOTS * SOUNDS, STRIP), BF16),
             ((SLOTS * SOUNDS, STRIP), BF16),
             strip_rows,
             strip_rows,
-            strip_rows,
             narrow,
-            ((SLOTS, SLOTS * SOUNDS), F32),
             table_rows,
-            strip_rows,
-            ((owners * ROWS, 3 * 4 * SLOTS), BF16),
-            ((SLOTS, SLOTS), F32),
-            narrow,
-            message,
         ],
         flat,
         observed,
@@ -825,12 +830,29 @@
         cols,
         block_count,
         bands,
+        in_specs=[
+            pl.BlockSpec(memory_space=pltpu.SMEM if i == 4 else pltpu.VMEM) for i in range(6)
+        ],
+    )
+    tables = with_sectors(table)
+    twin, start_grad, row_match, limit, send, strip_match, top_matrix, prepared, rank = call(
+        functools.partial(prepare_kernel, strips, owners),
+        [
+            strip_rows,
+            strip_rows,
+            ((SLOTS, SLOTS * SOUNDS), F32),
+            strip_rows,
+            ((owners * ROWS, 3 * 4 * SLOTS), BF16),
+            ((SLOTS, SLOTS), F32),
+            narrow,
+            message,
+            narrow,
+        ],
+        column,
+        obs_grad,
+        table,
         weight,
-        in_specs=[
-            pl.BlockSpec(memory_space=pltpu.SMEM if i == 4 else pltpu.VMEM) for i in range(7)
-        ],
-    )
-    tables = with_sectors(table)
+    )
     point, top, second, hot, line_tops = call(
         functools.partial(first_step_kernel, strips, owners),
         [
@@ -880,6 +902,7 @@
         hot,
         line_tops,
         lead,
+        rank,
         send,
         point,
         top,

time: 41.7 us -> 41.9 us (level)
  Pallas kernels: 8.98 us -> 9.4 us
    ppermute x2, waiting for transfers between devices: 1.71 us -> 1.26 us  [with_sectors(): found.append(lax.ppermute(values, 'tile', pairs))]
    pallas_call x7 -> x8, Pallas kernels: 8.98 us -> 9.4 us  [call(): pl.pallas_call(kernel, out_shape=[jax.ShapeDtypeStruct(shape, dtype) for...]
  transfers between devices with their start and end apart: 5 -> 5, of which waited for: 5 -> 5; matrix products, arithmetic and copies ran while one was open for 0% -> 0% of each run, Pallas kernels for 7% -> 8%
where the time goes in v3:
time: 41.9 us; the launch traced here: 41.5 us
  waiting for transfers between devices  15.6 us (37%)
  starting transfers between devices  15.2 us (36%)
  Pallas kernels  9.4 us (22%)
  between operations  1.33 us (3%)
    all_to_all x3, starting transfers between devices, trade(): return lax.all_to_all(values, 'tile', 0, 0, tiled=True)  14.4 us
    all_to_all x3, waiting for transfers between devices, trade(): return lax.all_to_all(values, 'tile', 0, 0, tiled=True)  14.3 us
    pallas_call x8, Pallas kernels, call(): pl.pallas_call(kernel, out_shape=[jax.ShapeDtypeStruct(shape, dtype) for...  9.4 us
    ppermute x2, waiting for transfers between devices, with_sectors(): found.append(lax.ppermute(values, 'tile', pairs))  1.26 us
  transfers between devices with their start and end apart: 5, of which 5 were waited for; matrix products, arithmetic and copies ran while one was open for 0% of the time, Pallas kernels for 8%

profile of v3, /device:TPU:0, one launch (start us, length us, event | category | flops | bytes accessed | tf_op | source)
XLA Modules:
  0.0 41.5 jit_solution(5734010093172780190)
XLA Ops:
  0.6 2.1 %shard_map.95 = (s32[1,32]{1,0:T(1,128)S(1)}, f32[32,64]{1,0:T(8,128)S(1)}, s32[1,16]{1,0:T(1,128)S(1)}, s32[1,16]{1,0:T(1,128)S(1)}, f32[1,128]{1,0:T(1,128)S(1...) custom-call(s32[1,32]{1,0:T(1,128)} %bitcast.9, f32[32,64]{1,0:T(8,128)} %refs_1_.1, ...), custom_call_target="tpu_custom_call" | custom-call | tf_op jit(solution)/shard_map/pallas_call | solution.py:758
  2.7 7.4 %all-to-all-start = ((f32[16,2,128]{2,1,0:T(2,128)}), f32[16,2,128]{2,1,0:T(2,128)S(1)}, u32[]{:S(2)}, u32[]{:S(2)}) async-start(f32[16,2,128]{2,1,0:T(2,128)} %get-tuple-element.42), calls=%async_computation | async-start | bytes 32768 | tf_op jit(solution)/shard_map/all_to_all | solution.py:796
  10.8 1.3 %shard_map.96 = (bf16[1024,256]{1,0:T(8,128)(2,1)S(1)}, bf16[1024,256]{1,0:T(8,128)(2,1)S(1)}, f32[16,256]{1,0:T(8,128)S(1)}, f32[16,256]{1,0:T(8,128)S(1)}, f32...) custom-call(f32[1024,256]{1,0:T(8,128)S(1)} %get-tuple-element.43.jac_ref, f32[32,64]{1,0:T(8,128)S(1)} %get-tuple-element.44.obs_ref, ...), custom_call_target="tpu_custom_call" | custom-call | tf_op jit(solution)/shard_map/pallas_call | solution.py:758
  12.1 0.5 %collective-permute-start = (f32[24,128]{1,0:T(8,128)S(1)}, f32[24,128]{1,0:T(8,128)S(1)}, u32[]{:S(2)}, u32[]{:S(2)}) collective-permute-start(f32[24,128]{1,0:T(8,128)S(1)} %get-tuple-element.50.table_ref.rest_0_), channel_id=1, source_target_pairs={{0,1},{1,0},{2,3},{3,2},{4,5},{5,4},{6,7},{7,6},{8,9},{9,8},{10,11... | collective-permute-start | bytes 36872 | tf_op jit(solution)/shard_map/ppermute | solution.py:804
  12.5 0.5 %shard_map.97 = (f32[16,256]{1,0:T(8,128)S(1)}, f32[16,256]{1,0:T(8,128)S(1)}, f32[16,1024]{1,0:T(8,128)S(1)}, f32[16,256]{1,0:T(8,128)S(1)}, bf16[128,192]{1,0:...) custom-call(f32[16,256]{1,0:T(8,128)S(1)} %get-tuple-element.48.colu, ...), custom_call_target="tpu_custom_call" | custom-call | tf_op jit(solution)/shard_map/pallas_call | solution.py:758
  13.0 0.4 collective-permute-done.rest_1_
  13.4 3.3 %all-to-all-done.first_ref = f32[16,2,128]{2,1,0:T(2,128)S(1)} async-done(((f32[16,2,128]{2,1,0:T(2,128)}), f32[16,2,128]{2,1,0:T(2,128)S(1)}, u32[]{:S(2)}, u32[]{:S(2)}) %all-to-all-start) | async-done | bytes 16416 | tf_op jit(solution)/shard_map/all_to_all | solution.py:796
  16.6 1.0 %shard_map.98 = (f32[16,256]{1,0:T(8,128)S(1)}, f32[16,128]{1,0:T(8,128)S(1)}, f32[16,8,128]{2,1,0:T(8,128)}, f32[32,128]{1,0:T(8,128)S(1)}, f32[64,128]{1,0:T(8,128)S(1)}) custom-call(f32[16,2,128]{2,1,0:T(2,128)S(1)} %all-to-all-done.first_ref, f32[16,256]{1,0:T(8,128)S(1)} %get-tuple-element.48.column_ref, f32[16,256]{1,0:T(8,128)S(1)} %get-tuple-element.52.twin_ref, ...), custom_call_target="tpu_custom_call" | custom-call | tf_op jit(solution)/shard_map/pallas_call | solution.py:758
  17.7 3.5 %all-to-all-start.1 = ((f32[16,8,128]{2,1,0:T(8,128)}), f32[16,8,128]{2,1,0:T(8,128)S(1)}, u32[]{:S(2)}, u32[]{:S(2)}) async-start(f32[16,8,128]{2,1,0:T(8,128)} %get-tuple-element.59), calls=%async_computation.1 | async-start | bytes 131072 | tf_op jit(solution)/shard_map/all_to_all | solution.py:796
  21.2 1.1 %shard_map.99 = (f32[16,256]{1,0:T(8,128)S(1)}, f32[8,128]{1,0:T(8,128)S(1)}, f32[16,128]{1,0:T(8,128)S(1)}) custom-call(f32[16,256]{1,0:T(8,128)S(1)} %get-tuple-element.60.point_ref, bf16[1024,256]{1,0:T(8,128)(2,1)S(1)} %get-tuple-element.61.high_ref, bf16[1024,256]{1,0:T(8,128)(2,1)S(1)} %get-tuple-element.62.low_ref, ...), custom_call_target="tpu_custom_call" | custom-call | tf_op jit(solution)/shard_map/pallas_call | solution.py:758
  22.3 0.3 collective-permute-start.1
  22.6 0.9 %collective-permute-done.1.rest_3_ = f32[8,128]{1,0:T(8,128)S(1)} collective-permute-done((f32[8,128]{1,0:T(8,128)S(1)}, f32[8,128]{1,0:T(8,128)S(1)}, u32[]{:S(2)}, u32[]{:S(2)}) %collective-permute-start.1) | collective-permute-done | bytes 4128 | tf_op jit(solution)/shard_map/ppermute | solution.py:804
  23.5 4.6 %all-to-all-done.1.second_ref = f32[16,8,128]{2,1,0:T(8,128)S(1)} async-done(((f32[16,8,128]{2,1,0:T(8,128)}), f32[16,8,128]{2,1,0:T(8,128)S(1)}, u32[]{:S(2)}, u32[]{:S(2)}) %all-to-all-start.1) | async-done | bytes 65568 | tf_op jit(solution)/shard_map/all_to_all | solution.py:796
  28.1 1.9 %shard_map.100 = (f32[16,8,128]{2,1,0:T(8,128)}, f32[1,1024]{1,0:T(1,128)S(1)}) custom-call(f32[16,2,128]{2,1,0:T(2,128)S(1)} %all-to-all-done.first_ref, f32[16,8,128]{2,1,0:T(8,128)S(1)} %all-to-all-done.1.second_ref, f32[16,256]{1,0:T(8,128)S(1)} %get-tuple-element.48.column_ref, f32[16,256]{1,0:T(8,128)S(1)} %get-tuple-element.52.twin_ref, ...), custom_call_target="tpu_custom_call" | custom-call | tf_op jit(solution)/shard_map/pallas_call | solution.py:758
  30.0 3.5 %all-to-all-start.2 = ((f32[16,8,128]{2,1,0:T(8,128)}), f32[16,8,128]{2,1,0:T(8,128)S(1)}, u32[]{:S(2)}, u32[]{:S(2)}) async-start(f32[16,8,128]{2,1,0:T(8,128)} %get-tuple-element.73), calls=%async_computation.2 | async-start | bytes 131072 | tf_op jit(solution)/shard_map/all_to_all | solution.py:796
  33.5 0.4 shard_map.101
  33.8 6.5 %all-to-all-done.2.third_ref = f32[16,8,128]{2,1,0:T(8,128)S(1)} async-done(((f32[16,8,128]{2,1,0:T(8,128)}), f32[16,8,128]{2,1,0:T(8,128)S(1)}, u32[]{:S(2)}, u32[]{:S(2)}) %all-to-all-start.2) | async-done | bytes 65568 | tf_op jit(solution)/shard_map/all_to_all | solution.py:796
  40.3 1.2 %shard_map.102 = (f32[32,1024]{1,0:T(8,128)}, f32[32,64]{1,0:T(8,128)}) custom-call(f32[16,2,128]{2,1,0:T(2,128)S(1)} %all-to-all-done.first_ref, f32[16,8,128]{2,1,0:T(8,128)S(1)} %all-to-all-done.2.third_ref, bf16[320,384]{1,0:T(8,128)(2,1)S(1)} %get-tuple-element.75.place_ref, f32[128,128]{1,0:T(8,128)S(1)} %get-tuple-element.76.band_hot_ref, ...), custom_call_target="tpu_custom_call" | custom-call | tf_op jit(solution)/shard_map/pallas_call | solution.py:758
Async XLA Ops:
  2.7 13.9 %all-to-all-start = ((f32[16,2,128]{2,1,0:T(2,128)}), f32[16,2,128]{2,1,0:T(2,128)S(1)}, u32[]{:S(2)}, u32[]{:S(2)}) async-start(f32[16,2,128]{2,1,0:T(2,128)} %get-tuple-element.42), calls=%async_computation | async-start | bytes 32768 | tf_op jit(solution)/shard_map/all_to_all | solution.py:796
  12.1 1.3 %collective-permute-start = (f32[24,128]{1,0:T(8,128)S(1)}, f32[24,128]{1,0:T(8,128)S(1)}, u32[]{:S(2)}, u32[]{:S(2)}) collective-permute-start(f32[24,128]{1,0:T(8,128)S(1)} %get-tuple-element.50.table_ref.rest_0_), channel_id=1, source_target_pairs={{0,1},{1,0},{2,3},{3,2},{4,5},{5,4},{6,7},{7,6},{8,9},{9,8},{10,11... | collective-permute-start | bytes 36872 | tf_op jit(solution)/shard_map/ppermute | solution.py:804
  17.7 10.4 %all-to-all-start.1 = ((f32[16,8,128]{2,1,0:T(8,128)}), f32[16,8,128]{2,1,0:T(8,128)S(1)}, u32[]{:S(2)}, u32[]{:S(2)}) async-start(f32[16,8,128]{2,1,0:T(8,128)} %get-tuple-element.59), calls=%async_computation.1 | async-start | bytes 131072 | tf_op jit(solution)/shard_map/all_to_all | solution.py:796
  22.3 1.2 %collective-permute-start.1 = (f32[8,128]{1,0:T(8,128)S(1)}, f32[8,128]{1,0:T(8,128)S(1)}, u32[]{:S(2)}, u32[]{:S(2)}) collective-permute-start(f32[8,128]{1,0:T(8,128)S(1)} %get-tuple-element.72.rest_2_), channel_id=1, source_target_pairs={{0,1},{1,0},{2,3},{3,2},{4,5},{5,4},{6,7},{7,6},{8,9},{9,8},{10,11... | collective-permute-start | bytes 12296 | tf_op jit(solution)/shard_map/ppermute | solution.py:804
  30.0 10.4 %all-to-all-start.2 = ((f32[16,8,128]{2,1,0:T(8,128)}), f32[16,8,128]{2,1,0:T(8,128)S(1)}, u32[]{:S(2)}, u32[]{:S(2)}) async-start(f32[16,8,128]{2,1,0:T(8,128)} %get-tuple-element.73), calls=%async_computation.2 | async-start | bytes 131072 | tf_op jit(solution)/shard_map/all_to_all | solution.py:796

commit v4 on v3

--- a/solution.py
+++ b/solution.py
@@ -20,7 +20,6 @@
 LANES = 128
 ROWS = 8
 STEP = 0.2
-PIECES = 8
 
 F32 = jnp.float32
 BF16 = jnp.bfloat16
@@ -86,18 +85,18 @@
 
 
 def haar_signs():
-    cell = iota((STRIP, STRIP), 0)
-    coef = iota((STRIP, STRIP), 1)
-    out = jnp.where(coef == 0, 1.0, 0.0)
-    m = 1
+    coef = iota((1, STRIP), 1).astype(F32)
+    level = jnp.zeros((1, STRIP), F32) + 1.0
+    m = 2
     while m < STRIP:
-        span = STRIP // m
-        level = (coef >= m) & (coef < 2 * m)
-        within = cell - (coef - m) * span
-        sign = jnp.where(within < span // 2, 1.0, -1.0)
-        out = jnp.where(level & (within >= 0) & (within < span), sign, out)
+        level = jnp.where(coef >= m, float(m), level)
         m *= 2
-    return out.astype(BF16)
+    first = coef == 0.0
+    shift = jnp.where(first, 0.0, coef - level)
+    half = jnp.where(first, 2.0, 0.5)
+    within = iota((STRIP, STRIP), 0).astype(F32) * (level / STRIP) - shift
+    inside = (within >= 0.0) & (within < 1.0)
+    return jnp.where(inside, jnp.where(within < half, 1.0, -1.0), 0.0).astype(BF16)
 
 
 def haar_scales():
@@ -197,17 +196,12 @@
 
 
 def start_kernel(*refs):
-    fetched = (len(refs) - 2) // 2
+    fetched = (len(refs) - 3) // 2
     sources, targets = refs[:fetched], refs[fetched : 2 * fetched]
-    out_ref, sems = refs[2 * fetched :]
-    pairs = list(zip(sources, targets))
-    wide_source, wide_target = pairs.pop()
-    part = wide_source.shape[0] // PIECES
-    for start in range(0, wide_source.shape[0], part):
-        pairs.append((wide_source.at[start : start + part], wide_target.at[start : start + part]))
+    out_ref, made_ref, sems = refs[2 * fetched :]
     copies = [
         pltpu.make_async_copy(source, target, sems.at[i])
-        for i, (source, target) in enumerate(pairs)
+        for i, (source, target) in enumerate(zip(sources, targets))
     ]
     for copy in copies:
         copy.start()
@@ -218,11 +212,14 @@
     sums = jnp.sum(obs_ref[...], axis=1, keepdims=True)
     counted = jnp.sum(hot, axis=0, keepdims=True)
     summed = jnp.sum(hot * sums, axis=0, keepdims=True)
-    for t in range(out_ref.shape[0]):
-        out_ref[t, 0:1, :] = counted
-        out_ref[t, 1:2, :] = summed
+    for t in range(made_ref.shape[0]):
+        made_ref[t, 0:1, :] = counted
+        made_ref[t, 1:2, :] = summed
+    sent = pltpu.make_async_copy(made_ref, out_ref, sems.at[fetched])
+    sent.start()
     for copy in copies[2:]:
         copy.wait()
+    sent.wait()
 
 
 def along_lanes(col):
@@ -443,6 +440,10 @@
     return jnp.where(iota((SLOTS, SLOTS), 0) == iota((SLOTS, SLOTS), 1), 0.0, strip_match)
 
 
+def matched(match, grads):
+    return dot(jnp.concatenate([match] * 3, axis=1).astype(BF16), split_rows(grads))
+
+
 def first_step_kernel(
     strips,
     owners,
@@ -456,12 +457,17 @@
     decay_ref,
     weight_ref,
     prepared_ref,
+    high_ref,
+    low_ref,
+    row_match_ref,
+    obs_slot_ref,
     *rest,
 ):
     sectors = strips // SEC_STRIPS
     tables = rest[:sectors]
-    point_ref, top_ref, message_ref, hot_ref, line_tops_ref = rest[sectors:]
-    window = lax.axis_index("tile") // sectors
+    point_ref, top_ref, message_ref, hot_ref, line_tops_ref, grad_out_ref, lead_ref = rest[sectors:]
+    my_index = lax.axis_index("tile")
+    window = my_index // sectors
     sums = weekly([first_ref[t, 1:2, :] for t in range(owners)], sectors)
     returned = scan_back([-s for s in sums], decay_ref[...])
     scalar = pick(returned, window) / SOUNDS
@@ -497,39 +503,24 @@
     point_ref[...] = point
     top_ref[...] = top
     partial = band_partial(point, column, hot[:SLOTS])
-    is_partial = iota(message_ref.shape, 1) == 4
-    message_ref[...] = jnp.where(is_partial, partial.reshape(1, 1, LANES), prepared_ref[...])
-
-
-def local_grad_kernel(
-    strips,
-    point_ref,
-    high_ref,
-    low_ref,
-    row_match_ref,
-    obs_slot_ref,
-    strip_match_ref,
-    *rest,
-):
-    sectors = strips // SEC_STRIPS
-    tables = rest[:sectors]
-    grad_ref, approx_ref, lead_ref = rest[sectors:]
-    values = forward(point_ref[...], high_ref, low_ref)
+    values = forward(point, high_ref, low_ref)
     chosen = fold(row_match_ref[...], values) - obs_slot_ref[...]
     grad = back_project(chosen, high_ref, low_ref)
-    grad_ref[...] = exact_dot(strip_match_ref[...], grad)
+    grad_out_ref[...] = matched(strip_match_ref[...], grad)
     info = tables[0][0:SLOTS, :]
-    approx = grad[:, 0:1] * info[:, VALID : VALID + 1]
-    approx_ref[...] = jnp.broadcast_to(along_lanes(approx), approx_ref.shape)
-
-    sector = lax.rem(lax.axis_index("tile"), sectors).astype(F32)
-    line_row = side_by_side([t[LINE_ROW : LINE_ROW + 1, :] for t in tables])
-    spot_row = side_by_side([t[SPOT_ROW : SPOT_ROW + 1, :] for t in tables])
-    sector_row = jnp.floor((spot_row - 1.0) / SEC_STRIPS)
+    approx = along_lanes(grad[:, 0:1] * info[:, VALID : VALID + 1])
+    kind = iota(message_ref.shape, 1)
+    message_ref[...] = jnp.where(
+        kind == 4,
+        partial.reshape(1, 1, LANES),
+        jnp.where(kind == 6, approx.reshape(1, 1, LANES), prepared_ref[...]),
+    )
+
+    sector = lax.rem(my_index, sectors).astype(F32)
+    sector_row = jnp.floor(spot_row / SEC_STRIPS)
     lane = iota((SLOTS, LANES), 1)
     before = jnp.where(lane < iota((SLOTS, LANES), 0), 1.0, 0.0)
     earlier = jnp.where(lane < SLOTS, before, jnp.where(sector_row < sector, 1.0, 0.0))
-    on_line = info[:, LINE : LINE + 1] + 1.0 == line_row
     taken = jnp.sum(jnp.where(on_line, earlier, 0.0), axis=1, keepdims=True)
     lead_ref[...] = jnp.broadcast_to(jnp.where(taken > 0.0, 0.0, 1.0), lead_ref.shape)
 
@@ -563,9 +554,14 @@
 ):
     sectors = strips // SEC_STRIPS
     tables, rest = rest[:sectors], rest[sectors:]
-    approx_refs, rest = rest[:sectors], rest[sectors:]
     message_ref, values_ref = rest
-    window = lax.axis_index("tile") // sectors
+    my_index = lax.axis_index("tile")
+    window = my_index // sectors
+    sector = lax.rem(my_index, sectors)
+    approx_rows = []
+    for shift in range(sectors):
+        pair = window * sectors + lax.rem(sector + (sectors - shift), sectors)
+        approx_rows.append(second_ref[pair, 6:7, :])
     combined, _ = background(
         first_ref, [second_ref[t, 4:5, :] for t in range(owners)], decay_ref[...], sectors
     )
@@ -580,7 +576,7 @@
         column,
         twin_ref[...],
         twins(strip_match_ref[...]),
-        side_by_side([r[0:1, :] for r in approx_refs]),
+        side_by_side(approx_rows),
         side_by_side([t[TOTAL_ROW : TOTAL_ROW + 1, :] for t in tables]),
         line_tops_ref[...],
     )
@@ -607,20 +603,7 @@
     message_ref[...] = rows.reshape(message_ref.shape)
 
 
-def place_kernel(
-    strips,
-    owners,
-    second_ref,
-    table_ref,
-    values_ref,
-    obs_ref,
-    band_ref,
-    place_ref,
-    band_hot_ref,
-    scaled_ref,
-    differ_ref,
-    block_hot_ref,
-):
+def placing(strips, owners, second_ref, table_ref, values_ref, obs_ref, band_ref):
     sectors = strips // SEC_STRIPS
     lines = NLAT // owners
     count = owners * ROWS
@@ -639,8 +622,8 @@
         strip_rows.append(jnp.sum(jnp.where(pair_of, strip, 0.0), axis=0, keepdims=True) - 1.0)
         band_tall = jnp.sum(jnp.where(tall_pair, to_row(band), 0.0), axis=1, keepdims=True)
         band_col = jnp.where(tall_kind // 2 == q, band_tall, band_col)
-    band_hot_ref[...] = one_hot_bands(band_col - 1.0)
-    scaled_ref[...] = jnp.where(tall_kind < 4, STEP * second_ref[...].reshape(count, LANES), 0.0)
+    band_hot = one_hot_bands(band_col - 1.0)
+    scaled = jnp.where(tall_kind < 4, STEP * second_ref[...].reshape(count, LANES), 0.0)
 
     def line_of(strip):
         return jnp.floor(strip / SEC_STRIPS)
@@ -665,7 +648,7 @@
         hit = (window == window_col) & (line_of(strip_rows[q]) == line_col) & (strip_rows[q] >= 0.0) & (kind == 5)
         parts.append(jnp.where(hit, 1.0, 0.0))
     place = jnp.concatenate(parts, axis=0).astype(BF16)
-    place_ref[...] = jnp.concatenate([place, place, place], axis=1)
+    place = jnp.concatenate([place, place, place], axis=1)
 
     info = table_ref[0:SLOTS, :]
     lane = iota((SLOTS, SLOTS * SOUNDS), 1) // SOUNDS
@@ -676,8 +659,9 @@
         keepdims=True,
     )
     per_row = jnp.where(iota((SB_DEV, SLOTS * SOUNDS), 0).astype(F32) + 1.0 == row_lane, 1.0, 0.0)
-    differ_ref[...] = fold(per_row, values_ref[...])[:, :SOUNDS] - obs_ref[...]
-    block_hot_ref[...] = one_hot_bands(to_col(band_ref[...].astype(F32)))
+    differ = fold(per_row, values_ref[...])[:, :SOUNDS] - obs_ref[...]
+    block_hot = one_hot_bands(to_col(band_ref[...].astype(F32)))
+    return place, band_hot, scaled, differ, block_hot
 
 
 def finish_kernel(
@@ -685,13 +669,13 @@
     owners,
     first_ref,
     third_ref,
-    place_ref,
-    band_hot_ref,
-    scaled_ref,
+    second_ref,
+    table_ref,
+    values_ref,
+    obs_ref,
+    band_ref,
     decay_ref,
     weight_ref,
-    differ_ref,
-    block_hot_ref,
     out_ref,
     misfit_ref,
 ):
@@ -699,17 +683,20 @@
     blocks = NLAT // owners * WIN
     count = owners * ROWS
     window = lax.axis_index("tile") // sectors
+    place, band_hot, scaled, differ, block_hot = placing(
+        strips, owners, second_ref, table_ref, values_ref, obs_ref, band_ref
+    )
     combined, carried = background(
         first_ref, [third_ref[t, 4:5, :] for t in range(owners)], decay_ref[...], sectors
     )
     spread = jnp.concatenate(
         [jnp.broadcast_to(row, (sectors * ROWS, NBANDS)) for row in combined], axis=0
     )
-    scalars = jnp.sum(band_hot_ref[...] * spread, axis=1, keepdims=True)
-    rows = third_ref[...].reshape(count, LANES) - scalars * scaled_ref[...]
-    placed = dot(place_ref[...], split_rows(rows))
-    offset = jnp.sum(block_hot_ref[...] * pick(carried, window), axis=1, keepdims=True)
-    misfit_ref[...] = differ_ref[...] + offset
+    scalars = jnp.sum(band_hot * spread, axis=1, keepdims=True)
+    rows = third_ref[...].reshape(count, LANES) - scalars * scaled
+    placed = dot(place, split_rows(rows))
+    offset = jnp.sum(block_hot * pick(carried, window), axis=1, keepdims=True)
+    misfit_ref[...] = differ + offset
 
     lane = iota((1, LANES), 1)
     for j in range(strips):
@@ -810,8 +797,12 @@
         [(a.shape, a.dtype) for a in arguments] + [((owners, 2, LANES), F32)],
         *arguments,
         in_specs=[pl.BlockSpec(memory_space=pltpu.HBM)] * len(arguments),
-        out_specs=[pl.BlockSpec(memory_space=pltpu.VMEM)] * (len(arguments) + 1),
-        scratch_shapes=[pltpu.SemaphoreType.DMA((len(arguments) - 1 + PIECES,))],
+        out_specs=[pl.BlockSpec(memory_space=pltpu.VMEM)] * len(arguments)
+        + [pl.BlockSpec(memory_space=pltpu.HBM)],
+        scratch_shapes=[
+            pltpu.VMEM((owners, 2, LANES), F32),
+            pltpu.SemaphoreType.DMA((len(arguments) + 1,)),
+        ],
     )
     first = trade(first)
     high, low, column, obs_grad, obs_slot, table = call(
@@ -853,7 +844,7 @@
         table,
         weight,
     )
-    point, top, second, hot, line_tops = call(
+    point, top, second, hot, line_tops, grad, lead = call(
         functools.partial(first_step_kernel, strips, owners),
         [
             strip_rows,
@@ -861,6 +852,8 @@
             message,
             ((sectors * SLOTS, NBANDS), F32),
             ((strips * SLOTS, LANES), F32),
+            strip_rows,
+            narrow,
         ],
         first,
         column,
@@ -872,20 +865,13 @@
         decay,
         weight,
         prepared,
-        *tables,
-    )
-    second = trade(second)
-    grad, approx, lead = call(
-        functools.partial(local_grad_kernel, strips),
-        [strip_rows, ((ROWS, LANES), F32), narrow],
-        point,
         high,
         low,
         row_match,
         obs_slot,
-        strip_match,
         *tables,
     )
+    second = trade(second)
     third, values = call(
         functools.partial(second_step_kernel, strips, owners, betas[1]),
         [message, ((1, SLOTS * SOUNDS), F32)],
@@ -911,37 +897,20 @@
         row_match,
         obs_slot,
         *tables,
-        *with_sectors(approx),
     )
     third = trade(third)
-    placed_rows = (2 * strips + 2) * lines * WIN
-    place, band_hot, scaled, differ, block_hot = call(
-        functools.partial(place_kernel, strips, owners),
-        [
-            ((placed_rows, 3 * owners * ROWS), BF16),
-            ((owners * ROWS, NBANDS), F32),
-            ((owners * ROWS, LANES), F32),
-            ((SB_DEV, SOUNDS), F32),
-            ((SB_DEV, NBANDS), F32),
-        ],
+    coeffs, misfit = call(
+        functools.partial(finish_kernel, strips, owners),
+        [((lines * WIN, strips * STRIP), F32), ((SB_DEV, SOUNDS), F32)],
+        first,
+        third,
         second,
         table,
         values,
         observed,
         bands,
-    )
-    coeffs, misfit = call(
-        functools.partial(finish_kernel, strips, owners),
-        [((lines * WIN, strips * STRIP), F32), ((SB_DEV, SOUNDS), F32)],
-        first,
-        third,
-        place,
-        band_hot,
-        scaled,
         decay,
         weight,
-        differ,
-        block_hot,
     )
     return (coeffs.reshape(lines, WIN, strips * STRIP), misfit)
 

time: 41.9 us -> 39.3 us (0.938)
  blocking collectives: 0 us -> 19 us
  waiting for transfers between devices: 15.6 us -> 3.84 us
  starting transfers between devices: 15.2 us -> 7.87 us
  Pallas kernels: 9.4 us -> 7.05 us
    all_to_all x0 -> x2, blocking collectives: none -> 19 us  [trade(): return lax.all_to_all(values, 'tile', 0, 0, tiled=True)]
    all_to_all x3 -> x1, waiting for transfers between devices: 14.3 us -> 3.46 us  [trade(): return lax.all_to_all(values, 'tile', 0, 0, tiled=True)]
    all_to_all x3 -> x1, starting transfers between devices: 14.4 us -> 7.4 us  [trade(): return lax.all_to_all(values, 'tile', 0, 0, tiled=True)]
    pallas_call x8 -> x6, Pallas kernels: 9.4 us -> 7.05 us  [call(): pl.pallas_call(kernel, out_shape=[jax.ShapeDtypeStruct(shape, dtype) for...]
    ppermute x2 -> x1, waiting for transfers between devices: 1.26 us -> 0.38 us  [with_sectors(): found.append(lax.ppermute(values, 'tile', pairs))]
  transfers between devices with their start and end apart: 5 -> 2, of which waited for: 5 -> 2; matrix products, arithmetic and copies ran while one was open for 0% -> 0% of each run, Pallas kernels for 8% -> 4%
where the time goes in v4:
time: 39.3 us; the launch traced here: 39 us
  blocking collectives  19 us (48%)
  starting transfers between devices  7.87 us (20%)
  Pallas kernels  7.05 us (18%)
  waiting for transfers between devices  3.84 us (10%)
  between operations  1.31 us (3%)
    all_to_all x2, blocking collectives, trade(): return lax.all_to_all(values, 'tile', 0, 0, tiled=True)  19 us
    all_to_all x1, starting transfers between devices, trade(): return lax.all_to_all(values, 'tile', 0, 0, tiled=True)  7.4 us
    pallas_call x6, Pallas kernels, call(): pl.pallas_call(kernel, out_shape=[jax.ShapeDtypeStruct(shape, dtype) for...  7.05 us
    all_to_all x1, waiting for transfers between devices, trade(): return lax.all_to_all(values, 'tile', 0, 0, tiled=True)  3.46 us
  transfers between devices with their start and end apart: 2, of which 2 were waited for; matrix products, arithmetic and copies ran while one was open for 0% of the time, Pallas kernels for 4%

profile of v4, /device:TPU:0, one launch (start us, length us, event | category | flops | bytes accessed | tf_op | source)
XLA Modules:
  0.0 39.0 jit_solution(12646272542748902093)
XLA Ops:
  0.6 1.5 %shard_map.95 = (s32[1,32]{1,0:T(1,128)S(1)}, f32[32,64]{1,0:T(8,128)S(1)}, s32[1,16]{1,0:T(1,128)S(1)}, s32[1,16]{1,0:T(1,128)S(1)}, f32[1,128]{1,0:T(1,128)S(1...) custom-call(s32[1,32]{1,0:T(1,128)} %bitcast.9, f32[32,64]{1,0:T(8,128)} %refs_1_.1, ...), custom_call_target="tpu_custom_call" | custom-call | tf_op jit(solution)/shard_map/pallas_call | solution.py:745
  2.1 7.4 %all-to-all-start = ((f32[16,2,128]{2,1,0:T(2,128)}), f32[16,2,128]{2,1,0:T(2,128)S(1)}, u32[]{:S(2)}, u32[]{:S(2)}) async-start(f32[16,2,128]{2,1,0:T(2,128)} %get-tuple-element.36), calls=%async_computation | async-start | bytes 32768 | tf_op jit(solution)/shard_map/all_to_all | solution.py:783
  10.2 1.1 %shard_map.96 = (bf16[1024,256]{1,0:T(8,128)(2,1)S(1)}, bf16[1024,256]{1,0:T(8,128)(2,1)S(1)}, f32[16,256]{1,0:T(8,128)S(1)}, f32[16,256]{1,0:T(8,128)S(1)}, f32...) custom-call(f32[1024,256]{1,0:T(8,128)S(1)} %get-tuple-element.37.jac_ref, f32[32,64]{1,0:T(8,128)S(1)} %get-tuple-element.38.obs_ref, ...), custom_call_target="tpu_custom_call" | custom-call | tf_op jit(solution)/shard_map/pallas_call | solution.py:745
  11.3 0.5 %collective-permute-start = (f32[24,128]{1,0:T(8,128)S(1)}, f32[24,128]{1,0:T(8,128)S(1)}, u32[]{:S(2)}, u32[]{:S(2)}) collective-permute-start(f32[24,128]{1,0:T(8,128)S(1)} %get-tuple-element.44.table_ref.rest_0_), channel_id=1, source_target_pairs={{0,1},{1,0},{2,3},{3,2},{4,5},{5,4},{6,7},{7,6},{8,9},{9,8},{10,11... | collective-permute-start | bytes 36872 | tf_op jit(solution)/shard_map/ppermute | solution.py:791
  11.8 0.5 %shard_map.97 = (f32[16,256]{1,0:T(8,128)S(1)}, f32[16,256]{1,0:T(8,128)S(1)}, f32[16,1024]{1,0:T(8,128)S(1)}, f32[16,256]{1,0:T(8,128)S(1)}, bf16[128,192]{1,0:...) custom-call(f32[16,256]{1,0:T(8,128)S(1)} %get-tuple-element.42.colu, ...), custom_call_target="tpu_custom_call" | custom-call | tf_op jit(solution)/shard_map/pallas_call | solution.py:745
  12.2 0.4 collective-permute-done.rest_1_
  12.6 3.5 %all-to-all-done.first_ref = f32[16,2,128]{2,1,0:T(2,128)S(1)} async-done(((f32[16,2,128]{2,1,0:T(2,128)}), f32[16,2,128]{2,1,0:T(2,128)S(1)}, u32[]{:S(2)}, u32[]{:S(2)}) %all-to-all-start) | async-done | bytes 16416 | tf_op jit(solution)/shard_map/all_to_all | solution.py:783
  16.1 1.3 %shard_map.98 = (f32[16,256]{1,0:T(8,128)S(1)}, f32[16,128]{1,0:T(8,128)S(1)}, f32[16,8,128]{2,1,0:T(8,128)S(1)}, f32[32,128]{1,0:T(8,128)S(1)}, f32[64,128]{1,0...) custom-call(f32[16,2,128]{2,1,0:T(2,128)S(1)} %all-to-all-done.first_ref, ...), custom_call_target="tpu_custom_call" | custom-call | tf_op jit(solution)/shard_map/pallas_call | solution.py:745
  17.4 9.5 %all_to_all.15.second_ref = f32[16,8,128]{2,1,0:T(8,128)S(1)} all-to-all(f32[16,8,128]{2,1,0:T(8,128)S(1)} %get-tuple-element.57), channel_id=1, replica_groups=mesh['ens'=2,'tile'=16] {'tile'}, dimensions={0} | all-to-all | bytes 131072 | tf_op jit(solution)/shard_map/all_to_all | solution.py:783
  26.9 1.3 %shard_map.99 = (f32[16,8,128]{2,1,0:T(8,128)S(1)}, f32[1,1024]{1,0:T(1,128)S(1)}) custom-call(f32[16,2,128]{2,1,0:T(2,128)S(1)} %all-to-all-done.first_ref, f32[16,8,128]{2,1,0:T(8,128)S(1)} %all_to_all.15.second_ref, f32[16,256]{1,0:T(8,128)S(1)} %get-tuple-element.42.column_ref, f32[16,256]{1,0:T(8,128)S(1)} %get-tuple-element.46.twin_ref, ...), custom_call_target="tpu_custom_call" | custom-call | tf_op jit(solution)/shard_map/pallas_call | solution.py:745
  28.1 9.5 %all_to_all.16.third_ref = f32[16,8,128]{2,1,0:T(8,128)S(1)} all-to-all(f32[16,8,128]{2,1,0:T(8,128)S(1)} %get-tuple-element.66), channel_id=1, replica_groups=mesh['ens'=2,'tile'=16] {'tile'}, dimensions={0} | all-to-all | bytes 131072 | tf_op jit(solution)/shard_map/all_to_all | solution.py:783
  37.6 1.4 %shard_map.100 = (f32[32,1024]{1,0:T(8,128)}, f32[32,64]{1,0:T(8,128)}) custom-call(f32[16,2,128]{2,1,0:T(2,128)S(1)} %all-to-all-done.first_ref, f32[16,8,128]{2,1,0:T(8,128)S(1)} %all_to_all.16.third_ref, f32[16,8,128]{2,1,0:T(8,128)S(1)} %all_to_all.15.second_ref, f32[24,128]{1,0:T(8,128)S(1)} %get-tuple-element.44.table_ref.rest_0_, ...), custom_call_target="tpu_custom_call" | custom-call | tf_op jit(solution)/shard_map/pallas_call | solution.py:745
Async XLA Ops:
  2.1 13.9 %all-to-all-start = ((f32[16,2,128]{2,1,0:T(2,128)}), f32[16,2,128]{2,1,0:T(2,128)S(1)}, u32[]{:S(2)}, u32[]{:S(2)}) async-start(f32[16,2,128]{2,1,0:T(2,128)} %get-tuple-element.36), calls=%async_computation | async-start | bytes 32768 | tf_op jit(solution)/shard_map/all_to_all | solution.py:783
  11.3 1.3 %collective-permute-start = (f32[24,128]{1,0:T(8,128)S(1)}, f32[24,128]{1,0:T(8,128)S(1)}, u32[]{:S(2)}, u32[]{:S(2)}) collective-permute-start(f32[24,128]{1,0:T(8,128)S(1)} %get-tuple-element.44.table_ref.rest_0_), channel_id=1, source_target_pairs={{0,1},{1,0},{2,3},{3,2},{4,5},{5,4},{6,7},{7,6},{8,9},{9,8},{10,11... | collective-permute-start | bytes 36872 | tf_op jit(solution)/shard_map/ppermute | solution.py:791

commit v5 on v4

--- a/solution.py
+++ b/solution.py
@@ -20,6 +20,7 @@
 LANES = 128
 ROWS = 8
 STEP = 0.2
+MISFIT = 32
 
 F32 = jnp.float32
 BF16 = jnp.bfloat16
@@ -168,31 +169,40 @@
     return jnp.where(band_col == iota((band_col.shape[0], NBANDS), 1).astype(F32), 1.0, 0.0)
 
 
-def own_block_mask(rows):
-    return iota((rows, SLOTS * SOUNDS), 0) == iota((rows, SLOTS * SOUNDS), 1) // SOUNDS
-
-
-def back_project(chosen, high_ref, low_ref):
-    wide = jnp.concatenate([chosen] * (SLOTS * SOUNDS // LANES), axis=1)
-    spread = jnp.where(own_block_mask(SLOTS), wide, 0.0)
-    high, low = split(spread)
-    both = dot(jnp.concatenate([high, low], axis=0), high_ref[...])
-    return both[:SLOTS] + both[SLOTS:] + dot(high, low_ref[...])
-
-
-def forward(point, high_ref, low_ref):
-    high, low = split(point)
-    both = dot_nt(jnp.concatenate([high, low], axis=0), high_ref[...])
-    full = both[:SLOTS] + both[SLOTS:] + dot_nt(high, low_ref[...])
-    return jnp.sum(jnp.where(own_block_mask(SLOTS), full, 0.0), axis=0, keepdims=True)
-
-
-def fold(weights, values):
-    product = weights * values
-    total = product[:, :LANES]
-    for start in range(LANES, SLOTS * SOUNDS, LANES):
-        total = total + product[:, start : start + LANES]
-    return total + pltpu.roll(total, SOUNDS, 1)
+def forward(point, blocks_ref, mix):
+    total = None
+    for k in range(SLOTS):
+        product = blocks_ref[k * SOUNDS : (k + 1) * SOUNDS, :] * point[k : k + 1, :]
+        values = jnp.sum(product[:, :LANES] + product[:, LANES:], axis=1, keepdims=True)
+        term = values * mix[k : k + 1, :]
+        total = term if total is None else total + term
+    return total
+
+
+def back_rows(chosen, blocks_ref):
+    return [
+        jnp.sum(
+            blocks_ref[k * SOUNDS : (k + 1) * SOUNDS, :] * chosen[:, k : k + 1],
+            axis=0,
+            keepdims=True,
+        )
+        for k in range(SLOTS)
+    ]
+
+
+def stack_rows(rows):
+    at = iota((SLOTS, STRIP), 0)
+    out = jnp.broadcast_to(rows[0], (SLOTS, STRIP))
+    for k in range(1, SLOTS):
+        out = jnp.where(at == k, rows[k], out)
+    return out
+
+
+def mix_rows(match, rows):
+    out = match[:, 0:1] * rows[0]
+    for k in range(1, SLOTS):
+        out = out + match[:, k : k + 1] * rows[k]
+    return out
 
 
 def start_kernel(*refs):
@@ -236,11 +246,11 @@
     col_ref,
     count_ref,
     band_ref,
-    high_ref,
-    low_ref,
+    blocks_ref,
     column_ref,
     obs_grad_ref,
     obs_slot_ref,
+    mix_ref,
     table_ref,
 ):
     sectors = strips // SEC_STRIPS
@@ -248,16 +258,9 @@
     signs = haar_signs()
     scales = haar_scales()
     chunk = STRIP
-    per = chunk // SOUNDS
-    columns = []
     for start in range(0, SLOTS * SOUNDS, chunk):
         high, low = split(jac_ref[start : start + chunk, :])
-        changed = (dot(high, signs) + dot(low, signs)) * scales
-        high, low = split(changed)
-        high_ref[start : start + chunk, :] = high
-        low_ref[start : start + chunk, :] = low
-        columns.append(jnp.sum(changed.reshape(per, SOUNDS, STRIP), axis=1))
-    column = jnp.concatenate(columns, axis=0)
+        blocks_ref[start : start + chunk, :] = (dot(high, signs) + dot(low, signs)) * scales
 
     row_of = to_col(row_ref[...].astype(F32))
     col_of = to_col(col_ref[...].astype(F32))
@@ -268,12 +271,21 @@
     band_row = band_ref[...].astype(F32)
     band = jnp.sum(row_hot * band_row, axis=1, keepdims=True)
     band = jnp.where(valid > 0.0, band, -1.0)
-    observed = obs_ref[...]
-    obs_slot = exact_dot(row_hot, jnp.concatenate([observed, observed], axis=1))
+    lane = iota((1, LANES), 1)
+    wanted = jnp.where(lane < SLOTS, along_lanes(row_of), -1.0)
+    wanted_hot = jnp.where(iota((SB_DEV, LANES), 0).astype(F32) == wanted, 1.0, 0.0)
+    obs_slot = exact_dot(obs_ref[...].T, wanted_hot)
     obs_slot_ref[...] = obs_slot
-    obs_grad = back_project(obs_slot, high_ref, low_ref)
+    block_lane = (lane >= MISFIT) & (lane < MISFIT + SB_DEV)
+    wanted = jnp.where(block_lane, (lane - MISFIT).astype(F32), wanted)
+    mix_ref[...] = jnp.where(row_of == wanted, valid, 0.0)
+    obs_grad = stack_rows(back_rows(obs_slot, blocks_ref))
     obs_grad_ref[...] = obs_grad
-    column = column * valid
+    ones = [
+        jnp.sum(blocks_ref[k * SOUNDS : (k + 1) * SOUNDS, :], axis=0, keepdims=True)
+        for k in range(SLOTS)
+    ]
+    column = stack_rows(ones) * valid
     column_ref[...] = column
 
     at = iota((SLOTS, LANES), 1)
@@ -305,7 +317,6 @@
     weight_ref,
     twin_ref,
     start_grad_ref,
-    row_match_ref,
     limit_ref,
     send_ref,
     strip_match_ref,
@@ -318,18 +329,10 @@
     info = table_ref[0:SLOTS, :]
     spot = info[:, SPOT : SPOT + 1]
     band = info[:, BAND : BAND + 1]
-    row_of = info[:, ROW : ROW + 1]
     col_of = info[:, COL : COL + 1]
     valid = info[:, VALID : VALID + 1]
     col_row = to_row(col_of)
     valid_row = to_row(valid)
-
-    lane = iota((SLOTS, SLOTS * SOUNDS), 1) // SOUNDS
-    slot = iota((SLOTS, SLOTS * SOUNDS), 0)
-    row_lane = jnp.sum(
-        jnp.where(lane == slot, (row_of + 1.0) * valid - 1.0, 0.0), axis=0, keepdims=True
-    )
-    row_match_ref[...] = jnp.where(row_of == row_lane, 1.0, 0.0)
 
     same = jnp.where(col_of == col_row, 1.0, 0.0)
     before = jnp.where(iota((SLOTS, SLOTS), 1) < iota((SLOTS, SLOTS), 0), 1.0, 0.0)
@@ -440,10 +443,6 @@
     return jnp.where(iota((SLOTS, SLOTS), 0) == iota((SLOTS, SLOTS), 1), 0.0, strip_match)
 
 
-def matched(match, grads):
-    return dot(jnp.concatenate([match] * 3, axis=1).astype(BF16), split_rows(grads))
-
-
 def first_step_kernel(
     strips,
     owners,
@@ -457,9 +456,8 @@
     decay_ref,
     weight_ref,
     prepared_ref,
-    high_ref,
-    low_ref,
-    row_match_ref,
+    blocks_ref,
+    mix_ref,
     obs_slot_ref,
     *rest,
 ):
@@ -503,12 +501,15 @@
     point_ref[...] = point
     top_ref[...] = top
     partial = band_partial(point, column, hot[:SLOTS])
-    values = forward(point, high_ref, low_ref)
-    chosen = fold(row_match_ref[...], values) - obs_slot_ref[...]
-    grad = back_project(chosen, high_ref, low_ref)
-    grad_out_ref[...] = matched(strip_match_ref[...], grad)
+    chosen = forward(point, blocks_ref, mix_ref[...]) - obs_slot_ref[...]
+    rows = back_rows(chosen, blocks_ref)
+    grad_out_ref[...] = mix_rows(strip_match_ref[...], rows)
     info = tables[0][0:SLOTS, :]
-    approx = along_lanes(grad[:, 0:1] * info[:, VALID : VALID + 1])
+    at = iota((SLOTS, LANES), 0)
+    fronts = jnp.broadcast_to(rows[0][:, :LANES], (SLOTS, LANES))
+    for k in range(1, SLOTS):
+        fronts = jnp.where(at == k, rows[k][:, :LANES], fronts)
+    approx = along_lanes(fronts[:, 0:1] * info[:, VALID : VALID + 1])
     kind = iota(message_ref.shape, 1)
     message_ref[...] = jnp.where(
         kind == 4,
@@ -546,9 +547,8 @@
     send_ref,
     point_ref,
     top_ref,
-    high_ref,
-    low_ref,
-    row_match_ref,
+    blocks_ref,
+    mix_ref,
     obs_slot_ref,
     *rest,
 ):
@@ -587,10 +587,9 @@
     point = updated + beta * (updated - old)
     top = top + beta * (top - old_top)
     point = with_approx(point, top, top_matrix_ref[...])
-    values = forward(point, high_ref, low_ref)
+    values = forward(point, blocks_ref, mix_ref[...])
     values_ref[...] = values
-    chosen = fold(row_match_ref[...], values) - obs_slot_ref[...]
-    grad = back_project(chosen, high_ref, low_ref)
+    grad = stack_rows(back_rows(values - obs_slot_ref[...], blocks_ref))
 
     partial = band_partial(point, column, hot[:SLOTS])
     info = tables[0][0:SLOTS, :]
@@ -603,7 +602,7 @@
     message_ref[...] = rows.reshape(message_ref.shape)
 
 
-def placing(strips, owners, second_ref, table_ref, values_ref, obs_ref, band_ref):
+def placing(strips, owners, second_ref, values_ref, obs_ref, band_ref):
     sectors = strips // SEC_STRIPS
     lines = NLAT // owners
     count = owners * ROWS
@@ -650,16 +649,7 @@
     place = jnp.concatenate(parts, axis=0).astype(BF16)
     place = jnp.concatenate([place, place, place], axis=1)
 
-    info = table_ref[0:SLOTS, :]
-    lane = iota((SLOTS, SLOTS * SOUNDS), 1) // SOUNDS
-    slot = iota((SLOTS, SLOTS * SOUNDS), 0)
-    row_lane = jnp.sum(
-        jnp.where(lane == slot, (info[:, ROW : ROW + 1] + 1.0) * info[:, VALID : VALID + 1], 0.0),
-        axis=0,
-        keepdims=True,
-    )
-    per_row = jnp.where(iota((SB_DEV, SLOTS * SOUNDS), 0).astype(F32) + 1.0 == row_lane, 1.0, 0.0)
-    differ = fold(per_row, values_ref[...])[:, :SOUNDS] - obs_ref[...]
+    differ = values_ref[...].T[MISFIT : MISFIT + SB_DEV, :] - obs_ref[...]
     block_hot = one_hot_bands(to_col(band_ref[...].astype(F32)))
     return place, band_hot, scaled, differ, block_hot
 
@@ -670,7 +660,6 @@
     first_ref,
     third_ref,
     second_ref,
-    table_ref,
     values_ref,
     obs_ref,
     band_ref,
@@ -684,7 +673,7 @@
     count = owners * ROWS
     window = lax.axis_index("tile") // sectors
     place, band_hot, scaled, differ, block_hot = placing(
-        strips, owners, second_ref, table_ref, values_ref, obs_ref, band_ref
+        strips, owners, second_ref, values_ref, obs_ref, band_ref
     )
     combined, carried = background(
         first_ref, [third_ref[t, 4:5, :] for t in range(owners)], decay_ref[...], sectors
@@ -805,13 +794,13 @@
         ],
     )
     first = trade(first)
-    high, low, column, obs_grad, obs_slot, table = call(
+    blocks, column, obs_grad, obs_slot, mix, table = call(
         functools.partial(transform_kernel, strips),
         [
-            ((SLOTS * SOUNDS, STRIP), BF16),
-            ((SLOTS * SOUNDS, STRIP), BF16),
+            ((SLOTS * SOUNDS, STRIP), F32),
             strip_rows,
             strip_rows,
+            ((SOUNDS, LANES), F32),
             narrow,
             table_rows,
         ],
@@ -826,12 +815,11 @@
         ],
     )
     tables = with_sectors(table)
-    twin, start_grad, row_match, limit, send, strip_match, top_matrix, prepared, rank = call(
+    twin, start_grad, limit, send, strip_match, top_matrix, prepared, rank = call(
         functools.partial(prepare_kernel, strips, owners),
         [
             strip_rows,
             strip_rows,
-            ((SLOTS, SLOTS * SOUNDS), F32),
             strip_rows,
             ((owners * ROWS, 3 * 4 * SLOTS), BF16),
             ((SLOTS, SLOTS), F32),
@@ -865,16 +853,15 @@
         decay,
         weight,
         prepared,
-        high,
-        low,
-        row_match,
+        blocks,
+        mix,
         obs_slot,
         *tables,
     )
     second = trade(second)
     third, values = call(
         functools.partial(second_step_kernel, strips, owners, betas[1]),
-        [message, ((1, SLOTS * SOUNDS), F32)],
+        [message, ((SOUNDS, LANES), F32)],
         first,
         second,
         column,
@@ -892,9 +879,8 @@
         send,
         point,
         top,
-        high,
-        low,
-        row_match,
+        blocks,
+        mix,
         obs_slot,
         *tables,
     )
@@ -905,7 +891,6 @@
         first,
         third,
         second,
-        table,
         values,
         observed,
         bands,

time: 39.3 us -> 38.5 us (0.980)
  Pallas kernels: 7.05 us -> 6.11 us
    pallas_call x6, Pallas kernels: 7.05 us -> 6.11 us  [call(): pl.pallas_call(kernel, out_shape=[jax.ShapeDtypeStruct(shape, dtype) for...]
where the time goes in v5:
time: 38.5 us; the launch traced here: 38.2 us
  blocking collectives  19 us (49%)
  starting transfers between devices  7.82 us (20%)
  Pallas kernels  6.11 us (16%)
  waiting for transfers between devices  4.01 us (10%)
  between operations  1.31 us (3%)
    all_to_all x2, blocking collectives, trade(): return lax.all_to_all(values, 'tile', 0, 0, tiled=True)  19 us
    all_to_all x1, starting transfers between devices, trade(): return lax.all_to_all(values, 'tile', 0, 0, tiled=True)  7.4 us
    pallas_call x6, Pallas kernels, call(): pl.pallas_call(kernel, out_shape=[jax.ShapeDtypeStruct(shape, dtype) for...  6.11 us
    all_to_all x1, waiting for transfers between devices, trade(): return lax.all_to_all(values, 'tile', 0, 0, tiled=True)  3.63 us
  transfers between devices with their start and end apart: 2, of which 2 were waited for; matrix products, arithmetic and copies ran while one was open for 0% of the time, Pallas kernels for 4%

profile of v5, /device:TPU:0, one launch (start us, length us, event | category | flops | bytes accessed | tf_op | source)
XLA Modules:
  0.0 38.2 jit_solution(11676662451728857310)
XLA Ops:
  0.6 1.5 %shard_map.95 = (s32[1,32]{1,0:T(1,128)S(1)}, f32[32,64]{1,0:T(8,128)S(1)}, s32[1,16]{1,0:T(1,128)S(1)}, s32[1,16]{1,0:T(1,128)S(1)}, f32[1,128]{1,0:T(1,128)S(1...) custom-call(s32[1,32]{1,0:T(1,128)} %bitcast.9, f32[32,64]{1,0:T(8,128)} %refs_1_.1, ...), custom_call_target="tpu_custom_call" | custom-call | tf_op jit(solution)/shard_map/pallas_call | solution.py:734
  2.1 7.4 %all-to-all-start = ((f32[16,2,128]{2,1,0:T(2,128)}), f32[16,2,128]{2,1,0:T(2,128)S(1)}, u32[]{:S(2)}, u32[]{:S(2)}) async-start(f32[16,2,128]{2,1,0:T(2,128)} %get-tuple-element.35), calls=%async_computation | async-start | bytes 32768 | tf_op jit(solution)/shard_map/all_to_all | solution.py:772
  10.2 1.0 %shard_map.96 = (f32[1024,256]{1,0:T(8,128)S(1)}, f32[16,256]{1,0:T(8,128)S(1)}, f32[16,256]{1,0:T(8,128)S(1)}, f32[64,128]{1,0:T(8,128)S(1)}, f32[16,128]{1,0:T(8,128)S(1)}, /*index=5*/f32[24,128]{1,0:T(8,128)S(1)}) custom-call(f32[1024,256]{1,0:T(8,128)S(1)} %get-tuple-element.36.jac_ref, f32[32,64]{1,0:T(8,128)S(1)} %get-tuple-element.37.obs_ref, ...), custom_call_target="tpu_custom_call" | custom-call | tf_op jit(solution)/shard_map/pallas_call | solution.py:734
  11.2 0.4 %collective-permute-start = (f32[24,128]{1,0:T(8,128)S(1)}, f32[24,128]{1,0:T(8,128)S(1)}, u32[]{:S(2)}, u32[]{:S(2)}) collective-permute-start(f32[24,128]{1,0:T(8,128)S(1)} %get-tuple-element.43.table_ref.rest_0_), channel_id=1, source_target_pairs={{0,1},{1,0},{2,3},{3,2},{4,5},{5,4},{6,7},{7,6},{8,9},{9,8},{10,11... | collective-permute-start | bytes 36872 | tf_op jit(solution)/shard_map/ppermute | solution.py:780
  11.6 0.5 %shard_map.97 = (f32[16,256]{1,0:T(8,128)S(1)}, f32[16,256]{1,0:T(8,128)S(1)}, f32[16,256]{1,0:T(8,128)S(1)}, bf16[128,192]{1,0:T(8,128)(2,1)S(1)}, f32[16,16]{1...) custom-call(f32[16,256]{1,0:T(8,128)S(1)} %get-tuple-element.41.column_ref, ...), custom_call_target="tpu_custom_call" | custom-call | tf_op jit(solution)/shard_map/pallas_call | solution.py:734
  12.0 0.4 collective-permute-done.rest_1_
  12.4 3.6 %all-to-all-done.first_ref = f32[16,2,128]{2,1,0:T(2,128)S(1)} async-done(((f32[16,2,128]{2,1,0:T(2,128)}), f32[16,2,128]{2,1,0:T(2,128)S(1)}, u32[]{:S(2)}, u32[]{:S(2)}) %all-to-all-start) | async-done | bytes 16416 | tf_op jit(solution)/shard_map/all_to_all | solution.py:772
  16.1 0.9 %shard_map.98 = (f32[16,256]{1,0:T(8,128)S(1)}, f32[16,128]{1,0:T(8,128)S(1)}, f32[16,8,128]{2,1,0:T(8,128)S(1)}, f32[32,128]{1,0:T(8,128)S(1)}, f32[64,128]{1,0...) custom-call(f32[16,2,128]{2,1,0:T(2,128)S(1)} %all-to-all-done.first_ref, ...), custom_call_target="tpu_custom_call" | custom-call | tf_op jit(solution)/shard_map/pallas_call | solution.py:734
  16.9 9.5 %all_to_all.15.second_ref = f32[16,8,128]{2,1,0:T(8,128)S(1)} all-to-all(f32[16,8,128]{2,1,0:T(8,128)S(1)} %get-tuple-element.55), channel_id=1, replica_groups=mesh['ens'=2,'tile'=16] {'tile'}, dimensions={0} | all-to-all | bytes 131072 | tf_op jit(solution)/shard_map/all_to_all | solution.py:772
  26.4 0.9 %shard_map.99 = (f32[16,8,128]{2,1,0:T(8,128)S(1)}, f32[64,128]{1,0:T(8,128)S(1)}) custom-call(f32[16,2,128]{2,1,0:T(2,128)S(1)} %all-to-all-done.first_ref, f32[16,8,128]{2,1,0:T(8,128)S(1)} %all_to_all.15.second_ref, f32[16,256]{1,0:T(8,128)S(1)} %get-tuple-element.41.column_ref, f32[16,256]{1,0:T(8,128)S(1)} %get-tuple-element.45.twin_ref, ...), custom_call_target="tpu_custom_call" | custom-call | tf_op jit(solution)/shard_map/pallas_call | solution.py:734
  27.3 9.5 %all_to_all.16.third_ref = f32[16,8,128]{2,1,0:T(8,128)S(1)} all-to-all(f32[16,8,128]{2,1,0:T(8,128)S(1)} %get-tuple-element.64), channel_id=1, replica_groups=mesh['ens'=2,'tile'=16] {'tile'}, dimensions={0} | all-to-all | bytes 131072 | tf_op jit(solution)/shard_map/all_to_all | solution.py:772
  36.9 1.4 %shard_map.100 = (f32[32,1024]{1,0:T(8,128)}, f32[32,64]{1,0:T(8,128)}) custom-call(f32[16,2,128]{2,1,0:T(2,128)S(1)} %all-to-all-done.first_ref, f32[16,8,128]{2,1,0:T(8,128)S(1)} %all_to_all.16.third_ref, f32[16,8,128]{2,1,0:T(8,128)S(1)} %all_to_all.15.second_ref, f32[64,128]{1,0:T(8,128)S(1)} %get-tuple-element.65.values_ref, ...), custom_call_target="tpu_custom_call" | custom-call | tf_op jit(solution)/shard_map/pallas_call | solution.py:734
Async XLA Ops:
  2.1 13.9 %all-to-all-start = ((f32[16,2,128]{2,1,0:T(2,128)}), f32[16,2,128]{2,1,0:T(2,128)S(1)}, u32[]{:S(2)}, u32[]{:S(2)}) async-start(f32[16,2,128]{2,1,0:T(2,128)} %get-tuple-element.35), calls=%async_computation | async-start | bytes 32768 | tf_op jit(solution)/shard_map/all_to_all | solution.py:772
  11.2 1.3 %collective-permute-start = (f32[24,128]{1,0:T(8,128)S(1)}, f32[24,128]{1,0:T(8,128)S(1)}, u32[]{:S(2)}, u32[]{:S(2)}) collective-permute-start(f32[24,128]{1,0:T(8,128)S(1)} %get-tuple-element.43.table_ref.rest_0_), channel_id=1, source_target_pairs={{0,1},{1,0},{2,3},{3,2},{4,5},{5,4},{6,7},{7,6},{8,9},{9,8},{10,11... | collective-permute-start | bytes 36872 | tf_op jit(solution)/shard_map/ppermute | solution.py:780

commit v6 on v5

--- a/solution.py
+++ b/solution.py
@@ -26,9 +26,11 @@
 BF16 = jnp.bfloat16
 HIGHEST = lax.Precision.HIGHEST
 
-LINE, SPOT, BAND, TOTAL, ROW, COL, VALID = range(7)
-LINE_ROW, SPOT_ROW, TOTAL_ROW, APPROX_ROW = range(SLOTS, SLOTS + 4)
-TABLE_ROWS = SLOTS + ROWS
+LINE, SPOT, BAND, COL, VALID = range(5)
+GRADS, COLUMNS, GROUP = 0, SLOTS, 2 * SLOTS
+COUNTS, META, SUMS, SLOT_ROW = (GROUP + 4 + i for i in range(4))
+FIRST_ROWS = GROUP + ROWS
+S_STRIP, S_SPOT, S_BAND, S_VALID, S_TOTAL, S_APPROX = (i * SLOTS for i in range(6))
 
 
 def momentum_weights(total_steps):
@@ -78,11 +80,15 @@
     return high, (values - high.astype(F32)).astype(BF16)
 
 
-def split_rows(values):
+def split_parts(values):
     high = values.astype(BF16)
     rest = values - high.astype(F32)
     middle = rest.astype(BF16)
-    return jnp.concatenate([high, middle, (rest - middle.astype(F32)).astype(BF16)], axis=0)
+    return [high, middle, (rest - middle.astype(F32)).astype(BF16)]
+
+
+def split_rows(values):
+    return jnp.concatenate(split_parts(values), axis=0)
 
 
 def haar_signs():
@@ -153,10 +159,10 @@
     return out
 
 
-def background(first, partial_rows, decay, sectors):
-    counts = weekly([first[t, 0:1, :] for t in range(WIN * sectors)], sectors)
-    sums = weekly([first[t, 1:2, :] for t in range(WIN * sectors)], sectors)
-    partials = weekly(partial_rows, sectors)
+def background(first, partials, decay, sectors):
+    pairs = range(WIN * sectors)
+    counts = weekly([first[t, COUNTS : COUNTS + 1, :] for t in pairs], sectors)
+    sums = weekly([first[t, SUMS : SUMS + 1, :] for t in pairs], sectors)
     carried = scan_ahead(partials, decay)
     back = [
         SOUNDS * partials[w] + (SOUNDS * counts[w]) * carried[w] - sums[w] for w in range(WIN)
@@ -205,70 +211,80 @@
     return out
 
 
-def start_kernel(*refs):
-    fetched = (len(refs) - 3) // 2
-    sources, targets = refs[:fetched], refs[fetched : 2 * fetched]
-    out_ref, made_ref, sems = refs[2 * fetched :]
-    copies = [
-        pltpu.make_async_copy(source, target, sems.at[i])
-        for i, (source, target) in enumerate(zip(sources, targets))
-    ]
-    for copy in copies:
-        copy.start()
-    copies[0].wait()
-    copies[1].wait()
-    band_ref, obs_ref = targets[:2]
-    hot = one_hot_bands(to_col(band_ref[...].astype(F32)))
-    sums = jnp.sum(obs_ref[...], axis=1, keepdims=True)
-    counted = jnp.sum(hot, axis=0, keepdims=True)
-    summed = jnp.sum(hot * sums, axis=0, keepdims=True)
-    for t in range(made_ref.shape[0]):
-        made_ref[t, 0:1, :] = counted
-        made_ref[t, 1:2, :] = summed
-    sent = pltpu.make_async_copy(made_ref, out_ref, sems.at[fetched])
-    sent.start()
-    for copy in copies[2:]:
-        copy.wait()
-    sent.wait()
-
-
 def along_lanes(col):
     n = col.shape[0]
     here = iota((n, LANES), 0) == iota((n, LANES), 1)
     return jnp.sum(jnp.where(here, col, 0.0), axis=0, keepdims=True)
 
 
-def transform_kernel(
+def open_kernel(
     strips,
-    jac_ref,
+    owners,
+    band_in,
+    obs_in,
+    row_in,
+    col_in,
+    weight_in,
+    decay_in,
+    jac_in,
+    count_ref,
+    band_ref,
     obs_ref,
+    weight_ref,
+    decay_ref,
+    blocks_ref,
+    column_ref,
+    twin_ref,
+    start_grad_ref,
+    obs_slot_ref,
+    mix_ref,
+    info_ref,
+    limit_ref,
+    limit_rows_ref,
+    send_ref,
+    strip_match_ref,
+    top_matrix_ref,
+    rank_ref,
+    message_ref,
     row_ref,
     col_ref,
-    count_ref,
-    band_ref,
-    blocks_ref,
-    column_ref,
-    obs_grad_ref,
-    obs_slot_ref,
-    mix_ref,
-    table_ref,
+    jac_ref,
+    sems,
 ):
+    half = SLOTS * SOUNDS // 2
+    moves = [
+        (band_in, band_ref),
+        (obs_in, obs_ref),
+        (row_in, row_ref),
+        (col_in, col_ref),
+        (weight_in, weight_ref),
+        (decay_in, decay_ref),
+        (jac_in.at[:half], jac_ref.at[:half]),
+        (jac_in.at[half:], jac_ref.at[half:]),
+    ]
+    copies = [pltpu.make_async_copy(a, b, sems.at[i]) for i, (a, b) in enumerate(moves)]
+    for copy in copies:
+        copy.start()
     sectors = strips // SEC_STRIPS
+    strips_owner = NLAT * SEC_STRIPS // owners
     sector = lax.rem(lax.axis_index("tile"), sectors).astype(F32)
     signs = haar_signs()
     scales = haar_scales()
-    chunk = STRIP
-    for start in range(0, SLOTS * SOUNDS, chunk):
-        high, low = split(jac_ref[start : start + chunk, :])
-        blocks_ref[start : start + chunk, :] = (dot(high, signs) + dot(low, signs)) * scales
-
+    for copy in copies[:6]:
+        copy.wait()
+
+    band_row = band_ref[...].astype(F32)
+    block_hot = one_hot_bands(to_col(band_row))
+    counted = jnp.sum(block_hot, axis=0, keepdims=True)
+    summed = jnp.sum(block_hot * jnp.sum(obs_ref[...], axis=1, keepdims=True), axis=0, keepdims=True)
     row_of = to_col(row_ref[...].astype(F32))
-    col_of = to_col(col_ref[...].astype(F32))
+    col_row = col_ref[...].astype(F32)
+    col_of = to_col(col_row)
     valid = jnp.where(iota((SLOTS, 1), 0) < count_ref[0], 1.0, 0.0)
+    valid_row = jnp.where(iota((1, SLOTS), 1) < count_ref[0], 1.0, 0.0)
     line = jnp.floor(col_of / SEC_STRIPS)
     spot = sector * SEC_STRIPS + (col_of - line * SEC_STRIPS)
     row_hot = jnp.where(row_of == iota((SLOTS, SB_DEV), 1).astype(F32), 1.0, 0.0)
-    band_row = band_ref[...].astype(F32)
     band = jnp.sum(row_hot * band_row, axis=1, keepdims=True)
     band = jnp.where(valid > 0.0, band, -1.0)
     lane = iota((1, LANES), 1)
@@ -279,67 +295,11 @@
     block_lane = (lane >= MISFIT) & (lane < MISFIT + SB_DEV)
     wanted = jnp.where(block_lane, (lane - MISFIT).astype(F32), wanted)
     mix_ref[...] = jnp.where(row_of == wanted, valid, 0.0)
-    obs_grad = stack_rows(back_rows(obs_slot, blocks_ref))
-    obs_grad_ref[...] = obs_grad
-    ones = [
-        jnp.sum(blocks_ref[k * SOUNDS : (k + 1) * SOUNDS, :], axis=0, keepdims=True)
-        for k in range(SLOTS)
-    ]
-    column = stack_rows(ones) * valid
-    column_ref[...] = column
-
-    at = iota((SLOTS, LANES), 1)
-    info = jnp.zeros((SLOTS, LANES), F32)
-    for place, values in (
-        (LINE, line),
-        (SPOT, spot),
-        (BAND, band),
-        (TOTAL, column[:, 0:1]),
-        (ROW, row_of),
-        (COL, col_of),
-        (VALID, valid),
-    ):
-        info = jnp.where(at == place, values, info)
-    table_ref[0:SLOTS, :] = info
-    table_ref[SLOTS:TABLE_ROWS, :] = jnp.zeros((TABLE_ROWS - SLOTS, LANES), F32)
-    table_ref[LINE_ROW : LINE_ROW + 1, :] = along_lanes(line + 1.0)
-    table_ref[SPOT_ROW : SPOT_ROW + 1, :] = along_lanes(spot + 1.0)
-    table_ref[TOTAL_ROW : TOTAL_ROW + 1, :] = along_lanes(column[:, 0:1])
-    table_ref[APPROX_ROW : APPROX_ROW + 1, :] = along_lanes(-obs_grad[:, 0:1] * valid)
-
-
-def prepare_kernel(
-    strips,
-    owners,
-    column_ref,
-    obs_grad_ref,
-    table_ref,
-    weight_ref,
-    twin_ref,
-    start_grad_ref,
-    limit_ref,
-    send_ref,
-    strip_match_ref,
-    top_matrix_ref,
-    message_ref,
-    rank_ref,
-):
-    strips_owner = NLAT * SEC_STRIPS // owners
-    column = column_ref[...]
-    info = table_ref[0:SLOTS, :]
-    spot = info[:, SPOT : SPOT + 1]
-    band = info[:, BAND : BAND + 1]
-    col_of = info[:, COL : COL + 1]
-    valid = info[:, VALID : VALID + 1]
-    col_row = to_row(col_of)
-    valid_row = to_row(valid)
 
     same = jnp.where(col_of == col_row, 1.0, 0.0)
     before = jnp.where(iota((SLOTS, SLOTS), 1) < iota((SLOTS, SLOTS), 0), 1.0, 0.0)
     other = jnp.where(iota((SLOTS, SLOTS), 1) != iota((SLOTS, SLOTS), 0), same, 0.0)
     strip_match_ref[...] = same * valid_row
-    start_grad_ref[...] = -exact_dot(same * valid_row, obs_grad_ref[...])
-    twin_ref[...] = exact_dot(other, column)
     first = jnp.where(jnp.sum(same * before, axis=1, keepdims=True) > 0.0, 0.0, 1.0)
     owner = jnp.floor(col_of / strips_owner)
     owner_row = jnp.floor(col_row / strips_owner)
@@ -347,6 +307,10 @@
 
     at = iota((SLOTS, LANES), 1)
     rank_ref[...] = jnp.where(at == 0, rank, jnp.where(at == 1, first, 0.0))
+    info = jnp.zeros((SLOTS, LANES), F32)
+    for place, values in ((LINE, line), (SPOT, spot), (BAND, band), (COL, col_of), (VALID, valid)):
+        info = jnp.where(at == place, values, info)
+    info_ref[...] = info
     matrix = jnp.zeros((SLOTS, LANES), F32)
     for t in range(strips):
         matrix = jnp.where(at == t, top_entry(spot, t, strips), matrix)
@@ -366,6 +330,8 @@
             low_row = jnp.where((local >= m) & (local < 2 * m), moved, low_row)
             m *= 2
         high_row = weight_ref[0:1, (strips + j) * LANES : (strips + j + 1) * LANES]
+        limit_rows_ref[j : j + 1, :] = STEP * low_row
+        limit_rows_ref[strips + j : strips + j + 1, :] = STEP * high_row
         limits_low = jnp.where(spot == float(j), low_row, limits_low)
         limits_high = jnp.where(spot == float(j), high_row, limits_high)
     limit_ref[:, :LANES] = STEP * limits_low
@@ -392,7 +358,62 @@
     base = rank * (LANES // 2)
     meta = jnp.where(at_f == base, col_of - owner * strips_owner + 1.0, 0.0)
     meta = jnp.where(at_f == base + 1.0, band + 1.0, meta)
-    message_ref[...] = message_rows(send, column, meta, None).reshape(message_ref.shape)
+
+    per = SLOTS // 2
+    grads = []
+    ones = []
+    for part in range(2):
+        copies[6 + part].wait()
+        for start in range(part * half, part * half + half, STRIP):
+            high, low = split(jac_ref[start : start + STRIP, :])
+            blocks_ref[start : start + STRIP, :] = (dot(high, signs) + dot(low, signs)) * scales
+        for k in range(part * per, part * per + per):
+            block = blocks_ref[k * SOUNDS : (k + 1) * SOUNDS, :]
+            grads.append(jnp.sum(block * obs_slot[:, k : k + 1], axis=0, keepdims=True))
+            ones.append(jnp.sum(block, axis=0, keepdims=True))
+    obs_grad = -stack_rows(grads)
+    column = stack_rows(ones) * valid
+    column_ref[...] = column
+    start_grad_ref[...] = mix_rows(same * valid_row, [-g for g in grads])
+    twin_ref[...] = mix_rows(other, [column[k : k + 1, :] for k in range(SLOTS)])
+
+    slots = jnp.zeros((1, LANES), F32)
+    for base, values in (
+        (S_STRIP, col_of),
+        (S_SPOT, spot),
+        (S_BAND, band),
+        (S_VALID, valid),
+        (S_TOTAL, column[:, 0:1]),
+        (S_APPROX, obs_grad[:, 0:1] * valid),
+    ):
+        slots = slots + moved_lanes(along_lanes(values), base)
+    group = message_rows(send, column, meta, None).reshape(owners, ROWS, LANES)
+    kind = iota((owners, ROWS, LANES), 1)
+    for at_kind, row in ((4, counted), (6, summed), (7, slots)):
+        group = jnp.where(kind == at_kind, row.reshape(1, 1, LANES), group)
+    message_ref[:, GROUP:, :] = group
+    for t in range(owners):
+        lanes = slice(t % 2 * LANES, t % 2 * LANES + LANES)
+        message_ref[t, GRADS : GRADS + SLOTS, :] = obs_grad[:, lanes]
+        message_ref[t, COLUMNS : COLUMNS + SLOTS, :] = column[:, lanes]
+
+
+def moved_lanes(row, by):
+    by = by % LANES
+    return pltpu.roll(jnp.broadcast_to(row, (ROWS, LANES)), by, 1)[0:1] if by else row
+
+
+def window_row(rows, base):
+    lane = iota((1, LANES), 1)
+    out = jnp.zeros((1, LANES), F32)
+    for i, row in enumerate(rows):
+        inside = (lane >= i * SLOTS) & (lane < (i + 1) * SLOTS)
+        out = jnp.where(inside, moved_lanes(row, i * SLOTS - base), out)
+    return out
+
+
+def thrice(match):
+    return jnp.concatenate([match] * 3, axis=1).astype(BF16)
 
 
 def message_rows(send, strips_part, meta, partial):
@@ -443,46 +464,137 @@
     return jnp.where(iota((SLOTS, SLOTS), 0) == iota((SLOTS, SLOTS), 1), 0.0, strip_match)
 
 
+def everyones_step(strips, owners, first_ref, scalars, limit_rows_ref, top_limit, share_ref):
+    sectors = strips // SEC_STRIPS
+    odd = lax.rem(lax.axis_index("tile"), 2)
+    lane = iota((1, LANES), 1)
+    count = sectors * SLOTS
+    slots = first_ref[:, SLOT_ROW, :]
+    tall = slots.T
+
+    def col(base):
+        return jnp.concatenate([tall[base : base + SLOTS, d : d + 1] for d in range(owners)], axis=0)
+
+    def rows(base):
+        turned = []
+        for i in range(sectors):
+            by = (i * SLOTS - base) % LANES
+            turned.append(pltpu.roll(slots, by, 1) if by else slots)
+        out = []
+        for w in range(WIN):
+            row = turned[0][w * sectors : w * sectors + 1, :]
+            for i in range(1, sectors):
+                d = w * sectors + i
+                row = jnp.where(lane >= i * SLOTS, turned[i][d : d + 1, :], row)
+            out.append(row[:, :count])
+        return out
+
+    def part(values, w):
+        return values[w * count : (w + 1) * count]
+
+    strip = col(S_STRIP)
+    spot = col(S_SPOT)
+    hot = one_hot_bands(col(S_BAND))
+    spread = jnp.concatenate([jnp.broadcast_to(s, (count, NBANDS)) for s in scalars], axis=0)
+    along = jnp.sum(hot * spread, axis=1, keepdims=True)
+    column = first_ref[:, COLUMNS : COLUMNS + SLOTS, :].reshape(owners * SLOTS, LANES)
+    grads = first_ref[:, GRADS : GRADS + SLOTS, :].reshape(owners * SLOTS, LANES) + along * column
+    matrix = jnp.zeros((owners * SLOTS, LANES), F32)
+    limit = jnp.zeros((owners * SLOTS, LANES), F32)
+    for j in range(strips):
+        entries = jnp.zeros((1, LANES), F32)
+        for t in range(strips):
+            entries = jnp.where(lane == t, top_value(j, t, strips), entries)
+        low, high = limit_rows_ref[j : j + 1, :], limit_rows_ref[strips + j : strips + j + 1, :]
+        here = spot == float(j)
+        matrix = jnp.where(here, entries, matrix)
+        limit = jnp.where(here, jnp.where(odd == 0, low, high), limit)
+    fronts = (grads[:, 0:1] * col(S_VALID)) * matrix
+    parts = split(jnp.concatenate([grads, fronts], axis=1))
+    strip_rows = rows(S_STRIP)
+    spot_rows = rows(S_SPOT)
+    valid_rows = rows(S_VALID)
+    full = []
+    top_grad = []
+    for w in range(WIN):
+        line = jnp.floor(part(strip, w) / SEC_STRIPS)
+        same_line = line == jnp.floor(strip_rows[w] / SEC_STRIPS)
+        same_strip = same_line & (part(spot, w) == spot_rows[w])
+        match = jnp.concatenate(
+            [jnp.where(same_strip, valid_rows[w], 0.0), jnp.where(same_line, 1.0, 0.0)], axis=0
+        ).astype(BF16)
+        both = dot(match, part(parts[0], w)) + dot(match, part(parts[1], w))
+        full.append(both[:count, :LANES])
+        top_grad.append(both[count:, LANES:])
+    full = jnp.concatenate(full, axis=0)
+    top = shrink(-STEP * jnp.concatenate(top_grad, axis=0), top_limit)
+    approx = jnp.sum(matrix * top, axis=1, keepdims=True)
+    point = shrink(-STEP * full, limit)
+    point = jnp.where((lane == 0) & (odd == 0), approx, point)
+    dots = jnp.sum(point * column, axis=1, keepdims=True)
+    weighed = hot * dots
+    for w in range(WIN):
+        share_ref[w : w + 1, :] = jnp.sum(part(weighed, w), axis=0, keepdims=True) / SOUNDS
+
+
+def window_slots(first_ref, sectors):
+    my_index = lax.axis_index("tile")
+    base = my_index - lax.rem(my_index, sectors)
+    rows = []
+    for shift in range(sectors):
+        pair = base + lax.rem(my_index - base + (sectors - shift), sectors)
+        rows.append(first_ref[pair, SLOT_ROW : SLOT_ROW + 1, :])
+    return rows
+
+
 def first_step_kernel(
     strips,
     owners,
     first_ref,
+    info_ref,
     column_ref,
     twin_ref,
     grad_ref,
     limit_ref,
+    limit_rows_ref,
     strip_match_ref,
     top_matrix_ref,
     decay_ref,
     weight_ref,
-    prepared_ref,
     blocks_ref,
     mix_ref,
     obs_slot_ref,
-    *rest,
+    point_ref,
+    top_ref,
+    share_ref,
+    hot_ref,
+    line_tops_ref,
+    grad_out_ref,
+    lead_ref,
 ):
     sectors = strips // SEC_STRIPS
-    tables = rest[:sectors]
-    point_ref, top_ref, message_ref, hot_ref, line_tops_ref, grad_out_ref, lead_ref = rest[sectors:]
     my_index = lax.axis_index("tile")
     window = my_index // sectors
-    sums = weekly([first_ref[t, 1:2, :] for t in range(owners)], sectors)
-    returned = scan_back([-s for s in sums], decay_ref[...])
-    scalar = pick(returned, window) / SOUNDS
-    hot = jnp.concatenate([one_hot_bands(t[0:SLOTS, BAND : BAND + 1]) for t in tables], axis=0)
+    top_limit = STEP * weight_ref[0:1, :LANES]
+    sums = weekly([first_ref[t, SUMS : SUMS + 1, :] for t in range(owners)], sectors)
+    scalars = [r / SOUNDS for r in scan_back([-s for s in sums], decay_ref[...])]
+    everyones_step(strips, owners, first_ref, scalars, limit_rows_ref, top_limit, share_ref)
+
+    info = info_ref[...]
+    slots = window_slots(first_ref, sectors)
+    lane = iota((1, LANES), 1)
+    count = sectors * SLOTS
+    hot = one_hot_bands(to_col(window_row(slots, S_BAND)[:, :count]))
     hot_ref[...] = hot
-
-    def row(index):
-        return side_by_side([t[index : index + 1, :] for t in tables])
-
-    spot_row = row(SPOT_ROW) - 1.0
-    on_line = tables[0][0:SLOTS, LINE : LINE + 1] + 1.0 == row(LINE_ROW)
+    spot_row = window_row(slots, S_SPOT)
+    line_row = jnp.where(lane < count, jnp.floor(window_row(slots, S_STRIP) / SEC_STRIPS), -1.0)
+    on_line = info[:, LINE : LINE + 1] == line_row
     line_tops = jnp.concatenate(
         [jnp.where(on_line, top_entry(spot_row, t, strips), 0.0) for t in range(strips)], axis=0
     )
     line_tops_ref[...] = line_tops
     column = column_ref[...]
-    col, along = slot_scalars(hot, scalar)
+    col, along = slot_scalars(hot, pick(scalars, window))
     grads, top_grad = advance(
         strips,
         col,
@@ -491,31 +603,24 @@
         column,
         twin_ref[...],
         twins(strip_match_ref[...]),
-        row(APPROX_ROW),
-        row(TOTAL_ROW),
+        window_row(slots, S_APPROX),
+        window_row(slots, S_TOTAL),
         line_tops,
     )
     updated = shrink(-STEP * grads, limit_ref[...])
-    top = shrink(-STEP * top_grad, STEP * weight_ref[0:1, :LANES])
+    top = shrink(-STEP * top_grad, top_limit)
     point = with_approx(updated, top, top_matrix_ref[...])
     point_ref[...] = point
     top_ref[...] = top
-    partial = band_partial(point, column, hot[:SLOTS])
     chosen = forward(point, blocks_ref, mix_ref[...]) - obs_slot_ref[...]
     rows = back_rows(chosen, blocks_ref)
     grad_out_ref[...] = mix_rows(strip_match_ref[...], rows)
-    info = tables[0][0:SLOTS, :]
     at = iota((SLOTS, LANES), 0)
     fronts = jnp.broadcast_to(rows[0][:, :LANES], (SLOTS, LANES))
     for k in range(1, SLOTS):
         fronts = jnp.where(at == k, rows[k][:, :LANES], fronts)
-    approx = along_lanes(fronts[:, 0:1] * info[:, VALID : VALID + 1])
-    kind = iota(message_ref.shape, 1)
-    message_ref[...] = jnp.where(
-        kind == 4,
-        partial.reshape(1, 1, LANES),
-        jnp.where(kind == 6, approx.reshape(1, 1, LANES), prepared_ref[...]),
-    )
+    share_ref[WIN : WIN + 1, :] = along_lanes(fronts[:, 0:1] * info[:, VALID : VALID + 1])
+    share_ref[WIN + 1 :, :] = jnp.zeros((ROWS - 1, LANES), F32)
 
     sector = lax.rem(my_index, sectors).astype(F32)
     sector_row = jnp.floor(spot_row / SEC_STRIPS)
@@ -531,7 +636,7 @@
     owners,
     beta,
     first_ref,
-    second_ref,
+    info_ref,
     column_ref,
     twin_ref,
     grad_ref,
@@ -553,18 +658,13 @@
     *rest,
 ):
     sectors = strips // SEC_STRIPS
-    tables, rest = rest[:sectors], rest[sectors:]
+    shares, rest = rest[:sectors], rest[sectors:]
     message_ref, values_ref = rest
     my_index = lax.axis_index("tile")
     window = my_index // sectors
-    sector = lax.rem(my_index, sectors)
-    approx_rows = []
-    for shift in range(sectors):
-        pair = window * sectors + lax.rem(sector + (sectors - shift), sectors)
-        approx_rows.append(second_ref[pair, 6:7, :])
-    combined, _ = background(
-        first_ref, [second_ref[t, 4:5, :] for t in range(owners)], decay_ref[...], sectors
-    )
+    odd = lax.rem(my_index, 2)
+    totals = shares[0][0:WIN, :] + jnp.where(odd == 1, shares[1][0:WIN, :], shares[-1][0:WIN, :])
+    combined, _ = background(first_ref, [totals[w : w + 1, :] for w in range(WIN)], decay_ref[...], sectors)
     hot = hot_ref[...]
     column = column_ref[...]
     col, along = slot_scalars(hot, pick(combined, window))
@@ -576,8 +676,8 @@
         column,
         twin_ref[...],
         twins(strip_match_ref[...]),
-        side_by_side(approx_rows),
-        side_by_side([t[TOTAL_ROW : TOTAL_ROW + 1, :] for t in tables]),
+        side_by_side([share[WIN : WIN + 1, :] for share in shares]),
+        window_row(window_slots(first_ref, sectors), S_TOTAL),
         line_tops_ref[...],
     )
     old = point_ref[...]
@@ -592,7 +692,7 @@
     grad = stack_rows(back_rows(values - obs_slot_ref[...], blocks_ref))
 
     partial = band_partial(point, column, hot[:SLOTS])
-    info = tables[0][0:SLOTS, :]
+    info = info_ref[...]
     valid = info[:, VALID : VALID + 1]
     top = top * lead_ref[:, 0:1]
     rank = rank_ref[:, 0:1]
@@ -602,11 +702,11 @@
     message_ref[...] = rows.reshape(message_ref.shape)
 
 
-def placing(strips, owners, second_ref, values_ref, obs_ref, band_ref):
+def placing(strips, owners, first_ref, values_ref, obs_ref, band_ref):
     sectors = strips // SEC_STRIPS
     lines = NLAT // owners
     count = owners * ROWS
-    meta = second_ref[:, 5, :]
+    meta = first_ref[:, META, :]
     wide = (owners, count)
     pair_of = iota(wide, 1) // ROWS == iota(wide, 0)
     kind = iota((1, count), 1) % ROWS
@@ -622,7 +722,7 @@
         band_tall = jnp.sum(jnp.where(tall_pair, to_row(band), 0.0), axis=1, keepdims=True)
         band_col = jnp.where(tall_kind // 2 == q, band_tall, band_col)
     band_hot = one_hot_bands(band_col - 1.0)
-    scaled = jnp.where(tall_kind < 4, STEP * second_ref[...].reshape(count, LANES), 0.0)
+    scaled = jnp.where(tall_kind < 4, STEP * first_ref[:, GROUP:, :].reshape(count, LANES), 0.0)
 
     def line_of(strip):
         return jnp.floor(strip / SEC_STRIPS)
@@ -659,7 +759,6 @@
     owners,
     first_ref,
     third_ref,
-    second_ref,
     values_ref,
     obs_ref,
     band_ref,
@@ -673,11 +772,10 @@
     count = owners * ROWS
     window = lax.axis_index("tile") // sectors
     place, band_hot, scaled, differ, block_hot = placing(
-        strips, owners, second_ref, values_ref, obs_ref, band_ref
+        strips, owners, first_ref, values_ref, obs_ref, band_ref
     )
-    combined, carried = background(
-        first_ref, [third_ref[t, 4:5, :] for t in range(owners)], decay_ref[...], sectors
-    )
+    partials = weekly([third_ref[t, 4:5, :] for t in range(owners)], sectors)
+    combined, carried = background(first_ref, partials, decay_ref[...], sectors)
     spread = jnp.concatenate(
         [jnp.broadcast_to(row, (sectors * ROWS, NBANDS)) for row in combined], axis=0
     )
@@ -759,14 +857,13 @@
         observations,
         block_row.reshape(1, SLOTS),
         block_col.reshape(1, SLOTS),
+        sparsity_weight.reshape(1, -1),
         carry_decay.reshape(1, NBANDS),
-        sparsity_weight.reshape(1, -1),
         jacobian.reshape(SLOTS * SOUNDS, STRIP),
     ]
     message = ((owners, ROWS, LANES), F32)
     narrow = ((SLOTS, LANES), F32)
     strip_rows = ((SLOTS, STRIP), F32)
-    table_rows = ((TABLE_ROWS, LANES), F32)
 
     def trade(values):
         return lax.all_to_all(values, "tile", 0, 0, tiled=True)
@@ -781,89 +878,91 @@
         return found
 
     arguments = [pltpu.with_memory_space_constraint(a, pltpu.HBM) for a in arguments]
-    bands, observed, rows, cols, decay, weight, flat, first = call(
-        start_kernel,
-        [(a.shape, a.dtype) for a in arguments] + [((owners, 2, LANES), F32)],
+    outs = [
+        ((1, SB_DEV), jnp.int32),
+        ((SB_DEV, SOUNDS), F32),
+        ((1, strips * STRIP), F32),
+        ((1, NBANDS), F32),
+        ((SLOTS * SOUNDS, STRIP), F32),
+        strip_rows,
+        strip_rows,
+        strip_rows,
+        ((SOUNDS, LANES), F32),
+        narrow,
+        narrow,
+        strip_rows,
+        ((2 * strips, LANES), F32),
+        ((owners * ROWS, 3 * 4 * SLOTS), BF16),
+        ((SLOTS, SLOTS), F32),
+        narrow,
+        narrow,
+        ((owners, FIRST_ROWS, LANES), F32),
+    ]
+    (
+        bands,
+        observed,
+        weight,
+        decay,
+        blocks,
+        column,
+        twin,
+        start_grad,
+        obs_slot,
+        mix,
+        info,
+        limit,
+        limit_rows,
+        send,
+        strip_match,
+        top_matrix,
+        rank,
+        first,
+    ) = call(
+        functools.partial(open_kernel, strips, owners),
+        outs,
         *arguments,
-        in_specs=[pl.BlockSpec(memory_space=pltpu.HBM)] * len(arguments),
-        out_specs=[pl.BlockSpec(memory_space=pltpu.VMEM)] * len(arguments)
-        + [pl.BlockSpec(memory_space=pltpu.HBM)],
+        block_count,
+        in_specs=[pl.BlockSpec(memory_space=pltpu.HBM)] * len(arguments)
+        + [pl.BlockSpec(memory_space=pltpu.SMEM)],
         scratch_shapes=[
-            pltpu.VMEM((owners, 2, LANES), F32),
+            pltpu.VMEM((1, SLOTS), jnp.int32),
+            pltpu.VMEM((1, SLOTS), jnp.int32),
+            pltpu.VMEM((SLOTS * SOUNDS, STRIP), F32),
             pltpu.SemaphoreType.DMA((len(arguments) + 1,)),
         ],
     )
     first = trade(first)
-    blocks, column, obs_grad, obs_slot, mix, table = call(
-        functools.partial(transform_kernel, strips),
-        [
-            ((SLOTS * SOUNDS, STRIP), F32),
-            strip_rows,
-            strip_rows,
-            ((SOUNDS, LANES), F32),
-            narrow,
-            table_rows,
-        ],
-        flat,
-        observed,
-        rows,
-        cols,
-        block_count,
-        bands,
-        in_specs=[
-            pl.BlockSpec(memory_space=pltpu.SMEM if i == 4 else pltpu.VMEM) for i in range(6)
-        ],
-    )
-    tables = with_sectors(table)
-    twin, start_grad, limit, send, strip_match, top_matrix, prepared, rank = call(
-        functools.partial(prepare_kernel, strips, owners),
-        [
-            strip_rows,
-            strip_rows,
-            strip_rows,
-            ((owners * ROWS, 3 * 4 * SLOTS), BF16),
-            ((SLOTS, SLOTS), F32),
-            narrow,
-            message,
-            narrow,
-        ],
-        column,
-        obs_grad,
-        table,
-        weight,
-    )
-    point, top, second, hot, line_tops, grad, lead = call(
+    point, top, share, hot, line_tops, grad, lead = call(
         functools.partial(first_step_kernel, strips, owners),
         [
             strip_rows,
             narrow,
-            message,
+            ((2 * ROWS, LANES), F32),
             ((sectors * SLOTS, NBANDS), F32),
             ((strips * SLOTS, LANES), F32),
             strip_rows,
             narrow,
         ],
         first,
+        info,
         column,
         twin,
         start_grad,
         limit,
+        limit_rows,
         strip_match,
         top_matrix,
         decay,
         weight,
-        prepared,
         blocks,
         mix,
         obs_slot,
-        *tables,
     )
-    second = trade(second)
     third, values = call(
         functools.partial(second_step_kernel, strips, owners, betas[1]),
         [message, ((SOUNDS, LANES), F32)],
         first,
-        second,
+        info,
         column,
         twin,
         grad,
@@ -882,7 +981,7 @@
         blocks,
         mix,
         obs_slot,
-        *tables,
+        *with_sectors(share),
     )
     third = trade(third)
     coeffs, misfit = call(
@@ -890,7 +989,6 @@
         [((lines * WIN, strips * STRIP), F32), ((SB_DEV, SOUNDS), F32)],
         first,
         third,
-        second,
         values,
         observed,
         bands,

time: 38.5 us -> 37.5 us (0.974)
  blocking collectives: 19 us -> 28.2 us
  starting transfers between devices: 7.82 us -> 0.17 us
  waiting for transfers between devices: 4.01 us -> 1.07 us
    all_to_all x2, blocking collectives: 19 us -> 28.2 us  [trade(): return lax.all_to_all(values, 'tile', 0, 0, tiled=True)]
    all_to_all x1 -> x0, starting transfers between devices: 7.4 us -> none  [trade(): return lax.all_to_all(values, 'tile', 0, 0, tiled=True)]
    all_to_all x1 -> x0, waiting for transfers between devices: 3.63 us -> none  [trade(): return lax.all_to_all(values, 'tile', 0, 0, tiled=True)]
    ppermute x1, waiting for transfers between devices: 0.38 us -> 1.07 us  [with_sectors(): found.append(lax.ppermute(values, 'tile', pairs))]
    pallas_call x6 -> x4, Pallas kernels: 6.11 us -> 6.49 us  [call(): pl.pallas_call(kernel, out_shape=[jax.ShapeDtypeStruct(shape, dtype) for...]
  transfers between devices with their start and end apart: 2 -> 1, of which waited for: 2 -> 1; matrix products, arithmetic and copies ran while one was open for 0% -> 0% of each run, Pallas kernels for 4% -> 0%
where the time goes in v6:
time: 37.5 us; the launch traced here: 37.3 us
  blocking collectives  28.2 us (75%)
  Pallas kernels  6.49 us (17%)
  between operations  1.29 us (3%)
  waiting for transfers between devices  1.07 us (3%)
    all_to_all x2, blocking collectives, trade(): return lax.all_to_all(values, 'tile', 0, 0, tiled=True)  28.2 us
    pallas_call x4, Pallas kernels, call(): pl.pallas_call(kernel, out_shape=[jax.ShapeDtypeStruct(shape, dtype) for...  6.49 us
    ppermute x1, waiting for transfers between devices, with_sectors(): found.append(lax.ppermute(values, 'tile', pairs))  1.07 us
  transfers between devices with their start and end apart: 1, of which 1 were waited for; matrix products, arithmetic and copies ran while one was open for 0% of the time, Pallas kernels for 0%

profile of v6, /device:TPU:0, one launch (start us, length us, event | category | flops | bytes accessed | tf_op | source)
XLA Modules:
  0.0 37.3 jit_solution(640836618982537651)
XLA Ops:
  1.3 2.1 %shard_map.95 = (s32[1,32]{1,0:T(1,128)S(1)}, f32[32,64]{1,0:T(8,128)S(1)}, f32[1,1024]{1,0:T(1,128)S(1)}, f32[1,128]{1,0:T(1,128)S(1)}, f32[1024,256]{1,0:T(8,1...) custom-call(s32[1,32]{1,0:T(1,128)} %bitcast.9, ...), custom_call_target="tpu_custom_call" | custom-call | tf_op jit(solution)/shard_map/pallas_call | solution.py:832
  3.4 18.3 %all_to_all.10.first_ref = f32[16,40,128]{2,1,0:T(8,128)S(1)} all-to-all(f32[16,40,128]{2,1,0:T(8,128)S(1)} %get-tuple-element.31), channel_id=1, replica_groups=mesh['ens'=2,'tile'=16] {'tile'}, dimensions={0} | all-to-all | bytes 655360 | tf_op jit(solution)/shard_map/all_to_all | solution.py:869
  21.7 2.1 %shard_map.96 = (f32[16,256]{1,0:T(8,128)S(1)}, f32[16,128]{1,0:T(8,128)S(1)}, f32[16,128]{1,0:T(8,128)S(1)}, f32[32,128]{1,0:T(8,128)S(1)}, f32[64,128]{1,0:T(8...) custom-call(f32[16,40,128]{2,1,0:T(8,128)S(1)} %all_to_all.10.first_ref, ...), custom_call_target="tpu_custom_call" | custom-call | tf_op jit(solution)/shard_map/pallas_call | solution.py:832
  23.8 0.2 collective-permute-start
  23.9 1.1 %collective-permute-done.rest_1_ = f32[16,128]{1,0:T(8,128)S(1)} collective-permute-done((f32[16,128]{1,0:T(8,128)S(1)}, f32[16,128]{1,0:T(8,128)S(1)}, u32[]{:S(2)}, u32[]{:S(2)}) %collective-permute-start) | collective-permute-done | bytes 8224 | tf_op jit(solution)/shard_map/ppermute | solution.py:877
  25.0 0.9 %shard_map.97 = (f32[16,8,128]{2,1,0:T(8,128)S(1)}, f32[64,128]{1,0:T(8,128)S(1)}) custom-call(f32[16,40,128]{2,1,0:T(8,128)S(1)} %all_to_all.10.first_ref, f32[16,128]{1,0:T(8,128)S(1)} %get-tuple-element.32.info_ref, f32[16,256]{1,0:T(8,128)S(1)} %get-tuple-element.33.column_ref, f32[16,256]{1,0:T(8,128)S(1)} %get-tuple-element.34.twin_ref, ...), custom_call_target="tpu_custom_call" | custom-call | tf_op jit(solution)/shard_map/pallas_call | solution.py:832
  25.9 10.0 %all_to_all.11.third_ref = f32[16,8,128]{2,1,0:T(8,128)S(1)} all-to-all(f32[16,8,128]{2,1,0:T(8,128)S(1)} %get-tuple-element.54), channel_id=1, replica_groups=mesh['ens'=2,'tile'=16] {'tile'}, dimensions={0} | all-to-all | bytes 131072 | tf_op jit(solution)/shard_map/all_to_all | solution.py:869
  35.9 1.4 %shard_map.98 = (f32[32,1024]{1,0:T(8,128)}, f32[32,64]{1,0:T(8,128)}) custom-call(f32[16,40,128]{2,1,0:T(8,128)S(1)} %all_to_all.10.first_ref, f32[16,8,128]{2,1,0:T(8,128)S(1)} %all_to_all.11.third_ref, f32[64,128]{1,0:T(8,128)S(1)} %get-tuple-element.55.values_ref, f32[32,64]{1,0:T(8,128)S(1)} %get-tuple-element.56.obs_ref, ...), custom_call_target="tpu_custom_call" | custom-call | tf_op jit(solution)/shard_map/pallas_call | solution.py:832
Async XLA Ops:
  23.8 1.2 %collective-permute-start = (f32[16,128]{1,0:T(8,128)S(1)}, f32[16,128]{1,0:T(8,128)S(1)}, u32[]{:S(2)}, u32[]{:S(2)}) collective-permute-start(f32[16,128]{1,0:T(8,128)S(1)} %get-tuple-element.53.rest_0_), channel_id=1, source_target_pairs={{0,1},{1,0},{2,3},{3,2},{4,5},{5,4},{6,7},{7,6},{8,9},{9,8},{10,11... | collective-permute-start | bytes 24584 | tf_op jit(solution)/shard_map/ppermute | solution.py:877

commit v7 on v6

--- a/solution.py
+++ b/solution.py
@@ -21,15 +21,18 @@
 ROWS = 8
 STEP = 0.2
 MISFIT = 32
+PARTS = 6
+PIECES = 1
 
 F32 = jnp.float32
 BF16 = jnp.bfloat16
 HIGHEST = lax.Precision.HIGHEST
 
 LINE, SPOT, BAND, COL, VALID = range(5)
-GRADS, COLUMNS, GROUP = 0, SLOTS, 2 * SLOTS
-COUNTS, META, SUMS, SLOT_ROW = (GROUP + 4 + i for i in range(4))
-FIRST_ROWS = GROUP + ROWS
+BLOCK = 4
+GRADS, COLUMNS, SINGLES = 0, SLOTS // BLOCK, 2 * SLOTS // BLOCK
+COUNTS, SUMS, SLOT_ROW = range(3)
+FIRST_BLOCKS = SINGLES + 1
 S_STRIP, S_SPOT, S_BAND, S_VALID, S_TOTAL, S_APPROX = (i * SLOTS for i in range(6))
 
 
@@ -161,8 +164,8 @@
 
 def background(first, partials, decay, sectors):
     pairs = range(WIN * sectors)
-    counts = weekly([first[t, COUNTS : COUNTS + 1, :] for t in pairs], sectors)
-    sums = weekly([first[t, SUMS : SUMS + 1, :] for t in pairs], sectors)
+    counts = weekly([first[t, SINGLES, COUNTS : COUNTS + 1, :] for t in pairs], sectors)
+    sums = weekly([first[t, SINGLES, SUMS : SUMS + 1, :] for t in pairs], sectors)
     carried = scan_ahead(partials, decay)
     back = [
         SOUNDS * partials[w] + (SOUNDS * counts[w]) * carried[w] - sums[w] for w in range(WIN)
@@ -251,7 +254,7 @@
     jac_ref,
     sems,
 ):
-    half = SLOTS * SOUNDS // 2
+    piece = SLOTS * SOUNDS // PIECES
     moves = [
         (band_in, band_ref),
         (obs_in, obs_ref),
@@ -259,9 +262,9 @@
         (col_in, col_ref),
         (weight_in, weight_ref),
         (decay_in, decay_ref),
-        (jac_in.at[:half], jac_ref.at[:half]),
-        (jac_in.at[half:], jac_ref.at[half:]),
     ]
+    for start in range(0, SLOTS * SOUNDS, piece):
+        moves.append((jac_in.at[start : start + piece], jac_ref.at[start : start + piece]))
     copies = [pltpu.make_async_copy(a, b, sems.at[i]) for i, (a, b) in enumerate(moves)]
     for copy in copies:
         copy.start()
@@ -337,10 +340,10 @@
     limit_ref[:, :LANES] = STEP * limits_low
     limit_ref[:, LANES:] = STEP * limits_high
 
-    shape = (owners * ROWS, 3 * 4 * SLOTS)
+    shape = (owners * ROWS, 3 * PARTS * SLOTS)
     target = (iota(shape, 0) // ROWS).astype(F32)
     kind = iota(shape, 0) % ROWS
-    place = iota(shape, 1) % (4 * SLOTS)
+    place = iota(shape, 1) % (PARTS * SLOTS)
     group = place // SLOTS
     slim_shape = (SLOTS, shape[1])
     slim = iota(slim_shape, 1) % SLOTS == iota(slim_shape, 0)
@@ -350,21 +353,19 @@
     hit = (group == 0) & (kind_f == 2.0 * rank_wide)
     hit = hit | ((group == 1) & (kind_f == 2.0 * rank_wide + 1.0))
     hit = hit | ((group == 2) & (kind == 5))
+    even = iota(shape, 0) // ROWS % 2 == 0
+    hit = hit | ((group == 4) & (kind_f == 6.0 + rank_wide) & ~even)
+    hit = hit | ((group == 5) & (kind_f == 6.0 + rank_wide) & even)
     hit = (hit & (owner_wide == target)) | ((place == 3 * SLOTS) & (kind == 4))
     send = jnp.where(hit, 1.0, 0.0).astype(BF16)
     send_ref[...] = send
 
-    at_f = at.astype(F32)
-    base = rank * (LANES // 2)
-    meta = jnp.where(at_f == base, col_of - owner * strips_owner + 1.0, 0.0)
-    meta = jnp.where(at_f == base + 1.0, band + 1.0, meta)
-
-    per = SLOTS // 2
+    per = SLOTS // PIECES
     grads = []
     ones = []
-    for part in range(2):
+    for part in range(PIECES):
         copies[6 + part].wait()
-        for start in range(part * half, part * half + half, STRIP):
+        for start in range(part * piece, part * piece + piece, STRIP):
             high, low = split(jac_ref[start : start + STRIP, :])
             blocks_ref[start : start + STRIP, :] = (dot(high, signs) + dot(low, signs)) * scales
         for k in range(part * per, part * per + per):
@@ -387,15 +388,14 @@
         (S_APPROX, obs_grad[:, 0:1] * valid),
     ):
         slots = slots + moved_lanes(along_lanes(values), base)
-    group = message_rows(send, column, meta, None).reshape(owners, ROWS, LANES)
-    kind = iota((owners, ROWS, LANES), 1)
-    for at_kind, row in ((4, counted), (6, summed), (7, slots)):
-        group = jnp.where(kind == at_kind, row.reshape(1, 1, LANES), group)
-    message_ref[:, GROUP:, :] = group
+    singles = jnp.concatenate([counted, summed, slots, jnp.zeros((1, LANES), F32)], axis=0)
     for t in range(owners):
         lanes = slice(t % 2 * LANES, t % 2 * LANES + LANES)
-        message_ref[t, GRADS : GRADS + SLOTS, :] = obs_grad[:, lanes]
-        message_ref[t, COLUMNS : COLUMNS + SLOTS, :] = column[:, lanes]
+        for i in range(SLOTS // BLOCK):
+            rows = slice(i * BLOCK, (i + 1) * BLOCK)
+            message_ref[t, GRADS + i] = obs_grad[rows, lanes]
+            message_ref[t, COLUMNS + i] = column[rows, lanes]
+        message_ref[t, SINGLES] = singles
 
 
 def moved_lanes(row, by):
@@ -416,12 +416,19 @@
     return jnp.concatenate([match] * 3, axis=1).astype(BF16)
 
 
-def message_rows(send, strips_part, meta, partial):
-    if partial is None:
-        bottom = jnp.zeros((SLOTS, LANES), F32)
-    else:
-        bottom = jnp.where(iota((SLOTS, LANES), 0) == 0, partial, 0.0)
-    stacked = jnp.concatenate([strips_part[:, :LANES], strips_part[:, LANES:], meta, bottom], axis=0)
+def message_rows(send, strips_part, meta, partial, column):
+    bottom = jnp.where(iota((SLOTS, LANES), 0) == 0, partial, 0.0)
+    stacked = jnp.concatenate(
+        [
+            strips_part[:, :LANES],
+            strips_part[:, LANES:],
+            meta,
+            bottom,
+            column[:, :LANES],
+            column[:, LANES:],
+        ],
+        axis=0,
+    )
     return dot(send, split_rows(stacked))
 
 
@@ -464,12 +471,18 @@
     return jnp.where(iota((SLOTS, SLOTS), 0) == iota((SLOTS, SLOTS), 1), 0.0, strip_match)
 
 
+def all_slots(first_ref, start):
+    return jnp.concatenate(
+        [first_ref[d, start + i] for d in range(first_ref.shape[0]) for i in range(SLOTS // BLOCK)], axis=0
+    )
+
+
 def everyones_step(strips, owners, first_ref, scalars, limit_rows_ref, top_limit, share_ref):
     sectors = strips // SEC_STRIPS
     odd = lax.rem(lax.axis_index("tile"), 2)
     lane = iota((1, LANES), 1)
     count = sectors * SLOTS
-    slots = first_ref[:, SLOT_ROW, :]
+    slots = first_ref[:, SINGLES, SLOT_ROW, :]
     tall = slots.T
 
     def col(base):
@@ -497,8 +510,8 @@
     hot = one_hot_bands(col(S_BAND))
     spread = jnp.concatenate([jnp.broadcast_to(s, (count, NBANDS)) for s in scalars], axis=0)
     along = jnp.sum(hot * spread, axis=1, keepdims=True)
-    column = first_ref[:, COLUMNS : COLUMNS + SLOTS, :].reshape(owners * SLOTS, LANES)
-    grads = first_ref[:, GRADS : GRADS + SLOTS, :].reshape(owners * SLOTS, LANES) + along * column
+    column = all_slots(first_ref, COLUMNS)
+    grads = all_slots(first_ref, GRADS) + along * column
     matrix = jnp.zeros((owners * SLOTS, LANES), F32)
     limit = jnp.zeros((owners * SLOTS, LANES), F32)
     for j in range(strips):
@@ -543,7 +556,7 @@
     rows = []
     for shift in range(sectors):
         pair = base + lax.rem(my_index - base + (sectors - shift), sectors)
-        rows.append(first_ref[pair, SLOT_ROW : SLOT_ROW + 1, :])
+        rows.append(first_ref[pair, SINGLES, SLOT_ROW : SLOT_ROW + 1, :])
     return rows
 
 
@@ -576,7 +589,7 @@
     my_index = lax.axis_index("tile")
     window = my_index // sectors
     top_limit = STEP * weight_ref[0:1, :LANES]
-    sums = weekly([first_ref[t, SUMS : SUMS + 1, :] for t in range(owners)], sectors)
+    sums = weekly([first_ref[t, SINGLES, SUMS : SUMS + 1, :] for t in range(owners)], sectors)
     scalars = [r / SOUNDS for r in scan_back([-s for s in sums], decay_ref[...])]
     everyones_step(strips, owners, first_ref, scalars, limit_rows_ref, top_limit, share_ref)
 
@@ -655,6 +668,7 @@
     blocks_ref,
     mix_ref,
     obs_slot_ref,
+    _,
     *rest,
 ):
     sectors = strips // SEC_STRIPS
@@ -698,15 +712,33 @@
     rank = rank_ref[:, 0:1]
     meta = jnp.where(rank == 0.0, pltpu.roll(top, ROWS, 1), pltpu.roll(top, LANES // 2 + ROWS, 1))
     kept = jnp.where(iota((SLOTS, STRIP), 1) == 0, 0.0, point * rank_ref[:, 1:2])
-    rows = message_rows(send_ref[...], kept - STEP * (valid * grad), meta, partial)
+    rows = message_rows(send_ref[...], kept - STEP * (valid * grad), meta, partial, column)
     message_ref[...] = rows.reshape(message_ref.shape)
 
 
-def placing(strips, owners, first_ref, values_ref, obs_ref, band_ref):
+def place_kernel(
+    strips,
+    owners,
+    first_ref,
+    band_ref,
+    place_ref,
+    band_hot_ref,
+    scaled_ref,
+    block_hot_ref,
+):
     sectors = strips // SEC_STRIPS
     lines = NLAT // owners
     count = owners * ROWS
-    meta = first_ref[:, META, :]
+    my_index = lax.axis_index("tile")
+    odd = lax.rem(my_index, 2)
+    mine_at = my_index.astype(F32)
+    strips_owner = NLAT * SEC_STRIPS // owners
+    slots = first_ref[:, SINGLES, SLOT_ROW, :]
+    lane = iota((owners, LANES), 1).astype(F32)
+    mine = (lane < SLOTS) & (jnp.floor(slots / strips_owner) == mine_at)
+    front = jnp.min(jnp.where(mine, lane, float(LANES)), axis=1, keepdims=True)
+    back = jnp.max(jnp.where(mine, lane, -1.0), axis=1, keepdims=True)
+    back = jnp.where(back > front, back, float(LANES))
     wide = (owners, count)
     pair_of = iota(wide, 1) // ROWS == iota(wide, 0)
     kind = iota((1, count), 1) % ROWS
@@ -715,14 +747,22 @@
     tall_kind = iota((count, 1), 0) % ROWS
     strip_rows = []
     band_col = jnp.zeros((count, 1), F32)
-    for q in range(2):
-        strip = meta[:, q * (LANES // 2) : q * (LANES // 2) + 1]
-        band = meta[:, q * (LANES // 2) + 1 : q * (LANES // 2) + 2]
+    slot_col = jnp.zeros((count, 1), F32) - 1.0
+    for q, at in enumerate((front, back)):
+        strip = jnp.sum(jnp.where(lane == at, slots - mine_at * strips_owner + 1.0, 0.0), axis=1, keepdims=True)
+        band = jnp.sum(jnp.where((lane == at + S_BAND) & (at < SLOTS), slots + 1.0, 0.0), axis=1, keepdims=True)
         strip_rows.append(jnp.sum(jnp.where(pair_of, strip, 0.0), axis=0, keepdims=True) - 1.0)
         band_tall = jnp.sum(jnp.where(tall_pair, to_row(band), 0.0), axis=1, keepdims=True)
-        band_col = jnp.where(tall_kind // 2 == q, band_tall, band_col)
-    band_hot = one_hot_bands(band_col - 1.0)
-    scaled = jnp.where(tall_kind < 4, STEP * first_ref[:, GROUP:, :].reshape(count, LANES), 0.0)
+        slot_tall = jnp.sum(jnp.where(tall_pair, to_row(at), 0.0), axis=1, keepdims=True)
+        own_kind = (tall_kind == 2 * q) | (tall_kind == 2 * q + 1)
+        band_col = jnp.where(own_kind | (tall_kind == 6 + q), band_tall, band_col)
+        slot_col = jnp.where(tall_kind == 2 * q + odd, slot_tall, slot_col)
+    band_hot_ref[...] = one_hot_bands(band_col - 1.0)
+    square = (count, owners * SLOTS)
+    of_pair = iota(square, 1) // SLOTS == iota(square, 0) // ROWS
+    of_slot = (iota(square, 1) % SLOTS).astype(F32) == slot_col
+    chosen = thrice(jnp.where(of_pair & of_slot, 1.0, 0.0))
+    scaled_ref[...] = STEP * dot(chosen, split_rows(all_slots(first_ref, COLUMNS)))
 
     def line_of(strip):
         return jnp.floor(strip / SEC_STRIPS)
@@ -733,25 +773,24 @@
     sector = (pair - window * sectors).astype(F32)
     line_col = (iota((blocks, 1), 0) // WIN).astype(F32)
     window_col = iota((blocks, 1), 0) % WIN
-    strip_row = jnp.where(kind < 2, strip_rows[0], strip_rows[1])
+    strip_row = jnp.where((kind < 2) | (kind == 6), strip_rows[0], strip_rows[1])
+    half_of = jnp.where(kind < 4, kind % 2, 1 - odd)
     slot_line = line_of(strip_row)
     slot_spot = sector * SEC_STRIPS + strip_row - slot_line * SEC_STRIPS
     base = (window == window_col) & (slot_line == line_col) & (strip_row >= 0.0)
-    base = jnp.where(base & (kind < 4), 1.0, 0.0)
+    base = jnp.where(base & ((kind < 4) | (kind >= 6)), 1.0, 0.0)
     parts = []
     for half in range(2):
-        part = jnp.where(kind % 2 == half, base, 0.0)
+        part = jnp.where(half_of == half, base, 0.0)
         for j in range(strips):
             parts.append(jnp.where(slot_spot == float(j), part, 0.0))
     for q in range(2):
         hit = (window == window_col) & (line_of(strip_rows[q]) == line_col) & (strip_rows[q] >= 0.0) & (kind == 5)
         parts.append(jnp.where(hit, 1.0, 0.0))
     place = jnp.concatenate(parts, axis=0).astype(BF16)
-    place = jnp.concatenate([place, place, place], axis=1)
-
-    differ = values_ref[...].T[MISFIT : MISFIT + SB_DEV, :] - obs_ref[...]
-    block_hot = one_hot_bands(to_col(band_ref[...].astype(F32)))
-    return place, band_hot, scaled, differ, block_hot
+    place_ref[...] = jnp.concatenate([place, place, place], axis=1)
+
+    block_hot_ref[...] = one_hot_bands(to_col(band_ref[...].astype(F32)))
 
 
 def finish_kernel(
@@ -761,7 +800,10 @@
     third_ref,
     values_ref,
     obs_ref,
-    band_ref,
+    place_ref,
+    band_hot_ref,
+    scaled_ref,
+    block_hot_ref,
     decay_ref,
     weight_ref,
     out_ref,
@@ -771,18 +813,18 @@
     blocks = NLAT // owners * WIN
     count = owners * ROWS
     window = lax.axis_index("tile") // sectors
-    place, band_hot, scaled, differ, block_hot = placing(
-        strips, owners, first_ref, values_ref, obs_ref, band_ref
-    )
+    differ = values_ref[...].T[MISFIT : MISFIT + SB_DEV, :] - obs_ref[...]
     partials = weekly([third_ref[t, 4:5, :] for t in range(owners)], sectors)
     combined, carried = background(first_ref, partials, decay_ref[...], sectors)
     spread = jnp.concatenate(
         [jnp.broadcast_to(row, (sectors * ROWS, NBANDS)) for row in combined], axis=0
     )
-    scalars = jnp.sum(band_hot * spread, axis=1, keepdims=True)
-    rows = third_ref[...].reshape(count, LANES) - scalars * scaled
-    placed = dot(place, split_rows(rows))
-    offset = jnp.sum(block_hot * pick(carried, window), axis=1, keepdims=True)
+    scalars = jnp.sum(band_hot_ref[...] * spread, axis=1, keepdims=True)
+    third = third_ref[...].reshape(count, LANES)
+    kind = iota((count, 1), 0) % ROWS
+    rows = jnp.where(kind >= 6, -STEP * (scalars * third), third - scalars * scaled_ref[...])
+    placed = dot(place_ref[...], split_rows(rows))
+    offset = jnp.sum(block_hot_ref[...] * pick(carried, window), axis=1, keepdims=True)
     misfit_ref[...] = differ + offset
 
     lane = iota((1, LANES), 1)
@@ -892,11 +934,11 @@
         narrow,
         strip_rows,
         ((2 * strips, LANES), F32),
-        ((owners * ROWS, 3 * 4 * SLOTS), BF16),
+        ((owners * ROWS, 3 * PARTS * SLOTS), BF16),
         ((SLOTS, SLOTS), F32),
         narrow,
         narrow,
-        ((owners, FIRST_ROWS, LANES), F32),
+        ((owners, FIRST_BLOCKS, BLOCK, LANES), F32),
     ]
     (
         bands,
@@ -928,7 +970,7 @@
             pltpu.VMEM((1, SLOTS), jnp.int32),
             pltpu.VMEM((1, SLOTS), jnp.int32),
             pltpu.VMEM((SLOTS * SOUNDS, STRIP), F32),
-            pltpu.SemaphoreType.DMA((len(arguments) + 1,)),
+            pltpu.SemaphoreType.DMA((len(arguments) - 1 + PIECES,)),
         ],
     )
     first = trade(first)
@@ -958,6 +1000,18 @@
         mix,
         obs_slot,
     )
+    placed_rows = (2 * strips + 2) * lines * WIN
+    tables = call(
+        functools.partial(place_kernel, strips, owners),
+        [
+            ((placed_rows, 3 * owners * ROWS), BF16),
+            ((owners * ROWS, NBANDS), F32),
+            ((owners * ROWS, LANES), F32),
+            ((SB_DEV, NBANDS), F32),
+        ],
+        first,
+        bands,
+    )
     third, values = call(
         functools.partial(second_step_kernel, strips, owners, betas[1]),
         [message, ((SOUNDS, LANES), F32)],
@@ -981,6 +1035,7 @@
         blocks,
         mix,
         obs_slot,
+        tables[-1],
         *with_sectors(share),
     )
     third = trade(third)
@@ -991,7 +1046,7 @@
         third,
         values,
         observed,
-        bands,
+        *tables,
         decay,
         weight,
     )

time: 37.5 us -> 36.6 us (0.976)
  blocking collectives: 28.2 us -> 27.6 us
    all_to_all x2, blocking collectives: 28.2 us -> 27.6 us  [trade(): return lax.all_to_all(values, 'tile', 0, 0, tiled=True)]
    pallas_call x4 -> x5, Pallas kernels: 6.49 us -> 6.71 us  [call(): pl.pallas_call(kernel, out_shape=[jax.ShapeDtypeStruct(shape, dtype) for...]
  transfers between devices with their start and end apart: 1 -> 1, of which waited for: 1 -> 1; matrix products, arithmetic and copies ran while one was open for 0% -> 0% of each run, Pallas kernels for 0% -> 1%
where the time goes in v7:
time: 36.6 us; the launch traced here: 36.4 us
  blocking collectives  27.6 us (75%)
  Pallas kernels  6.71 us (18%)
  between operations  1.31 us (4%)
  waiting for transfers between devices  0.76 us (2%)
    all_to_all x2, blocking collectives, trade(): return lax.all_to_all(values, 'tile', 0, 0, tiled=True)  27.6 us
    pallas_call x5, Pallas kernels, call(): pl.pallas_call(kernel, out_shape=[jax.ShapeDtypeStruct(shape, dtype) for...  6.71 us
    ppermute x1, waiting for transfers between devices, with_sectors(): found.append(lax.ppermute(values, 'tile', pairs))  0.76 us
  transfers between devices with their start and end apart: 1, of which 1 were waited for; matrix products, arithmetic and copies ran while one was open for 0% of the time, Pallas kernels for 1%

profile of v7, /device:TPU:0, one launch (start us, length us, event | category | flops | bytes accessed | tf_op | source)
XLA Modules:
  0.0 36.4 jit_solution(14886335754370390254)
XLA Ops:
  1.3 2.1 %shard_map.95 = (s32[1,32]{1,0:T(1,128)S(1)}, f32[32,64]{1,0:T(8,128)S(1)}, f32[1,1024]{1,0:T(1,128)S(1)}, f32[1,128]{1,0:T(1,128)S(1)}, f32[1024,256]{1,0:T(8,1...) custom-call(s32[1,32]{1,0:T(1,128)} %bitcast.9, ...), custom_call_target="tpu_custom_call" | custom-call | tf_op jit(solution)/shard_map/pallas_call | solution.py:874
  3.4 17.8 %all_to_all.10.first_ref = f32[16,9,4,128]{3,2,1,0:T(4,128)S(1)} all-to-all(f32[16,9,4,128]{3,2,1,0:T(4,128)S(1)} %get-tuple-element.35), channel_id=1, replica_groups=mesh['ens'=2,'tile'=16] {'tile'}, dimensions={0} | all-to-all | bytes 589824 | tf_op jit(solution)/shard_map/all_to_all | solution.py:911
  21.1 2.1 %shard_map.96 = (f32[16,256]{1,0:T(8,128)S(1)}, f32[16,128]{1,0:T(8,128)S(1)}, f32[16,128]{1,0:T(8,128)S(1)}, f32[32,128]{1,0:T(8,128)S(1)}, f32[64,128]{1,0:T(8...) custom-call(f32[16,9,4,128]{3,2,1,0:T(4,128)S(1)} %all_to_all.10.first_ref, ...), custom_call_target="tpu_custom_call" | custom-call | tf_op jit(solution)/shard_map/pallas_call | solution.py:874
  23.2 0.1 collective-permute-start
  23.3 0.4 %shard_map.97 = (bf16[320,384]{1,0:T(8,128)(2,1)S(1)}, f32[128,128]{1,0:T(8,128)S(1)}, f32[128,128]{1,0:T(8,128)S(1)}, f32[32,128]{1,0:T(8,128)S(1)}) custom-call(f32[16,9,4,128]{3,2,1,0:T(4,128)S(1)} %all_to_all.10.first_ref, s32[1,32]{1,0:T(1,128)S(1)} %get-tuple-element.57.band_ref), custom_call_target="tpu_custom_call" | custom-call | tf_op jit(solution)/shard_map/pallas_call | solution.py:874
  23.7 0.8 %collective-permute-done.rest_1_ = f32[16,128]{1,0:T(8,128)S(1)} collective-permute-done((f32[16,128]{1,0:T(8,128)S(1)}, f32[16,128]{1,0:T(8,128)S(1)}, u32[]{:S(2)}, u32[]{:S(2)}) %collective-permute-start) | collective-permute-done | bytes 8224 | tf_op jit(solution)/shard_map/ppermute | solution.py:919
  24.4 1.0 %shard_map.98 = (f32[16,8,128]{2,1,0:T(8,128)S(1)}, f32[64,128]{1,0:T(8,128)S(1)}) custom-call(f32[16,9,4,128]{3,2,1,0:T(4,128)S(1)} %all_to_all.10.first_ref, f32[16,128]{1,0:T(8,128)S(1)} %get-tuple-element.36.info_ref, f32[16,256]{1,0:T(8,128)S(1)} %get-tuple-element.37.column_ref, f32[16,256]{1,0:T(8,128)S(1)} %get-tuple-element.38.twin_ref, ...), custom_call_target="tpu_custom_call" | custom-call | tf_op jit(solution)/shard_map/pallas_call | solution.py:874
  25.4 9.8 %all_to_all.11.third_ref = f32[16,8,128]{2,1,0:T(8,128)S(1)} all-to-all(f32[16,8,128]{2,1,0:T(8,128)S(1)} %get-tuple-element.60), channel_id=1, replica_groups=mesh['ens'=2,'tile'=16] {'tile'}, dimensions={0} | all-to-all | bytes 131072 | tf_op jit(solution)/shard_map/all_to_all | solution.py:911
  35.2 1.2 %shard_map.99 = (f32[32,1024]{1,0:T(8,128)}, f32[32,64]{1,0:T(8,128)}) custom-call(f32[16,9,4,128]{3,2,1,0:T(4,128)S(1)} %all_to_all.10.first_ref, f32[16,8,128]{2,1,0:T(8,128)S(1)} %all_to_all.11.third_ref, f32[64,128]{1,0:T(8,128)S(1)} %get-tuple-element.61.values_ref, f32[32,64]{1,0:T(8,128)S(1)} %get-tuple-element.62.obs_ref, ...), custom_call_target="tpu_custom_call" | custom-call | tf_op jit(solution)/shard_map/pallas_call | solution.py:874
Async XLA Ops:
  23.2 1.2 %collective-permute-start = (f32[16,128]{1,0:T(8,128)S(1)}, f32[16,128]{1,0:T(8,128)S(1)}, u32[]{:S(2)}, u32[]{:S(2)}) collective-permute-start(f32[16,128]{1,0:T(8,128)S(1)} %get-tuple-element.59.rest_0_), channel_id=1, source_target_pairs={{0,1},{1,0},{2,3},{3,2},{4,5},{5,4},{6,7},{7,6},{8,9},{9,8},{10,11... | collective-permute-start | bytes 24584 | tf_op jit(solution)/shard_map/ppermute | solution.py:919

commit v8 on v7

--- a/solution.py
+++ b/solution.py
@@ -244,10 +244,8 @@
     info_ref,
     limit_ref,
     limit_rows_ref,
-    send_ref,
     strip_match_ref,
     top_matrix_ref,
-    rank_ref,
     message_ref,
     row_ref,
     col_ref,
@@ -269,7 +267,6 @@
     for copy in copies:
         copy.start()
     sectors = strips // SEC_STRIPS
-    strips_owner = NLAT * SEC_STRIPS // owners
     sector = lax.rem(lax.axis_index("tile"), sectors).astype(F32)
     signs = haar_signs()
     scales = haar_scales()
@@ -300,16 +297,9 @@
     mix_ref[...] = jnp.where(row_of == wanted, valid, 0.0)
 
     same = jnp.where(col_of == col_row, 1.0, 0.0)
-    before = jnp.where(iota((SLOTS, SLOTS), 1) < iota((SLOTS, SLOTS), 0), 1.0, 0.0)
     other = jnp.where(iota((SLOTS, SLOTS), 1) != iota((SLOTS, SLOTS), 0), same, 0.0)
     strip_match_ref[...] = same * valid_row
-    first = jnp.where(jnp.sum(same * before, axis=1, keepdims=True) > 0.0, 0.0, 1.0)
-    owner = jnp.floor(col_of / strips_owner)
-    owner_row = jnp.floor(col_row / strips_owner)
-    rank = jnp.sum(jnp.where(owner == owner_row, before, 0.0), axis=1, keepdims=True)
-
     at = iota((SLOTS, LANES), 1)
-    rank_ref[...] = jnp.where(at == 0, rank, jnp.where(at == 1, first, 0.0))
     info = jnp.zeros((SLOTS, LANES), F32)
     for place, values in ((LINE, line), (SPOT, spot), (BAND, band), (COL, col_of), (VALID, valid)):
         info = jnp.where(at == place, values, info)
@@ -339,26 +329,6 @@
         limits_high = jnp.where(spot == float(j), high_row, limits_high)
     limit_ref[:, :LANES] = STEP * limits_low
     limit_ref[:, LANES:] = STEP * limits_high
-
-    shape = (owners * ROWS, 3 * PARTS * SLOTS)
-    target = (iota(shape, 0) // ROWS).astype(F32)
-    kind = iota(shape, 0) % ROWS
-    place = iota(shape, 1) % (PARTS * SLOTS)
-    group = place // SLOTS
-    slim_shape = (SLOTS, shape[1])
-    slim = iota(slim_shape, 1) % SLOTS == iota(slim_shape, 0)
-    owner_wide = jnp.sum(jnp.where(slim, owner, 0.0), axis=0, keepdims=True)
-    rank_wide = jnp.sum(jnp.where(slim, rank, 0.0), axis=0, keepdims=True)
-    kind_f = kind.astype(F32)
-    hit = (group == 0) & (kind_f == 2.0 * rank_wide)
-    hit = hit | ((group == 1) & (kind_f == 2.0 * rank_wide + 1.0))
-    hit = hit | ((group == 2) & (kind == 5))
-    even = iota(shape, 0) // ROWS % 2 == 0
-    hit = hit | ((group == 4) & (kind_f == 6.0 + rank_wide) & ~even)
-    hit = hit | ((group == 5) & (kind_f == 6.0 + rank_wide) & even)
-    hit = (hit & (owner_wide == target)) | ((place == 3 * SLOTS) & (kind == 4))
-    send = jnp.where(hit, 1.0, 0.0).astype(BF16)
-    send_ref[...] = send
 
     per = SLOTS // PIECES
     grads = []
@@ -583,7 +553,6 @@
     hot_ref,
     line_tops_ref,
     grad_out_ref,
-    lead_ref,
 ):
     sectors = strips // SEC_STRIPS
     my_index = lax.axis_index("tile")
@@ -591,7 +560,6 @@
     top_limit = STEP * weight_ref[0:1, :LANES]
     sums = weekly([first_ref[t, SINGLES, SUMS : SUMS + 1, :] for t in range(owners)], sectors)
     scalars = [r / SOUNDS for r in scan_back([-s for s in sums], decay_ref[...])]
-    everyones_step(strips, owners, first_ref, scalars, limit_rows_ref, top_limit, share_ref)
 
     info = info_ref[...]
     slots = window_slots(first_ref, sectors)
@@ -625,6 +593,7 @@
     point = with_approx(updated, top, top_matrix_ref[...])
     point_ref[...] = point
     top_ref[...] = top
+    everyones_step(strips, owners, first_ref, scalars, limit_rows_ref, top_limit, share_ref)
     chosen = forward(point, blocks_ref, mix_ref[...]) - obs_slot_ref[...]
     rows = back_rows(chosen, blocks_ref)
     grad_out_ref[...] = mix_rows(strip_match_ref[...], rows)
@@ -634,15 +603,6 @@
         fronts = jnp.where(at == k, rows[k][:, :LANES], fronts)
     share_ref[WIN : WIN + 1, :] = along_lanes(fronts[:, 0:1] * info[:, VALID : VALID + 1])
     share_ref[WIN + 1 :, :] = jnp.zeros((ROWS - 1, LANES), F32)
-
-    sector = lax.rem(my_index, sectors).astype(F32)
-    sector_row = jnp.floor(spot_row / SEC_STRIPS)
-    lane = iota((SLOTS, LANES), 1)
-    before = jnp.where(lane < iota((SLOTS, LANES), 0), 1.0, 0.0)
-    earlier = jnp.where(lane < SLOTS, before, jnp.where(sector_row < sector, 1.0, 0.0))
-    taken = jnp.sum(jnp.where(on_line, earlier, 0.0), axis=1, keepdims=True)
-    lead_ref[...] = jnp.broadcast_to(jnp.where(taken > 0.0, 0.0, 1.0), lead_ref.shape)
-
 
 def second_step_kernel(
     strips,
@@ -668,7 +628,6 @@
     blocks_ref,
     mix_ref,
     obs_slot_ref,
-    _,
     *rest,
 ):
     sectors = strips // SEC_STRIPS
@@ -721,10 +680,14 @@
     owners,
     first_ref,
     band_ref,
+    info_ref,
     place_ref,
     band_hot_ref,
     scaled_ref,
     block_hot_ref,
+    send_ref,
+    rank_ref,
+    lead_ref,
 ):
     sectors = strips // SEC_STRIPS
     lines = NLAT // owners
@@ -792,6 +755,51 @@
 
     block_hot_ref[...] = one_hot_bands(to_col(band_ref[...].astype(F32)))
 
+    info = info_ref[...]
+    col_of = info[:, COL : COL + 1]
+    col_row = to_row(col_of)
+    same = jnp.where(col_of == col_row, 1.0, 0.0)
+    before = jnp.where(iota((SLOTS, SLOTS), 1) < iota((SLOTS, SLOTS), 0), 1.0, 0.0)
+    first = jnp.where(jnp.sum(same * before, axis=1, keepdims=True) > 0.0, 0.0, 1.0)
+    owner = jnp.floor(col_of / strips_owner)
+    owner_row = jnp.floor(col_row / strips_owner)
+    rank = jnp.sum(jnp.where(owner == owner_row, before, 0.0), axis=1, keepdims=True)
+
+    at = iota((SLOTS, LANES), 1)
+    rank_ref[...] = jnp.where(at == 0, rank, jnp.where(at == 1, first, 0.0))
+    shape = (owners * ROWS, 3 * PARTS * SLOTS)
+    target = (iota(shape, 0) // ROWS).astype(F32)
+    kind = iota(shape, 0) % ROWS
+    place = iota(shape, 1) % (PARTS * SLOTS)
+    group = place // SLOTS
+    slim_shape = (SLOTS, shape[1])
+    slim = iota(slim_shape, 1) % SLOTS == iota(slim_shape, 0)
+    owner_wide = jnp.sum(jnp.where(slim, owner, 0.0), axis=0, keepdims=True)
+    rank_wide = jnp.sum(jnp.where(slim, rank, 0.0), axis=0, keepdims=True)
+    kind_f = kind.astype(F32)
+    hit = (group == 0) & (kind_f == 2.0 * rank_wide)
+    hit = hit | ((group == 1) & (kind_f == 2.0 * rank_wide + 1.0))
+    hit = hit | ((group == 2) & (kind == 5))
+    even = iota(shape, 0) // ROWS % 2 == 0
+    hit = hit | ((group == 4) & (kind_f == 6.0 + rank_wide) & ~even)
+    hit = hit | ((group == 5) & (kind_f == 6.0 + rank_wide) & even)
+    hit = (hit & (owner_wide == target)) | ((place == 3 * SLOTS) & (kind == 4))
+    send = jnp.where(hit, 1.0, 0.0).astype(BF16)
+    send_ref[...] = send
+
+    window = window_slots(first_ref, sectors)
+    spot_row = window_row(window, S_SPOT)
+    lane = iota((1, LANES), 1)
+    line_row = jnp.where(lane < sectors * SLOTS, jnp.floor(window_row(window, S_STRIP) / SEC_STRIPS), -1.0)
+    on_line = info[:, LINE : LINE + 1] == line_row
+    sector = lax.rem(my_index, sectors).astype(F32)
+    sector_row = jnp.floor(spot_row / SEC_STRIPS)
+    lane = iota((SLOTS, LANES), 1)
+    before = jnp.where(lane < iota((SLOTS, LANES), 0), 1.0, 0.0)
+    earlier = jnp.where(lane < SLOTS, before, jnp.where(sector_row < sector, 1.0, 0.0))
+    taken = jnp.sum(jnp.where(on_line, earlier, 0.0), axis=1, keepdims=True)
+    lead_ref[...] = jnp.broadcast_to(jnp.where(taken > 0.0, 0.0, 1.0), lead_ref.shape)
+
 
 def finish_kernel(
     strips,
@@ -934,9 +942,7 @@
         narrow,
         strip_rows,
         ((2 * strips, LANES), F32),
-        ((owners * ROWS, 3 * PARTS * SLOTS), BF16),
         ((SLOTS, SLOTS), F32),
-        narrow,
         narrow,
         ((owners, FIRST_BLOCKS, BLOCK, LANES), F32),
     ]
@@ -954,10 +960,8 @@
         info,
         limit,
         limit_rows,
-        send,
         strip_match,
         top_matrix,
-        rank,
         first,
     ) = call(
         functools.partial(open_kernel, strips, owners),
@@ -974,7 +978,7 @@
         ],
     )
     first = trade(first)
-    point, top, share, hot, line_tops, grad, lead = call(
+    point, top, share, hot, line_tops, grad = call(
         functools.partial(first_step_kernel, strips, owners),
         [
             strip_rows,
@@ -983,7 +987,6 @@
             ((sectors * SLOTS, NBANDS), F32),
             ((strips * SLOTS, LANES), F32),
             strip_rows,
-            narrow,
         ],
         first,
         info,
@@ -1001,16 +1004,20 @@
         obs_slot,
     )
     placed_rows = (2 * strips + 2) * lines * WIN
-    tables = call(
+    *tables, send, rank, lead = call(
         functools.partial(place_kernel, strips, owners),
         [
             ((placed_rows, 3 * owners * ROWS), BF16),
             ((owners * ROWS, NBANDS), F32),
             ((owners * ROWS, LANES), F32),
             ((SB_DEV, NBANDS), F32),
+            ((owners * ROWS, 3 * PARTS * SLOTS), BF16),
+            narrow,
+            narrow,
         ],
         first,
         bands,
+        info,
     )
     third, values = call(
         functools.partial(second_step_kernel, strips, owners, betas[1]),
@@ -1035,7 +1042,6 @@
         blocks,
         mix,
         obs_slot,
-        tables[-1],
         *with_sectors(share),
     )
     third = trade(third)

time: 36.6 us -> 36.3 us (level)
  transfers between devices with their start and end apart: 1 -> 1, of which waited for: 1 -> 1; matrix products, arithmetic and copies ran while one was open for 0% -> 0% of each run, Pallas kernels for 1% -> 2%
where the time goes in v8:
time: 36.3 us; the launch traced here: 36.1 us
  blocking collectives  27.6 us (76%)
  Pallas kernels  6.64 us (18%)
  between operations  1.31 us (4%)
  waiting for transfers between devices  0.47 us (1%)
    all_to_all x2, blocking collectives, trade(): return lax.all_to_all(values, 'tile', 0, 0, tiled=True)  27.6 us
    pallas_call x5, Pallas kernels, call(): pl.pallas_call(kernel, out_shape=[jax.ShapeDtypeStruct(shape, dtype) for...  6.64 us
  transfers between devices with their start and end apart: 1, of which 1 were waited for; matrix products, arithmetic and copies ran while one was open for 0% of the time, Pallas kernels for 2%

profile of v8, /device:TPU:0, one launch (start us, length us, event | category | flops | bytes accessed | tf_op | source)
XLA Modules:
  0.0 36.1 jit_solution(11986807150482552230)
XLA Ops:
  1.3 2.1 %shard_map.95 = (s32[1,32]{1,0:T(1,128)S(1)}, f32[32,64]{1,0:T(8,128)S(1)}, f32[1,1024]{1,0:T(1,128)S(1)}, f32[1,128]{1,0:T(1,128)S(1)}, f32[1024,256]{1,0:T(8,1...) custom-call(s32[1,32]{1,0:T(1,128)} %bitcast.9, ...), custom_call_target="tpu_custom_call" | custom-call | tf_op jit(solution)/shard_map/pallas_call | solution.py:882
  3.3 17.8 %all_to_all.10.first_ref = f32[16,9,4,128]{3,2,1,0:T(4,128)S(1)} all-to-all(f32[16,9,4,128]{3,2,1,0:T(4,128)S(1)} %get-tuple-element.35), channel_id=1, replica_groups=mesh['ens'=2,'tile'=16] {'tile'}, dimensions={0} | all-to-all | bytes 589824 | tf_op jit(solution)/shard_map/all_to_all | solution.py:919
  21.1 1.7 %shard_map.96 = (f32[16,256]{1,0:T(8,128)S(1)}, f32[16,128]{1,0:T(8,128)S(1)}, f32[16,128]{1,0:T(8,128)S(1)}, f32[32,128]{1,0:T(8,128)S(1)}, f32[64,128]{1,0:T(8,128)S(1)}, /*index=5*/f32[16,256]{1,0:T(8,128)S(1)}) custom-call(f32[16,9,4,128]{3,2,1,0:T(4,128)S(1)} %all_to_all.10.first_ref, f32[16,128]{1,0:T(8,128)S(1)} %get-tuple-element.36.info_ref, ...), custom_call_target="tpu_custom_call" | custom-call | tf_op jit(solution)/shard_map/pallas_call | solution.py:882
  22.8 0.1 collective-permute-start
  22.9 0.7 %shard_map.97 = (bf16[320,384]{1,0:T(8,128)(2,1)S(1)}, f32[128,128]{1,0:T(8,128)S(1)}, f32[128,128]{1,0:T(8,128)S(1)}, f32[32,128]{1,0:T(8,128)S(1)}, bf16[128,2...) custom-call(f32[16,9,4,128]{3,2,1,0:T(4,128)S(1)} %all_to_all.10.first_ref, ...), custom_call_target="tpu_custom_call" | custom-call | tf_op jit(solution)/shard_map/pallas_call | solution.py:882
  23.6 0.5 %collective-permute-done.rest_1_ = f32[16,128]{1,0:T(8,128)S(1)} collective-permute-done((f32[16,128]{1,0:T(8,128)S(1)}, f32[16,128]{1,0:T(8,128)S(1)}, u32[]{:S(2)}, u32[]{:S(2)}) %collective-permute-start) | collective-permute-done | bytes 8224 | tf_op jit(solution)/shard_map/ppermute | solution.py:927
  24.1 1.0 %shard_map.98 = (f32[16,8,128]{2,1,0:T(8,128)S(1)}, f32[64,128]{1,0:T(8,128)S(1)}) custom-call(f32[16,9,4,128]{3,2,1,0:T(4,128)S(1)} %all_to_all.10.first_ref, f32[16,128]{1,0:T(8,128)S(1)} %get-tuple-element.36.info_ref, f32[16,256]{1,0:T(8,128)S(1)} %get-tuple-element.37.column_ref, f32[16,256]{1,0:T(8,128)S(1)} %get-tuple-element.38.twin_ref, ...), custom_call_target="tpu_custom_call" | custom-call | tf_op jit(solution)/shard_map/pallas_call | solution.py:882
  25.1 9.8 %all_to_all.11.third_ref = f32[16,8,128]{2,1,0:T(8,128)S(1)} all-to-all(f32[16,8,128]{2,1,0:T(8,128)S(1)} %get-tuple-element.59), channel_id=1, replica_groups=mesh['ens'=2,'tile'=16] {'tile'}, dimensions={0} | all-to-all | bytes 131072 | tf_op jit(solution)/shard_map/all_to_all | solution.py:919
  34.9 1.2 %shard_map.99 = (f32[32,1024]{1,0:T(8,128)}, f32[32,64]{1,0:T(8,128)}) custom-call(f32[16,9,4,128]{3,2,1,0:T(4,128)S(1)} %all_to_all.10.first_ref, f32[16,8,128]{2,1,0:T(8,128)S(1)} %all_to_all.11.third_ref, f32[64,128]{1,0:T(8,128)S(1)} %get-tuple-element.60.values_ref, f32[32,64]{1,0:T(8,128)S(1)} %get-tuple-element.61.obs_ref, ...), custom_call_target="tpu_custom_call" | custom-call | tf_op jit(solution)/shard_map/pallas_call | solution.py:882
Async XLA Ops:
  22.8 1.2 %collective-permute-start = (f32[16,128]{1,0:T(8,128)S(1)}, f32[16,128]{1,0:T(8,128)S(1)}, u32[]{:S(2)}, u32[]{:S(2)}) collective-permute-start(f32[16,128]{1,0:T(8,128)S(1)} %get-tuple-element.58.rest_0_), channel_id=1, source_target_pairs={{0,1},{1,0},{2,3},{3,2},{4,5},{5,4},{6,7},{7,6},{8,9},{9,8},{10,11... | collective-permute-start | bytes 24584 | tf_op jit(solution)/shard_map/ppermute | solution.py:927

commit v9 on v8

--- a/solution.py
+++ b/solution.py
@@ -21,7 +21,7 @@
 ROWS = 8
 STEP = 0.2
 MISFIT = 32
-PARTS = 6
+PARTS = 4
 PIECES = 1
 
 F32 = jnp.float32
@@ -386,19 +386,9 @@
     return jnp.concatenate([match] * 3, axis=1).astype(BF16)
 
 
-def message_rows(send, strips_part, meta, partial, column):
+def message_rows(send, strips_part, meta, partial):
     bottom = jnp.where(iota((SLOTS, LANES), 0) == 0, partial, 0.0)
-    stacked = jnp.concatenate(
-        [
-            strips_part[:, :LANES],
-            strips_part[:, LANES:],
-            meta,
-            bottom,
-            column[:, :LANES],
-            column[:, LANES:],
-        ],
-        axis=0,
-    )
+    stacked = jnp.concatenate([strips_part[:, :LANES], strips_part[:, LANES:], meta, bottom], axis=0)
     return dot(send, split_rows(stacked))
 
 
@@ -623,6 +613,7 @@
     lead_ref,
     rank_ref,
     send_ref,
+    prepared_ref,
     point_ref,
     top_ref,
     blocks_ref,
@@ -671,7 +662,7 @@
     rank = rank_ref[:, 0:1]
     meta = jnp.where(rank == 0.0, pltpu.roll(top, ROWS, 1), pltpu.roll(top, LANES // 2 + ROWS, 1))
     kept = jnp.where(iota((SLOTS, STRIP), 1) == 0, 0.0, point * rank_ref[:, 1:2])
-    rows = message_rows(send_ref[...], kept - STEP * (valid * grad), meta, partial, column)
+    rows = message_rows(send_ref[...], kept - STEP * (valid * grad), meta, partial) + prepared_ref[...]
     message_ref[...] = rows.reshape(message_ref.shape)
 
 
@@ -681,6 +672,7 @@
     first_ref,
     band_ref,
     info_ref,
+    column_ref,
     place_ref,
     band_hot_ref,
     scaled_ref,
@@ -688,6 +680,7 @@
     send_ref,
     rank_ref,
     lead_ref,
+    prepared_ref,
 ):
     sectors = strips // SEC_STRIPS
     lines = NLAT // owners
@@ -780,12 +773,16 @@
     hit = (group == 0) & (kind_f == 2.0 * rank_wide)
     hit = hit | ((group == 1) & (kind_f == 2.0 * rank_wide + 1.0))
     hit = hit | ((group == 2) & (kind == 5))
-    even = iota(shape, 0) // ROWS % 2 == 0
-    hit = hit | ((group == 4) & (kind_f == 6.0 + rank_wide) & ~even)
-    hit = hit | ((group == 5) & (kind_f == 6.0 + rank_wide) & even)
     hit = (hit & (owner_wide == target)) | ((place == 3 * SLOTS) & (kind == 4))
     send = jnp.where(hit, 1.0, 0.0).astype(BF16)
     send_ref[...] = send
+    lower = (group == 0) & (kind_f == 6.0 + rank_wide) & (iota(shape, 0) // ROWS % 2 == 1)
+    upper = (group == 1) & (kind_f == 6.0 + rank_wide) & (iota(shape, 0) // ROWS % 2 == 0)
+    hit = (lower | upper) & (owner_wide == target)
+    column = column_ref[...]
+    zeros = jnp.zeros((2 * SLOTS, LANES), F32)
+    stacked = jnp.concatenate([column[:, :LANES], column[:, LANES:], zeros], axis=0)
+    prepared_ref[...] = dot(jnp.where(hit, 1.0, 0.0).astype(BF16), split_rows(stacked))
 
     window = window_slots(first_ref, sectors)
     spot_row = window_row(window, S_SPOT)
@@ -1004,7 +1001,7 @@
         obs_slot,
     )
     placed_rows = (2 * strips + 2) * lines * WIN
-    *tables, send, rank, lead = call(
+    *tables, send, rank, lead, prepared = call(
         functools.partial(place_kernel, strips, owners),
         [
             ((placed_rows, 3 * owners * ROWS), BF16),
@@ -1014,10 +1011,12 @@
             ((owners * ROWS, 3 * PARTS * SLOTS), BF16),
             narrow,
             narrow,
+            ((owners * ROWS, LANES), F32),
         ],
         first,
         bands,
         info,
+        column,
     )
     third, values = call(
         functools.partial(second_step_kernel, strips, owners, betas[1]),
@@ -1037,6 +1036,7 @@
         lead,
         rank,
         send,
+        prepared,
         point,
         top,
         blocks,

time: 36.3 us -> 36.3 us (level)
  transfers between devices with their start and end apart: 1 -> 1, of which waited for: 1 -> 1; matrix products, arithmetic and copies ran while one was open for 0% -> 0% of each run, Pallas kernels for 2% -> 1%
where the time goes in v9:
time: 36.3 us; the launch traced here: 36 us
  blocking collectives  27.6 us (76%)
  Pallas kernels  6.46 us (18%)
  between operations  1.31 us (4%)
  waiting for transfers between devices  0.63 us (2%)
    all_to_all x2, blocking collectives, trade(): return lax.all_to_all(values, 'tile', 0, 0, tiled=True)  27.6 us
    pallas_call x5, Pallas kernels, call(): pl.pallas_call(kernel, out_shape=[jax.ShapeDtypeStruct(shape, dtype) for...  6.46 us
  transfers between devices with their start and end apart: 1, of which 1 were waited for; matrix products, arithmetic and copies ran while one was open for 0% of the time, Pallas kernels for 1%

profile of v9, /device:TPU:0, one launch (start us, length us, event | category | flops | bytes accessed | tf_op | source)
XLA Modules:
  0.0 36.0 jit_solution(13317712595054847905)
XLA Ops:
  1.3 2.1 %shard_map.95 = (s32[1,32]{1,0:T(1,128)S(1)}, f32[32,64]{1,0:T(8,128)S(1)}, f32[1,1024]{1,0:T(1,128)S(1)}, f32[1,128]{1,0:T(1,128)S(1)}, f32[1024,256]{1,0:T(8,1...) custom-call(s32[1,32]{1,0:T(1,128)} %bitcast.9, ...), custom_call_target="tpu_custom_call" | custom-call | tf_op jit(solution)/shard_map/pallas_call | solution.py:879
  3.3 17.8 %all_to_all.10.first_ref = f32[16,9,4,128]{3,2,1,0:T(4,128)S(1)} all-to-all(f32[16,9,4,128]{3,2,1,0:T(4,128)S(1)} %get-tuple-element.36), channel_id=1, replica_groups=mesh['ens'=2,'tile'=16] {'tile'}, dimensions={0} | all-to-all | bytes 589824 | tf_op jit(solution)/shard_map/all_to_all | solution.py:916
  21.1 1.7 %shard_map.96 = (f32[16,256]{1,0:T(8,128)S(1)}, f32[16,128]{1,0:T(8,128)S(1)}, f32[16,128]{1,0:T(8,128)S(1)}, f32[32,128]{1,0:T(8,128)S(1)}, f32[64,128]{1,0:T(8,128)S(1)}, /*index=5*/f32[16,256]{1,0:T(8,128)S(1)}) custom-call(f32[16,9,4,128]{3,2,1,0:T(4,128)S(1)} %all_to_all.10.first_ref, f32[16,128]{1,0:T(8,128)S(1)} %get-tuple-element.37.info_ref, ...), custom_call_target="tpu_custom_call" | custom-call | tf_op jit(solution)/shard_map/pallas_call | solution.py:879
  22.8 0.1 collective-permute-start
  22.9 0.5 %shard_map.97 = (bf16[320,384]{1,0:T(8,128)(2,1)S(1)}, f32[128,128]{1,0:T(8,128)S(1)}, f32[128,128]{1,0:T(8,128)S(1)}, f32[32,128]{1,0:T(8,128)S(1)}, bf16[128,1...) custom-call(f32[16,9,4,128]{3,2,1,0:T(4,128)S(1)} %all_to_all.10.first_ref, ...), custom_call_target="tpu_custom_call" | custom-call | tf_op jit(solution)/shard_map/pallas_call | solution.py:879
  23.5 0.6 %collective-permute-done.rest_1_ = f32[16,128]{1,0:T(8,128)S(1)} collective-permute-done((f32[16,128]{1,0:T(8,128)S(1)}, f32[16,128]{1,0:T(8,128)S(1)}, u32[]{:S(2)}, u32[]{:S(2)}) %collective-permute-start) | collective-permute-done | bytes 8224 | tf_op jit(solution)/shard_map/ppermute | solution.py:924
  24.1 0.9 %shard_map.98 = (f32[16,8,128]{2,1,0:T(8,128)S(1)}, f32[64,128]{1,0:T(8,128)S(1)}) custom-call(f32[16,9,4,128]{3,2,1,0:T(4,128)S(1)} %all_to_all.10.first_ref, f32[16,128]{1,0:T(8,128)S(1)} %get-tuple-element.37.info_ref, f32[16,256]{1,0:T(8,128)S(1)} %get-tuple-element.38.column_ref, f32[16,256]{1,0:T(8,128)S(1)} %get-tuple-element.39.twin_ref, ...), custom_call_target="tpu_custom_call" | custom-call | tf_op jit(solution)/shard_map/pallas_call | solution.py:879
  25.0 9.8 %all_to_all.11.third_ref = f32[16,8,128]{2,1,0:T(8,128)S(1)} all-to-all(f32[16,8,128]{2,1,0:T(8,128)S(1)} %get-tuple-element.61), channel_id=1, replica_groups=mesh['ens'=2,'tile'=16] {'tile'}, dimensions={0} | all-to-all | bytes 131072 | tf_op jit(solution)/shard_map/all_to_all | solution.py:916
  34.8 1.2 %shard_map.99 = (f32[32,1024]{1,0:T(8,128)}, f32[32,64]{1,0:T(8,128)}) custom-call(f32[16,9,4,128]{3,2,1,0:T(4,128)S(1)} %all_to_all.10.first_ref, f32[16,8,128]{2,1,0:T(8,128)S(1)} %all_to_all.11.third_ref, f32[64,128]{1,0:T(8,128)S(1)} %get-tuple-element.62.values_ref, f32[32,64]{1,0:T(8,128)S(1)} %get-tuple-element.63.obs_ref, ...), custom_call_target="tpu_custom_call" | custom-call | tf_op jit(solution)/shard_map/pallas_call | solution.py:879
Async XLA Ops:
  22.8 1.2 %collective-permute-start = (f32[16,128]{1,0:T(8,128)S(1)}, f32[16,128]{1,0:T(8,128)S(1)}, u32[]{:S(2)}, u32[]{:S(2)}) collective-permute-start(f32[16,128]{1,0:T(8,128)S(1)} %get-tuple-element.60.rest_0_), channel_id=1, source_target_pairs={{0,1},{1,0},{2,3},{3,2},{4,5},{5,4},{6,7},{7,6},{8,9},{9,8},{10,11... | collective-permute-start | bytes 24584 | tf_op jit(solution)/shard_map/ppermute | solution.py:924
